TPU v7x, 32 devices: a whole 2x2x4 slice. The times are simulated.
32 devices in a mesh: row: 4 (over z), col: 2 (over x), layer: 4 (over y, core).
Axes of the slice: x: 2, y: 2, z: 4, core: 2. Of those that a mesh axis runs over, the one named last changes fastest.
Arguments:
- a_tiles: bfloat16 [4, 4, 2, 8, 4096], P('row', 'layer', 'col'), may hold values from -6 to 6
- b_tiles: bfloat16 [4, 4, 2, 16, 4096], P('layer', 'row', 'col'), may hold values from -0.25 to 0.25
- a_slots: int32 [4, 2, 4, 768], P('row', 'col', 'layer'), may hold values from 0 to 16, as said below
- b_slots: int32 [4, 2, 4, 768], P('row', 'col', 'layer'), may hold values from 0 to 63, as said below
Outputs:
- c_tiles: bfloat16 [4, 2, 96, 4096], P('row', 'col', 'layer')
Inputs may be any that keep to these rules, and one draw needn't show every extreme that they name: `a_slots`: entries s * 8 to s * 8 + 7 are the tasks of product tile s; the value 16 marks a dummy task (the zero tile); a tile's live tasks come first, every tile has at least 2 live tasks, and in every list some tile has 8 live tasks and some tile has dummies. `b_slots`: A dummy task holds 0 here.
All inputs are finite; a program needn't handle non-finite values.
Results may differ from a plain program's by a relative error of at most 0.013.
Values may be sent and summed in bfloat16 or wider, within the bound.
No kernel may reach another device: no remote copies, remote signals or barrier semaphores. Data moves between devices by JAX's collectives and lax.ppermute only.
A program may use at most 128 MiB of HBM per device.

v0:
```python
import jax
import jax.numpy as jnp
from jax import lax
from jax.sharding import PartitionSpec as P

TILE = 64
TASKS = 8


def tile_sums(a_panel, b_panel, a_index, b_index):
    tiles_here = a_index.shape[0] // TASKS
    a_stack = jnp.take(a_panel, a_index, axis=0).reshape(tiles_here, TASKS, TILE, TILE)
    b_stack = jnp.take(b_panel, b_index, axis=0).reshape(tiles_here, TASKS, TILE, TILE)
    return jnp.einsum("sgik,sgkj->sij", a_stack, b_stack, preferred_element_type=jnp.float32)


def shards(a_tiles, b_tiles, a_slots, b_slots):
    flat = TILE * TILE
    a_local = a_tiles.reshape(-1, flat)
    b_local = b_tiles.reshape(-1, flat)
    a_index = a_slots.reshape(-1)
    b_index = b_slots.reshape(-1)
    layer_count = lax.axis_size("layer")
    zero_tile = jnp.zeros((1, flat), jnp.bfloat16)
    a_panel = lax.all_gather(a_local, "col", axis=0, tiled=True)
    a_panel = jnp.concatenate([a_panel, zero_tile], axis=0)
    b_panel = lax.all_gather(b_local, "row", axis=0, tiled=True)
    owned_tiles = a_index.shape[0] // TASKS // layer_count
    partial_value = tile_sums(a_panel, b_panel, a_index, b_index).reshape(
        owned_tiles * layer_count, flat
    )
    summed = lax.psum_scatter(
        partial_value.astype(jnp.bfloat16), "layer", scatter_dimension=0, tiled=True
    )
    return summed.reshape(1, 1, -1, flat)


def solution(mesh):
    in_specs = (
        P("row", "layer", "col", None, None),
        P("layer", "row", "col", None, None),
        P("row", "col", "layer", None),
        P("row", "col", "layer", None),
    )
    out_specs = P("row", "col", "layer", None)
    return jax.shard_map(shards, mesh=mesh, in_specs=in_specs, out_specs=out_specs, check_vma=False)
```

profile of v0, /device:TPU:0, one launch (start us, length us, event | category | flops | bytes accessed | tf_op | source)
XLA Modules:
  0.0 127.2 jit_solution(3027567724155594780)
XLA Ops:
  6.5 0.0 reduce-scatter.4.cloned.1.call-start
  6.5 0.7 fusion.10
  7.2 0.7 reduce
  7.9 0.7 fusion.11
  8.6 0.7 reduce.2
  9.4 0.1 reshape.106
  9.5 0.1 reshape.103
  9.6 6.1 %all-gather = bf16[1,1,1,16,4096]{4,3,2,1,0:T(8,128)(2,1)S(1)} all-gather(bf16[1,1,1,8,4096]{4,3,2,1,0:T(8,128)(2,1)} %param.4), channel_id=2, replica_groups=mesh['row'=4,'col'=2,'layer'=4] {'col'}, dimensions={3}, use_global_device_ids=true | all-gather | bytes 196608 | tf_op jit(solution)/shard_map/all_gather | solution.py:25
  15.7 15.8 %all-gather.1 = bf16[1,1,1,64,4096]{4,3,2,1,0:T(8,128)(2,1)S(1)} all-gather(bf16[1,1,1,16,4096]{4,3,2,1,0:T(8,128)(2,1)} %param.5), channel_id=3, replica_groups=mesh['row'=4,'col'=2,'layer'=4] {'row'}, dimensions={3}, use_global_device_ids=true | all-gather | bytes 655360 | tf_op jit(solution)/shard_map/all_gather | solution.py:27
  31.5 5.8 %gather_fusion = bf16[768,4096]{1,0:T(8,128)(2,1)} fusion(bf16[17,4096]{1,0:T(8,128)(2,1)S(1)} %concatenate.3, s32[1024]{0:T(1024)S(1)} %pad_clamp_fusion.1), kind=kCustom, calls=%fused_computation | custom fusion | bytes 12585984 | tf_op jit(solution)/shard_map/jit(_take)/gather | solution.py:12
  37.3 17.9 %gather.13 = bf16[96,8,64,64]{3,2,1,0:T(8,128)(2,1)} reshape(bf16[768,4096]{1,0:T(8,128)(2,1)} %gather_fusion) | data formatting | bytes 12582912 | tf_op jit(solution)/shard_map/jit(_take)/gather | solution.py:12
  55.2 5.8 %gather_fusion.1 = bf16[768,4096]{1,0:T(8,128)(2,1)} fusion(bf16[64,4096]{1,0:T(8,128)(2,1)S(1)} %bitcast.12, s32[1024]{0:T(1024)S(1)} %pad_clamp_fusion), kind=kCustom, calls=%fused_computation.1 | custom fusion | bytes 12585984 | tf_op jit(solution)/shard_map/jit(_take)/gather | solution.py:13
  61.0 17.9 %gather.15 = bf16[96,8,64,64]{3,2,1,0:T(8,128)(2,1)} reshape(bf16[768,4096]{1,0:T(8,128)(2,1)} %gather_fusion.1) | data formatting | bytes 12582912 | tf_op jit(solution)/shard_map/jit(_take)/gather | solution.py:13
  78.9 11.1 %bitcast_convert_fusion = bf16[96,64,64]{2,1,0:T(8,128)(2,1)S(1)} fusion(bf16[96,8,64,64]{3,2,1,0:T(8,128)(2,1)} %gather.15, pred[96,8]{1,0:T(8,128)(4,1)S(1)} %get-tuple-element.5, bf16[96,8,64,64]{3,2,1,0:T(8,128)(2,1)} %gather.13, pred[96,8]{1,0:T(8,128)(4,1)S(1)} %get-tuple-element.6), kind=kOutput, calls=%fused_computation.8 | convolution fusion | flops 409337856 | bytes 13370880 | tf_op jit(solution)/shard_map/sgik,sgkj->sij/dot_general | solution.py:14
  90.0 1.7 %copy.7 = bf16[96,64,64]{0,2,1:T(8,128)(2,1)S(1)} copy(bf16[96,64,64]{2,1,0:T(8,128)(2,1)S(1)} %bitcast_convert_fusion) | data formatting | bytes 1572864 | tf_op jit(solution)/shard_map/convert_element_type | solution.py:33
  91.7 1.3 copy.10
  93.0 0.0 reduce-scatter.4.cloned.1.call-update
  93.0 24.9 %reduce-scatter.4.cloned.1.call-done = bf16[24,4096]{1,0:T(8,128)(2,1)} async-done(((bf16[96,4096]{1,0:T(8,128)(2,1)}), bf16[24,4096]{1,0:T(8,128)(2,1)}) %reduce-scatter.4.cloned.1.call-update) | async-done | bytes 196624
  117.9 1.4 %copy.11 = bf16[24,4096]{0,1:T(8,128)(2,1)S(1)} copy(bf16[24,4096]{1,0:T(8,128)(2,1)} %reduce-scatter.4.cloned.1.call-done) | data formatting | bytes 393216
  119.3 1.0 copy.8
  (4 shorter events, 0.1 us)
Async XLA Ops:
  6.5 111.4 %reduce-scatter.4.cloned.1.call-start = ((), (), s32[]{:S(2)}) async-start(), calls=%async_computation.1 | async-start | bytes 983040
Sparse Core Ops, SparseCore 0:
  93.1 24.7 reduce-scatter.3
where the time goes:
time: 128 us; the launch traced here: 127 us
  local copies, waits for them, and re-layouts  52.9 us (41%)
  waiting for transfers between devices  24.9 us (19%)
  blocking collectives  21.9 us (17%)
  between operations  13.5 us (11%)
  matrix products  11.1 us (9%)
  other arithmetic  2.84 us (2%)
    unnamed x2, waiting for transfers between devices  24.9 us
    gather x2, local copies, waits for them, and re-layouts, tile_sums(): jnp.take(b_panel, b_index, axis=0).reshape(tiles_here, TASKS, TILE, TILE)  23.7 us
    gather x2, local copies, waits for them, and re-layouts, tile_sums(): jnp.take(a_panel, a_index, axis=0).reshape(tiles_here, TASKS, TILE, TILE)  23.6 us
    all_gather x1, blocking collectives, shards(): b_panel = lax.all_gather(b_local, 'row', axis=0, tiled=True)  15.8 us
    dot_general x1, matrix products, tile_sums(): jnp.einsum('sgik,sgkj->sij', a_stack, b_stack, preferred_element_type=jnp...  11.1 us
    all_gather x1, blocking collectives, shards(): a_panel = lax.all_gather(a_local, 'col', axis=0, tiled=True)  6.11 us
    unnamed x2, local copies, waits for them, and re-layouts  2.66 us
  transfers between devices with their start and end apart: 1, of which 1 were waited for; matrix products, arithmetic and copies ran while one was open for 0% of the time, Pallas kernels for 0%

commit v1 on v0

v1 whole, which is shorter than its diff:
```python
import functools

import jax
import jax.numpy as jnp
from jax import lax
from jax.experimental import pallas as pl
from jax.experimental.pallas import tpu as pltpu
from jax.sharding import PartitionSpec as P

TILE = 64
TASKS = 8
FLAT = TILE * TILE
LANES = 128
LINES = FLAT // LANES
ROWS_AT_ONCE = 512
MIB = 1 << 20
F32, BF16 = jnp.float32, jnp.bfloat16
OWNER_ORDER = (0, 2, 3, 1)


def iota(shape, axis):
    return lax.broadcasted_iota(jnp.int32, shape, axis)


def split_inner_order():
    src, dst = iota((LANES, LANES), 0), iota((LANES, LANES), 1)
    half, rest = dst // TILE, dst % TILE
    wanted = half * TILE + 2 * (rest % (TILE // 2)) + rest // (TILE // 2)
    return jnp.where(src == wanted, 1.0, 0.0).astype(BF16)


def twice_on_diagonal(lines):
    low = iota(lines.shape, 1) < TILE
    turned = pltpu.roll(lines, TILE, 1)
    zero = jnp.zeros_like(lines)
    return jnp.concatenate(
        [
            jnp.where(low, lines, zero),
            jnp.where(low, turned, zero),
            jnp.where(low, zero, turned),
            jnp.where(low, zero, lines),
        ],
        axis=0,
    ).astype(BF16)


def loop(count, few, body):
    if count <= few:
        for i in range(count):
            body(i)
    else:
        pl.loop(0, count)(body)


def counts_kernel(swap, left_tiles, left_each, right_each, a_hbm, b_hbm, a_slots_hbm, b_slots_hbm, *refs):
    a_out, b_out, sel, a_slots, b_slots, sems = refs
    moves = [
        pltpu.make_async_copy(src, dst, sems.at[i])
        for i, (src, dst) in enumerate(
            ((a_slots_hbm, a_slots), (b_slots_hbm, b_slots), (a_hbm, a_out), (b_hbm, b_out))
        )
    ]
    for move in moves:
        move.start()
    row, col, layer = lax.axis_index("row"), lax.axis_index("col"), lax.axis_index("layer")
    tiles, pairs = sel.shape
    tasks = tiles * TASKS
    owned = tiles // len(OWNER_ORDER)
    place = iota((tiles, tasks), 0)
    group = place // owned
    owner = jnp.zeros_like(group)
    for g, q in enumerate(OWNER_ORDER):
        owner = jnp.where(group == g, q, owner)
    tile = (owner ^ layer) * owned + place % owned
    mine = jnp.where(iota((tiles, tasks), 1) // TASKS == tile, 1.0, 0.0).astype(BF16)
    entry = iota((2 * TASKS, tasks), 0)
    at = iota((2 * TASKS, tasks), 1) % TASKS
    moves[0].wait()
    moves[1].wait()
    a_index, b_index = a_slots[...], b_slots[...]
    a_place = a_index ^ (col * left_each) if swap else a_index
    a_place = jnp.where(a_index < left_tiles, a_place, left_tiles)
    b_place = ((b_index // right_each) ^ row) * right_each + b_index % right_each
    spread = jnp.where(at == entry, a_place, 0) + jnp.where(at + TASKS == entry, b_place, 0)
    lists = lax.dot_general(
        mine, spread.astype(F32).astype(BF16), (((1,), (1,)), ((), ())), preferred_element_type=F32
    ).astype(jnp.int32)
    width = min(pairs, 1024)

    def some(part):
        here = iota((tiles, width), 1) + part * width
        total = jnp.zeros((tiles, width), F32)
        for e in range(TASKS):
            a_at, b_at = lists[:, e:e + 1], lists[:, TASKS + e:TASKS + e + 1]
            pair = jnp.where(a_at < left_tiles, b_at * left_tiles + a_at, -1)
            total = total + jnp.where(here == pair, 1.0, 0.0)
        sel[:, pl.ds(pl.multiple_of(part * width, width), width)] = total.astype(BF16)

    loop(pairs // width, 1, some)
    moves[2].wait()
    moves[3].wait()


def left_lines(a_refs, a_lines):
    order = split_inner_order()
    left_tiles = sum(r.shape[0] for r in a_refs)
    lines_at_once = min(LINES, max(1, ROWS_AT_ONCE // left_tiles))
    for i in range(0, LINES, lines_at_once):
        block = jnp.concatenate(
            [
                r[:, j * LANES:(j + 1) * LANES].astype(F32)
                for j in range(i, i + lines_at_once)
                for r in a_refs
            ],
            axis=0,
        ).astype(BF16)
        got = jnp.dot(block, order, preferred_element_type=F32)
        a_lines[i * left_tiles:(i + lines_at_once) * left_tiles, :] = got.astype(BF16)


def all_products(a_lines, b_ref, raw, prod, first):
    right_tiles = b_ref.shape[0]
    left_tiles = a_lines.shape[0] // LINES
    for i in range(LINES):
        raw[i * right_tiles:(i + 1) * right_tiles, :] = b_ref[:, i * LANES:(i + 1) * LANES].astype(F32)
    lines_at_once = min(LINES, max(1, ROWS_AT_ONCE // left_tiles))
    rows = lines_at_once * left_tiles

    def pair(p):
        right = jnp.concatenate(
            [twice_on_diagonal(raw[pl.ds(2 * p + h, LINES, stride=right_tiles), :]) for h in range(2)], axis=1
        )

        def some(part):
            at = part * rows if isinstance(part, int) else pl.multiple_of(part * rows, rows)
            got = jnp.dot(a_lines[pl.ds(at, rows), :], right, preferred_element_type=F32).astype(BF16)
            for j in range(lines_at_once):
                for h in range(2):
                    to = first + (2 * p + h) * left_tiles
                    to = to if isinstance(to, int) else pl.multiple_of(to, left_tiles)
                    prod[part * lines_at_once + j, pl.ds(to, left_tiles), :] = got[
                        j * left_tiles:(j + 1) * left_tiles, h * LANES:(h + 1) * LANES
                    ]

        loop(LINES // lines_at_once, 1, some)

    loop(right_tiles // 2, 8 if rows == a_lines.shape[0] else 1, pair)


def chosen_sums(sel, first, count, prod, put):
    for j in range(0, LINES, 2):
        right = jnp.concatenate([prod[j, :count, :], prod[j + 1, :count, :]], axis=1)
        put(
            slice(j * LANES, (j + 2) * LANES),
            jnp.dot(sel[:, first:first + count], right, preferred_element_type=F32),
        )


def first_kernel(groups, n_left, sel, *refs):
    shards = sum(groups)
    a_refs, b_refs = refs[:n_left], refs[n_left:n_left + shards]
    acc, a_lines, raw, prod = refs[n_left + shards:]
    left_lines(a_refs, a_lines)
    pairs = b_refs[0].shape[0] * a_lines.shape[0] // LINES
    shard = 0
    for count in groups:
        start = shard
        for i in range(count):
            all_products(a_lines, b_refs[shard], raw, prod, i * pairs)
            shard += 1

        def put(columns, value):
            acc[:, columns] = value if start == 0 else acc[:, columns] + value

        chosen_sums(sel, start * pairs, count * pairs, prod, put)


def last_kernel(before, sel, a_lines, b_ref, acc, own, far, cross, near, raw, prod):
    pairs = b_ref.shape[0] * a_lines.shape[0] // LINES
    owned = own.shape[0]
    all_products(a_lines, b_ref, raw, prod, 0)

    def put(columns, value):
        value = value + acc[:, columns]
        for i, out in enumerate((own, far, cross, near)):
            out[:, columns] = value[i * owned:(i + 1) * owned].astype(out.dtype)

    chosen_sums(sel, before * pairs, pairs, prod, put)


def join_kernel(far, arrived, out):
    out[...] = (far[...] + arrived[...].astype(F32)).astype(out.dtype)


def add_kernel(own, arrived, joined, out):
    out[...] = (own[...] + arrived[...].astype(F32) + joined[...].astype(F32)).astype(out.dtype)


VMEM = pl.BlockSpec(memory_space=pltpu.VMEM)
HBM = pl.BlockSpec(memory_space=pltpu.HBM)


def shape(dims, kind):
    return jax.ShapeDtypeStruct(dims, kind)


def call(kernel, outs, scratch, n_in, name, flops, moved, place=VMEM, sems=()):
    held = sum(s.dtype.itemsize * functools.reduce(lambda x, y: x * y, s.shape) for s in outs + scratch)
    return pl.pallas_call(
        kernel,
        out_shape=outs,
        in_specs=[place] * n_in,
        out_specs=[VMEM] * len(outs),
        scratch_shapes=[pltpu.VMEM(s.shape, s.dtype) for s in scratch] + list(sems),
        compiler_params=pltpu.CompilerParams(vmem_limit_bytes=min(held + 16 * MIB, 58 * MIB)),
        cost_estimate=pl.CostEstimate(flops=flops, bytes_accessed=moved, transcendentals=0),
        name=name,
    )


def exchange(x, axis, q):
    size = lax.axis_size(axis)
    return lax.ppermute(x, axis, [(i, i ^ q) for i in range(size)])


def shards(a_tiles, b_tiles, a_slots, b_slots):
    a_local = a_tiles.reshape(-1, FLAT)
    b_local = b_tiles.reshape(-1, FLAT)
    a_index = a_slots.reshape(1, -1)
    b_index = b_slots.reshape(1, -1)
    rows, cols, layers = lax.axis_size("row"), lax.axis_size("col"), lax.axis_size("layer")
    left_each, right_each = a_local.shape[0], b_local.shape[0]
    left_tiles = cols * left_each
    tiles = a_index.shape[1] // TASKS
    owned = tiles // layers
    pairs = right_each * left_tiles
    assert rows == 4 and layers == len(OWNER_ORDER)

    b_far = exchange(b_local, "row", 2)
    if cols == 2:
        a_parts = [a_local, exchange(a_local, "col", 1)]
    else:
        a_parts = [lax.all_gather(a_local, "col", axis=0, tiled=True)]
    b_near = exchange(b_local, "row", 1)
    b_last = exchange(b_far, "row", 1)

    a_here, b_here, sel = call(
        functools.partial(counts_kernel, cols == 2, left_tiles, left_each, right_each),
        [
            shape(a_local.shape, BF16),
            shape(b_local.shape, BF16),
            shape((tiles, rows * pairs), BF16),
        ],
        [shape(a_index.shape, jnp.int32)] * 2,
        4,
        "counts",
        2 * tiles * tiles * TASKS * TASKS,
        2 * MIB,
        HBM,
        [pltpu.SemaphoreType.DMA((4,))],
    )(a_local, b_local, a_index, b_index)
    if cols == 2:
        a_parts[0] = a_here

    groups = (3,) if pairs * FLAT * 2 < 4 * MIB else (1, 1, 1)
    raw = shape((right_each * LINES, LANES), F32)
    shard_flops = 2 * pairs * LINES * LANES * LANES + 2 * pairs * tiles * FLAT
    acc, a_lines = call(
        functools.partial(first_kernel, groups, len(a_parts)),
        [shape((tiles, FLAT), F32), shape((left_tiles * LINES, LANES), BF16)],
        [raw, shape((LINES, max(groups) * pairs, LANES), BF16)],
        4 + len(a_parts),
        "own_and_near",
        3 * shard_flops,
        12 * MIB,
    )(sel, *a_parts, b_here, b_near, b_far)
    own, far, cross, near = call(
        functools.partial(last_kernel, 3),
        [shape((owned, FLAT), F32)] * 2 + [shape((owned, FLAT), BF16)] * 2,
        [raw, shape((LINES, pairs, LANES), BF16)],
        4,
        "last_shard",
        shard_flops,
        4 * MIB,
    )(sel, a_lines, b_last, acc)

    arrived_cross = exchange(cross, "layer", 1)
    arrived_near = exchange(near, "layer", 1)
    (joined,) = call(
        join_kernel, [shape((owned, FLAT), BF16)], [], 2, "join_cores", owned * FLAT, 1 * MIB
    )(far, arrived_cross)
    (out,) = call(
        add_kernel, [shape((owned, FLAT), BF16)], [], 3, "add_layers", 2 * owned * FLAT, 1 * MIB
    )(own, arrived_near, exchange(joined, "layer", 2))
    return out.reshape(1, 1, owned, FLAT)


def solution(mesh):
    in_specs = (
        P("row", "layer", "col", None, None),
        P("layer", "row", "col", None, None),
        P("row", "col", "layer", None),
        P("row", "col", "layer", None),
    )
    out_specs = P("row", "col", "layer", None)
    return jax.shard_map(shards, mesh=mesh, in_specs=in_specs, out_specs=out_specs, check_vma=False)
```

time: 128 us -> 26.9 us (0.21)
  local copies, waits for them, and re-layouts: 52.9 us -> 3.11 us
  blocking collectives: 21.9 us -> 0 us
  waiting for transfers between devices: 24.9 us -> 7.97 us
  between operations: 13.5 us -> 0.04 us
  matrix products: 11.1 us -> 0 us
  starting transfers between devices: 0.01 us -> 9.77 us
  Pallas kernels: 0 us -> 5.83 us
  other arithmetic: 2.84 us -> 0 us
    gather x4 -> x0, local copies, waits for them, and re-layouts: 47.3 us -> none  [the longest x2 23.7 us: tile_sums(): jnp.take(b_panel, b_index, axis=0).reshape(tiles_here, TASKS, TILE, TILE)]
    unnamed x2 -> x0, waiting for transfers between devices: 24.9 us -> none
    all_gather x2 -> x0, blocking collectives: 21.9 us -> none  [the longest x1 15.8 us: shards(): b_panel = lax.all_gather(b_local, 'row', axis=0, tiled=True)]
    dot_general x1 -> x0, matrix products: 11.1 us -> none  [tile_sums(): jnp.einsum('sgik,sgkj->sij', a_stack, b_stack, preferred_element_type=jnp...]
    ppermute x0 -> x7, starting transfers between devices: none -> 9.77 us  [exchange(): return lax.ppermute(x, axis, [(i, i ^ q) for i in range(size)])]
    ppermute x0 -> x7, waiting for transfers between devices: none -> 7.97 us  [exchange(): return lax.ppermute(x, axis, [(i, i ^ q) for i in range(size)])]
    pallas_call x0 -> x5, Pallas kernels: none -> 5.83 us  [the longest x1 2.91 us: shards(): call(functools.partial(first_kernel, groups, len(a_parts)), [shape((tiles...]
    convert_element_type x1 -> x0, local copies, waits for them, and re-layouts: 1.73 us -> none  [shards(): partial_value.astype(jnp.bfloat16)]
  transfers between devices with their start and end apart: 1 -> 7, of which waited for: 1 -> 3; matrix products, arithmetic and copies ran while one was open for 0% -> 0% of each run, Pallas kernels for 0% -> 15%
where the time goes in v1:
time: 26.9 us; the launch traced here: 26.7 us
  starting transfers between devices  9.77 us (36%)
  waiting for transfers between devices  7.97 us (30%)
  Pallas kernels  5.83 us (22%)
  local copies, waits for them, and re-layouts  3.11 us (12%)
    ppermute x7, starting transfers between devices, exchange(): return lax.ppermute(x, axis, [(i, i ^ q) for i in range(size)])  9.77 us
    ppermute x7, waiting for transfers between devices, exchange(): return lax.ppermute(x, axis, [(i, i ^ q) for i in range(size)])  7.97 us
    unnamed x8, local copies, waits for them, and re-layouts  3.11 us
    pallas_call x1, Pallas kernels, shards(): call(functools.partial(first_kernel, groups, len(a_parts)), [shape((tiles...  2.91 us
    pallas_call x1, Pallas kernels, shards(): call(functools.partial(last_kernel, 3), [shape((owned, FLAT), F32)] * 2 +...  1.1 us
    pallas_call x1, Pallas kernels, shards(): call(functools.partial(counts_kernel, cols == 2, left_tiles, left_each, r...  1.04 us
    pallas_call x1, Pallas kernels, shards(): call(add_kernel, [shape((owned, FLAT), BF16)], [], 3, 'add_layers', 2 * o...  0.74 us
  transfers between devices with their start and end apart: 7, of which 3 were waited for; matrix products, arithmetic and copies ran while one was open for 0% of the time, Pallas kernels for 15%

profile of v1, /device:TPU:0, one launch (start us, length us, event | category | flops | bytes accessed | tf_op | source)
XLA Modules:
  0.0 26.7 jit_solution(7631084279305713654)
XLA Ops:
  0.0 4.0 %collective-permute-start.2 = (bf16[16,4096]{1,0:T(8,128)(2,1)}, bf16[16,4096]{1,0:T(8,128)(2,1)S(1)}, u32[]{:S(2)}, u32[]{:S(2)}) collective-permute-start(bf16[16,4096]{1,0:T(8,128)(2,1)} %bitcast.5), channel_id=1, source_target_pairs={{0,16},{8,24},{16,0},{24,8},{1,17},{9,25},{17,1},{25,9},{2,18},{10... | collective-permute-start | bytes 393224 | tf_op jit(solution)/shard_map/ppermute | solution.py:223
  4.0 1.6 %collective-permute-start.1 = (bf16[16,4096]{1,0:T(8,128)(2,1)}, bf16[16,4096]{1,0:T(8,128)(2,1)S(1)}, u32[]{:S(2)}, u32[]{:S(2)}) collective-permute-start(bf16[16,4096]{1,0:T(8,128)(2,1)} %bitcast.6), channel_id=1, source_target_pairs={{0,8},{8,0},{16,24},{24,16},{1,9},{9,1},{17,25},{25,17},{2,10},{10... | collective-permute-start | bytes 393224 | tf_op jit(solution)/shard_map/ppermute | solution.py:223
  5.6 1.5 %collective-permute-start = (bf16[8,4096]{1,0:T(8,128)(2,1)}, bf16[8,4096]{1,0:T(8,128)(2,1)S(1)}, u32[]{:S(2)}, u32[]{:S(2)}) collective-permute-start(bf16[8,4096]{1,0:T(8,128)(2,1)} %bitcast.8), channel_id=1, source_target_pairs={{0,4},{4,0},{1,5},{5,1},{2,6},{6,2},{3,7},{7,3},{8,12},{12,8},{9,1... | collective-permute-start | bytes 196616 | tf_op jit(solution)/shard_map/ppermute | solution.py:223
  7.1 0.0 copy-start
  7.1 0.9 %copy-done = bf16[1,1,1,16,4096]{4,3,2,1,0:T(8,128)(2,1)S(1)} copy-done((bf16[1,1,1,16,4096]{4,3,2,1,0:T(8,128)(2,1)S(1)}, bf16[1,1,1,16,4096]{4,3,2,1,0:T(8,128)(2,1)}, u32[]{:S(2)}) %copy-start) | copy-done | bytes 131096
  8.0 0.0 copy-start.1
  8.0 0.8 %copy-done.1 = bf16[1,1,1,8,4096]{4,3,2,1,0:T(8,128)(2,1)S(1)} copy-done((bf16[1,1,1,8,4096]{4,3,2,1,0:T(8,128)(2,1)S(1)}, bf16[1,1,1,8,4096]{4,3,2,1,0:T(8,128)(2,1)}, u32[]{:S(2)}) %copy-start.1) | copy-done | bytes 65560
  8.9 0.7 %copy-done.2 = s32[1,1,1,768]{3,2,1,0:T(1,128)S(1)} copy-done((s32[1,1,1,768]{3,2,1,0:T(1,128)S(1)}, s32[1,1,1,768]{3,2,1,0:T(1,128)}, u32[]{:S(2)}) %copy-start.2) | copy-done | bytes 3096
  9.5 0.7 %copy-done.3 = s32[1,1,1,768]{3,2,1,0:T(1,128)S(1)} copy-done((s32[1,1,1,768]{3,2,1,0:T(1,128)S(1)}, s32[1,1,1,768]{3,2,1,0:T(1,128)}, u32[]{:S(2)}) %copy-start.3) | copy-done | bytes 3096
  10.2 1.0 %counts.1 = (bf16[8,4096]{1,0:T(8,128)(2,1)S(1)}, bf16[16,4096]{1,0:T(8,128)(2,1)S(1)}, bf16[96,1024]{1,0:T(8,128)(2,1)S(1)}) custom-call(bf16[8,4096]{1,0:T(8,128)(2,1)S(1)} %bitcast.9, bf16[16,4096]{1,0:T(8,128)(2,1)S(1)} %bitcast.7, s32[1,768]{1,0:T(1,128)S(1)} %bitcast.10, s32[1,768]{1,0:T(1,128)S(1)} %bitcast.11), custom_call_target="tpu_custom_call" | custom-call | flops 1179648 | bytes 2097152 | tf_op jit(solution)/shard_map/counts/pallas_call | solution.py:247
  11.3 0.0 collective-permute-done.2.refs_4_
  11.3 0.5 %collective-permute-start.3 = (bf16[16,4096]{1,0:T(8,128)(2,1)S(1)}, bf16[16,4096]{1,0:T(8,128)(2,1)S(1)}, u32[]{:S(2)}, u32[]{:S(2)}) collective-permute-start(bf16[16,4096]{1,0:T(8,128)(2,1)S(1)} %collective-permute-done.2.refs_4_), channel_id=1, source_target_pairs={{0,8},{8,0},{16,24},{24,16},{1,9},{9,1},{17,25},{25,17},{2,10},{10... | collective-permute-start | bytes 393224 | tf_op jit(solution)/shard_map/ppermute | solution.py:223
  11.8 0.0 collective-permute-done.refs_1_
  11.8 0.0 collective-permute-done.1.refs_3_
  11.8 2.9 %own_and_near.1 = (f32[96,4096]{1,0:T(8,128)S(1)}, bf16[512,128]{1,0:T(8,128)(2,1)S(1)}) custom-call(bf16[96,1024]{1,0:T(8,128)(2,1)S(1)} %get-tuple-element.14.sel, bf16[8,4096]{1,0:T(8,128)(2,1)S(1)} %get-tuple-element.15.refs_0_, bf16[8,4096]{1,0:T(8,128)(2,1)S(1)} %collective-permute-done.refs_1_, bf16[16,4096]{1,0:T(8,128)(2,1)S(1)} %get-tuple-element.16.refs_2_, ...), custom_call_target="tpu_custom_call" | custom-call | flops 1409286144 | bytes 12582912 | tf_op jit(solution)/shard_map/own_and_near/pallas_call | solution.py:268
  14.7 1.6 %collective-permute-done.3.b_ref = bf16[16,4096]{1,0:T(8,128)(2,1)S(1)} collective-permute-done((bf16[16,4096]{1,0:T(8,128)(2,1)S(1)}, bf16[16,4096]{1,0:T(8,128)(2,1)S(1)}, u32[]{:S(2)}, u32[]{:S(2)}) %collective-permute-start.3) | collective-permute-done | bytes 131104 | tf_op jit(solution)/shard_map/ppermute | solution.py:223
  16.3 1.1 %last_shard.1 = (f32[24,4096]{1,0:T(8,128)S(1)}, f32[24,4096]{1,0:T(8,128)S(1)}, bf16[24,4096]{1,0:T(8,128)(2,1)S(1)}, bf16[24,4096]{1,0:T(8,128)(2,1)S(1)}) custom-call(bf16[96,1024]{1,0:T(8,128)(2,1)S(1)} %get-tuple-element.14.sel, bf16[512,128]{1,0:T(8,128)(2,1)S(1)} %get-tuple-element.17.a_lines, bf16[16,4096]{1,0:T(8,128)(2,1)S(1)} %collective-permute-done.3.b_ref, ...), custom_call_target="tpu_custom_call" | custom-call | flops 469762048 | bytes 4194304 | tf_op jit(solution)/shard_map/last_shard/pallas_call | solution.py:277
  17.4 0.1 collective-permute-start.5
  17.5 0.5 %collective-permute-start.4 = (bf16[24,4096]{1,0:T(8,128)(2,1)S(1)}, bf16[24,4096]{1,0:T(8,128)(2,1)S(1)}, u32[]{:S(2)}, u32[]{:S(2)}) collective-permute-start(bf16[24,4096]{1,0:T(8,128)(2,1)S(1)} %get-tuple-element.20), channel_id=1, source_target_pairs={{0,1},{1,0},{2,3},{3,2},{4,5},{5,4},{6,7},{7,6},{8,9},{9,8},{10,11... | collective-permute-start | bytes 589832 | tf_op jit(solution)/shard_map/ppermute | solution.py:223
  18.0 0.9 %collective-permute-done.5.arrived = bf16[24,4096]{1,0:T(8,128)(2,1)S(1)} collective-permute-done((bf16[24,4096]{1,0:T(8,128)(2,1)S(1)}, bf16[24,4096]{1,0:T(8,128)(2,1)S(1)}, u32[]{:S(2)}, u32[]{:S(2)}) %collective-permute-start.5) | collective-permute-done | bytes 196640 | tf_op jit(solution)/shard_map/ppermute | solution.py:223
  19.0 1.6 %collective-permute-start.6 = (bf16[24,4096]{1,0:T(8,128)(2,1)S(1)}, bf16[24,4096]{1,0:T(8,128)(2,1)S(1)}, u32[]{:S(2)}, u32[]{:S(2)}) collective-permute-start(bf16[24,4096]{1,0:T(8,128)(2,1)S(1)} %join_cores.1), channel_id=1, source_target_pairs={{0,2},{1,3},{2,0},{3,1},{4,6},{5,7},{6,4},{7,5},{8,10},{9,11},{10,... | collective-permute-start | bytes 589832 | tf_op jit(solution)/shard_map/ppermute | solution.py:223
  20.6 0.0 collective-permute-done.4.arrived
  20.6 5.4 %collective-permute-done.6.joined = bf16[24,4096]{1,0:T(8,128)(2,1)S(1)} collective-permute-done((bf16[24,4096]{1,0:T(8,128)(2,1)S(1)}, bf16[24,4096]{1,0:T(8,128)(2,1)S(1)}, u32[]{:S(2)}, u32[]{:S(2)}) %collective-permute-start.6) | collective-permute-done | bytes 196640 | tf_op jit(solution)/shard_map/ppermute | solution.py:223
  26.0 0.7 %add_layers.1 = bf16[24,4096]{1,0:T(8,128)(2,1)} custom-call(f32[24,4096]{1,0:T(8,128)S(1)} %get-tuple-element.19.own, bf16[24,4096]{1,0:T(8,128)(2,1)S(1)} %collective-permute-done.4.arrived, bf16[24,4096]{1,0:T(8,128)(2,1)S(1)} %collective-permute-done.6.joined), custom_call_target="tpu_custom_call" | custom-call | flops 196608 | bytes 1048576 | tf_op jit(solution)/shard_map/add_layers/pallas_call | solution.py:292
  (3 shorter events, 0.0 us)
Async XLA Ops:
  0.0 11.3 %collective-permute-start.2 = (bf16[16,4096]{1,0:T(8,128)(2,1)}, bf16[16,4096]{1,0:T(8,128)(2,1)S(1)}, u32[]{:S(2)}, u32[]{:S(2)}) collective-permute-start(bf16[16,4096]{1,0:T(8,128)(2,1)} %bitcast.5), channel_id=1, source_target_pairs={{0,16},{8,24},{16,0},{24,8},{1,17},{9,25},{17,1},{25,9},{2,18},{10... | collective-permute-start | bytes 393224 | tf_op jit(solution)/shard_map/ppermute | solution.py:223
  4.0 7.8 %collective-permute-start.1 = (bf16[16,4096]{1,0:T(8,128)(2,1)}, bf16[16,4096]{1,0:T(8,128)(2,1)S(1)}, u32[]{:S(2)}, u32[]{:S(2)}) collective-permute-start(bf16[16,4096]{1,0:T(8,128)(2,1)} %bitcast.6), channel_id=1, source_target_pairs={{0,8},{8,0},{16,24},{24,16},{1,9},{9,1},{17,25},{25,17},{2,10},{10... | collective-permute-start | bytes 393224 | tf_op jit(solution)/shard_map/ppermute | solution.py:223
  5.6 6.2 %collective-permute-start = (bf16[8,4096]{1,0:T(8,128)(2,1)}, bf16[8,4096]{1,0:T(8,128)(2,1)S(1)}, u32[]{:S(2)}, u32[]{:S(2)}) collective-permute-start(bf16[8,4096]{1,0:T(8,128)(2,1)} %bitcast.8), channel_id=1, source_target_pairs={{0,4},{4,0},{1,5},{5,1},{2,6},{6,2},{3,7},{7,3},{8,12},{12,8},{9,1... | collective-permute-start | bytes 196616 | tf_op jit(solution)/shard_map/ppermute | solution.py:223
  7.1 0.9 %copy-start = (bf16[1,1,1,16,4096]{4,3,2,1,0:T(8,128)(2,1)S(1)}, bf16[1,1,1,16,4096]{4,3,2,1,0:T(8,128)(2,1)}, u32[]{:S(2)}) copy-start(bf16[1,1,1,16,4096]{4,3,2,1,0:T(8,128)(2,1)} %param.5) | copy-start | bytes 393220
  8.0 0.8 %copy-start.1 = (bf16[1,1,1,8,4096]{4,3,2,1,0:T(8,128)(2,1)S(1)}, bf16[1,1,1,8,4096]{4,3,2,1,0:T(8,128)(2,1)}, u32[]{:S(2)}) copy-start(bf16[1,1,1,8,4096]{4,3,2,1,0:T(8,128)(2,1)} %param.4) | copy-start | bytes 196612
  8.9 0.7 %copy-start.2 = (s32[1,1,1,768]{3,2,1,0:T(1,128)S(1)}, s32[1,1,1,768]{3,2,1,0:T(1,128)}, u32[]{:S(2)}) copy-start(s32[1,1,1,768]{3,2,1,0:T(1,128)} %param.6) | copy-start | bytes 9220
  9.5 0.7 %copy-start.3 = (s32[1,1,1,768]{3,2,1,0:T(1,128)S(1)}, s32[1,1,1,768]{3,2,1,0:T(1,128)}, u32[]{:S(2)}) copy-start(s32[1,1,1,768]{3,2,1,0:T(1,128)} %param.7) | copy-start | bytes 9220
  11.3 5.0 %collective-permute-start.3 = (bf16[16,4096]{1,0:T(8,128)(2,1)S(1)}, bf16[16,4096]{1,0:T(8,128)(2,1)S(1)}, u32[]{:S(2)}, u32[]{:S(2)}) collective-permute-start(bf16[16,4096]{1,0:T(8,128)(2,1)S(1)} %collective-permute-done.2.refs_4_), channel_id=1, source_target_pairs={{0,8},{8,0},{16,24},{24,16},{1,9},{9,1},{17,25},{25,17},{2,10},{10... | collective-permute-start | bytes 393224 | tf_op jit(solution)/shard_map/ppermute | solution.py:223
  17.4 1.5 %collective-permute-start.5 = (bf16[24,4096]{1,0:T(8,128)(2,1)S(1)}, bf16[24,4096]{1,0:T(8,128)(2,1)S(1)}, u32[]{:S(2)}, u32[]{:S(2)}) collective-permute-start(bf16[24,4096]{1,0:T(8,128)(2,1)S(1)} %get-tuple-element.22), channel_id=1, source_target_pairs={{0,1},{1,0},{2,3},{3,2},{4,5},{5,4},{6,7},{7,6},{8,9},{9,8},{10,11... | collective-permute-start | bytes 589832 | tf_op jit(solution)/shard_map/ppermute | solution.py:223
  17.5 3.1 %collective-permute-start.4 = (bf16[24,4096]{1,0:T(8,128)(2,1)S(1)}, bf16[24,4096]{1,0:T(8,128)(2,1)S(1)}, u32[]{:S(2)}, u32[]{:S(2)}) collective-permute-start(bf16[24,4096]{1,0:T(8,128)(2,1)S(1)} %get-tuple-element.20), channel_id=1, source_target_pairs={{0,1},{1,0},{2,3},{3,2},{4,5},{5,4},{6,7},{7,6},{8,9},{9,8},{10,11... | collective-permute-start | bytes 589832 | tf_op jit(solution)/shard_map/ppermute | solution.py:223
  19.0 7.0 %collective-permute-start.6 = (bf16[24,4096]{1,0:T(8,128)(2,1)S(1)}, bf16[24,4096]{1,0:T(8,128)(2,1)S(1)}, u32[]{:S(2)}, u32[]{:S(2)}) collective-permute-start(bf16[24,4096]{1,0:T(8,128)(2,1)S(1)} %join_cores.1), channel_id=1, source_target_pairs={{0,2},{1,3},{2,0},{3,1},{4,6},{5,7},{6,4},{7,5},{8,10},{9,11},{10,... | collective-permute-start | bytes 589832 | tf_op jit(solution)/shard_map/ppermute | solution.py:223

commit v2 on v1

--- a/solution.py
+++ b/solution.py
@@ -14,6 +14,7 @@
 LINES = FLAT // LANES
 ROWS_AT_ONCE = 512
 MIB = 1 << 20
+STAGE_FLOPS = 2 * 10**9
 F32, BF16 = jnp.float32, jnp.bfloat16
 OWNER_ORDER = (0, 2, 3, 1)
 
@@ -52,16 +53,16 @@
         pl.loop(0, count)(body)
 
 
-def counts_kernel(swap, left_tiles, left_each, right_each, a_hbm, b_hbm, a_slots_hbm, b_slots_hbm, *refs):
-    a_out, b_out, sel, a_slots, b_slots, sems = refs
-    moves = [
-        pltpu.make_async_copy(src, dst, sems.at[i])
-        for i, (src, dst) in enumerate(
-            ((a_slots_hbm, a_slots), (b_slots_hbm, b_slots), (a_hbm, a_out), (b_hbm, b_out))
-        )
-    ]
-    for move in moves:
-        move.start()
+def stage_kernel(b_ref, out, upper):
+    out[...] = b_ref[...]
+    upper[...] = b_ref[upper.shape[0]:, :]
+
+
+def lower_kernel(b_ref, out):
+    out[...] = b_ref[:out.shape[0], :]
+
+
+def counts_kernel(swap, left_tiles, left_each, right_each, a_slots, b_slots, sel):
     row, col, layer = lax.axis_index("row"), lax.axis_index("col"), lax.axis_index("layer")
     tiles, pairs = sel.shape
     tasks = tiles * TASKS
@@ -75,8 +76,6 @@
     mine = jnp.where(iota((tiles, tasks), 1) // TASKS == tile, 1.0, 0.0).astype(BF16)
     entry = iota((2 * TASKS, tasks), 0)
     at = iota((2 * TASKS, tasks), 1) % TASKS
-    moves[0].wait()
-    moves[1].wait()
     a_index, b_index = a_slots[...], b_slots[...]
     a_place = a_index ^ (col * left_each) if swap else a_index
     a_place = jnp.where(a_index < left_tiles, a_place, left_tiles)
@@ -97,8 +96,6 @@
         sel[:, pl.ds(pl.multiple_of(part * width, width), width)] = total.astype(BF16)
 
     loop(pairs // width, 1, some)
-    moves[2].wait()
-    moves[3].wait()
 
 
 def left_lines(a_refs, a_lines):
@@ -175,17 +172,21 @@
         chosen_sums(sel, start * pairs, count * pairs, prod, put)
 
 
-def last_kernel(before, sel, a_lines, b_ref, acc, own, far, cross, near, raw, prod):
-    pairs = b_ref.shape[0] * a_lines.shape[0] // LINES
+def last_kernel(start, n_parts, sel, a_lines, acc, *refs):
+    b_refs, (own, far, cross, near, raw, prod) = refs[:n_parts], refs[n_parts:]
+    each = a_lines.shape[0] // LINES
     owned = own.shape[0]
-    all_products(a_lines, b_ref, raw, prod, 0)
+    done = 0
+    for b_ref in b_refs:
+        all_products(a_lines, b_ref, raw, prod, done)
+        done += b_ref.shape[0] * each
 
     def put(columns, value):
         value = value + acc[:, columns]
         for i, out in enumerate((own, far, cross, near)):
             out[:, columns] = value[i * owned:(i + 1) * owned].astype(out.dtype)
 
-    chosen_sums(sel, before * pairs, pairs, prod, put)
+    chosen_sums(sel, start, done, prod, put)
 
 
 def join_kernel(far, arrived, out):
@@ -197,21 +198,20 @@
 
 
 VMEM = pl.BlockSpec(memory_space=pltpu.VMEM)
-HBM = pl.BlockSpec(memory_space=pltpu.HBM)
 
 
 def shape(dims, kind):
     return jax.ShapeDtypeStruct(dims, kind)
 
 
-def call(kernel, outs, scratch, n_in, name, flops, moved, place=VMEM, sems=()):
+def call(kernel, outs, scratch, n_in, name, flops, moved):
     held = sum(s.dtype.itemsize * functools.reduce(lambda x, y: x * y, s.shape) for s in outs + scratch)
     return pl.pallas_call(
         kernel,
         out_shape=outs,
-        in_specs=[place] * n_in,
+        in_specs=[VMEM] * n_in,
         out_specs=[VMEM] * len(outs),
-        scratch_shapes=[pltpu.VMEM(s.shape, s.dtype) for s in scratch] + list(sems),
+        scratch_shapes=[pltpu.VMEM(s.shape, s.dtype) for s in scratch],
         compiler_params=pltpu.CompilerParams(vmem_limit_bytes=min(held + 16 * MIB, 58 * MIB)),
         cost_estimate=pl.CostEstimate(flops=flops, bytes_accessed=moved, transcendentals=0),
         name=name,
@@ -241,29 +241,33 @@
         a_parts = [a_local, exchange(a_local, "col", 1)]
     else:
         a_parts = [lax.all_gather(a_local, "col", axis=0, tiled=True)]
-    b_near = exchange(b_local, "row", 1)
-    b_last = exchange(b_far, "row", 1)
-
-    a_here, b_here, sel = call(
+    upper = right_each // 2
+    b_here, b_upper = call(
+        stage_kernel,
+        [shape(b_local.shape, BF16), shape((upper, FLAT), BF16)],
+        [],
+        1,
+        "stage",
+        STAGE_FLOPS,
+        MIB,
+    )(b_local)
+    b_near = exchange(b_here, "row", 1)
+    last_upper = exchange(b_upper, "row", 3)
+    (sel,) = call(
         functools.partial(counts_kernel, cols == 2, left_tiles, left_each, right_each),
-        [
-            shape(a_local.shape, BF16),
-            shape(b_local.shape, BF16),
-            shape((tiles, rows * pairs), BF16),
-        ],
-        [shape(a_index.shape, jnp.int32)] * 2,
-        4,
+        [shape((tiles, rows * pairs), BF16)],
+        [],
+        2,
         "counts",
         2 * tiles * tiles * TASKS * TASKS,
-        2 * MIB,
-        HBM,
-        [pltpu.SemaphoreType.DMA((4,))],
-    )(a_local, b_local, a_index, b_index)
-    if cols == 2:
-        a_parts[0] = a_here
+        MIB,
+    )(a_index, b_index)
+    (b_lower,) = call(lower_kernel, [shape((right_each - upper, FLAT), BF16)], [], 1, "lower", upper * FLAT, MIB)(b_far)
+    last_lower = exchange(b_lower, "row", 1)
 
     groups = (3,) if pairs * FLAT * 2 < 4 * MIB else (1, 1, 1)
     raw = shape((right_each * LINES, LANES), F32)
+    half_raw = shape((upper * LINES, LANES), F32)
     shard_flops = 2 * pairs * LINES * LANES * LANES + 2 * pairs * tiles * FLAT
     acc, a_lines = call(
         functools.partial(first_kernel, groups, len(a_parts)),
@@ -275,14 +279,14 @@
         12 * MIB,
     )(sel, *a_parts, b_here, b_near, b_far)
     own, far, cross, near = call(
-        functools.partial(last_kernel, 3),
+        functools.partial(last_kernel, 3 * pairs, 2),
         [shape((owned, FLAT), F32)] * 2 + [shape((owned, FLAT), BF16)] * 2,
-        [raw, shape((LINES, pairs, LANES), BF16)],
-        4,
+        [half_raw, shape((LINES, pairs, LANES), BF16)],
+        5,
         "last_shard",
         shard_flops,
         4 * MIB,
-    )(sel, a_lines, b_last, acc)
+    )(sel, a_lines, acc, last_lower, last_upper)
 
     arrived_cross = exchange(cross, "layer", 1)
     arrived_near = exchange(near, "layer", 1)

time: 26.9 us -> 25.7 us (0.955)
  local copies, waits for them, and re-layouts: 3.11 us -> 0.95 us
  starting transfers between devices: 9.77 us -> 11.1 us
  Pallas kernels: 5.83 us -> 5.52 us
    unnamed x8, local copies, waits for them, and re-layouts: 3.11 us -> 0.95 us
    ppermute x7 -> x8, starting transfers between devices: 9.77 us -> 11.1 us  [exchange(): return lax.ppermute(x, axis, [(i, i ^ q) for i in range(size)])]
    pallas_call x1, Pallas kernels: 1.04 us -> 0.73 us  [shards(): call(functools.partial(counts_kernel, cols == 2, left_tiles, left_each, r...]
    ppermute x7 -> x8, waiting for transfers between devices: 7.97 us -> 7.9 us  [exchange(): return lax.ppermute(x, axis, [(i, i ^ q) for i in range(size)])]
    pallas_call x1 -> x3, Pallas kernels: 1.1 us -> 1.12 us  [the longest x1 1.1 us: shards(): call(functools.partial(last_kernel, 3 * pairs, 2), [shape((owned, FLAT),...]
  transfers between devices with their start and end apart: 7 -> 8, of which waited for: 3 -> 4; matrix products, arithmetic and copies ran while one was open for 0% -> 0% of each run, Pallas kernels for 15% -> 14%
where the time goes in v2:
time: 25.7 us; the launch traced here: 25.5 us
  starting transfers between devices  11.1 us (43%)
  waiting for transfers between devices  7.9 us (31%)
  Pallas kernels  5.52 us (21%)
  local copies, waits for them, and re-layouts  0.95 us (4%)
    ppermute x8, starting transfers between devices, exchange(): return lax.ppermute(x, axis, [(i, i ^ q) for i in range(size)])  11.1 us
    ppermute x8, waiting for transfers between devices, exchange(): return lax.ppermute(x, axis, [(i, i ^ q) for i in range(size)])  7.9 us
    pallas_call x1, Pallas kernels, shards(): call(functools.partial(first_kernel, groups, len(a_parts)), [shape((tiles...  2.9 us
    pallas_call x1, Pallas kernels, shards(): call(functools.partial(last_kernel, 3 * pairs, 2), [shape((owned, FLAT),...  1.1 us
    unnamed x8, local copies, waits for them, and re-layouts  0.95 us
    pallas_call x1, Pallas kernels, shards(): call(add_kernel, [shape((owned, FLAT), BF16)], [], 3, 'add_layers', 2 * o...  0.74 us
    pallas_call x1, Pallas kernels, shards(): call(functools.partial(counts_kernel, cols == 2, left_tiles, left_each, r...  0.73 us
  transfers between devices with their start and end apart: 8, of which 4 were waited for; matrix products, arithmetic and copies ran while one was open for 0% of the time, Pallas kernels for 14%

profile of v2, /device:TPU:0, one launch (start us, length us, event | category | flops | bytes accessed | tf_op | source)
XLA Modules:
  0.0 25.5 jit_solution(209913672343246573)
XLA Ops:
  0.0 4.0 %collective-permute-start.2 = (bf16[16,4096]{1,0:T(8,128)(2,1)}, bf16[16,4096]{1,0:T(8,128)(2,1)S(1)}, u32[]{:S(2)}, u32[]{:S(2)}) collective-permute-start(bf16[16,4096]{1,0:T(8,128)(2,1)} %bitcast.7), channel_id=1, source_target_pairs={{0,16},{8,24},{16,0},{24,8},{1,17},{9,25},{17,1},{25,9},{2,18},{10... | collective-permute-start | bytes 393224 | tf_op jit(solution)/shard_map/ppermute | solution.py:223
  4.0 0.9 %copy-done.2 = bf16[1,1,1,16,4096]{4,3,2,1,0:T(8,128)(2,1)S(1)} copy-done((bf16[1,1,1,16,4096]{4,3,2,1,0:T(8,128)(2,1)S(1)}, bf16[1,1,1,16,4096]{4,3,2,1,0:T(8,128)(2,1)}, u32[]{:S(2)}) %copy-start.2) | copy-done | bytes 131096
  5.0 1.6 %collective-permute-start.1 = (bf16[16,4096]{1,0:T(8,128)(2,1)S(1)}, bf16[16,4096]{1,0:T(8,128)(2,1)S(1)}, u32[]{:S(2)}, u32[]{:S(2)}) collective-permute-start(bf16[16,4096]{1,0:T(8,128)(2,1)S(1)} %get-tuple-element.13.refs_2_), channel_id=1, source_target_pairs={{0,8},{8,0},{16,24},{24,16},{1,9},{9,1},{17,25},{25,17},{2,10},{10... | collective-permute-start | bytes 393224 | tf_op jit(solution)/shard_map/ppermute | solution.py:223
  6.6 0.0 copy-done.3
  6.6 1.5 %collective-permute-start = (bf16[8,4096]{1,0:T(8,128)(2,1)S(1)}, bf16[8,4096]{1,0:T(8,128)(2,1)S(1)}, u32[]{:S(2)}, u32[]{:S(2)}) collective-permute-start(bf16[8,4096]{1,0:T(8,128)(2,1)S(1)} %bitcast.9), channel_id=1, source_target_pairs={{0,4},{4,0},{1,5},{5,1},{2,6},{6,2},{3,7},{7,3},{8,12},{12,8},{9,1... | collective-permute-start | bytes 196616 | tf_op jit(solution)/shard_map/ppermute | solution.py:223
  8.1 0.5 %collective-permute-start.4 = (bf16[8,4096]{1,0:T(8,128)(2,1)S(1)}, bf16[8,4096]{1,0:T(8,128)(2,1)S(1)}, u32[]{:S(2)}, u32[]{:S(2)}) collective-permute-start(bf16[8,4096]{1,0:T(8,128)(2,1)S(1)} %get-tuple-element.16), channel_id=1, source_target_pairs={{0,24},{8,16},{16,8},{24,0},{1,25},{9,17},{17,9},{25,1},{2,26},{10... | collective-permute-start | bytes 196616 | tf_op jit(solution)/shard_map/ppermute | solution.py:223
  8.7 0.0 copy-done
  8.7 0.0 copy-done.1
  8.7 0.7 %counts.1.sel = bf16[96,1024]{1,0:T(8,128)(2,1)S(1)} custom-call(s32[1,768]{1,0:T(1,128)S(1)} %bitcast.5, s32[1,768]{1,0:T(1,128)S(1)} %bitcast.6), custom_call_target="tpu_custom_call" | custom-call | flops 1179648 | bytes 1048576 | tf_op jit(solution)/shard_map/counts/pallas_call | solution.py:256
  9.4 1.4 %collective-permute-done.2.refs_4_.b_ref = bf16[16,4096]{1,0:T(8,128)(2,1)S(1)} collective-permute-done((bf16[16,4096]{1,0:T(8,128)(2,1)}, bf16[16,4096]{1,0:T(8,128)(2,1)S(1)}, u32[]{:S(2)}, u32[]{:S(2)}) %collective-permute-start.2) | collective-permute-done | bytes 131104 | tf_op jit(solution)/shard_map/ppermute | solution.py:223
  10.9 1.1 %collective-permute-start.3 = (bf16[8,4096]{1,0:T(8,128)(2,1)S(1)}, bf16[8,4096]{1,0:T(8,128)(2,1)S(1)}, u32[]{:S(2)}, u32[]{:S(2)}) collective-permute-start(bf16[8,4096]{1,0:T(8,128)(2,1)S(1)} %lower.1), channel_id=1, source_target_pairs={{0,8},{8,0},{16,24},{24,16},{1,9},{9,1},{17,25},{25,17},{2,10},{10... | collective-permute-start | bytes 196616 | tf_op jit(solution)/shard_map/ppermute | solution.py:223
  12.0 0.0 collective-permute-done.refs_1_
  12.0 0.0 collective-permute-done.1.refs_3_
  12.0 2.9 %own_and_near.1 = (f32[96,4096]{1,0:T(8,128)S(1)}, bf16[512,128]{1,0:T(8,128)(2,1)S(1)}) custom-call(bf16[96,1024]{1,0:T(8,128)(2,1)S(1)} %counts.1.sel, bf16[8,4096]{1,0:T(8,128)(2,1)S(1)} %bitcast.10, bf16[8,4096]{1,0:T(8,128)(2,1)S(1)} %collective-permute-done.refs_1_, bf16[16,4096]{1,0:T(8,128)(2,1)S(1)} %get-tuple-element.13.refs_2_, ...), custom_call_target="tpu_custom_call" | custom-call | flops 1409286144 | bytes 12582912 | tf_op jit(solution)/shard_map/own_and_near/pallas_call | solution.py:272
  14.9 0.0 collective-permute-done.4.refs_1_
  14.9 0.2 collective-permute-done.3.refs_0_
  15.1 1.1 %last_shard.1 = (f32[24,4096]{1,0:T(8,128)S(1)}, f32[24,4096]{1,0:T(8,128)S(1)}, bf16[24,4096]{1,0:T(8,128)(2,1)S(1)}, bf16[24,4096]{1,0:T(8,128)(2,1)S(1)}) custom-call(bf16[96,1024]{1,0:T(8,128)(2,1)S(1)} %counts.1.sel, bf16[512,128]{1,0:T(8,128)(2,1)S(1)} %get-tuple-element.14.a_lines, f32[96,4096]{1,0:T(8,128)S(1)} %get-tuple-element.15.acc, ...), custom_call_target="tpu_custom_call" | custom-call | flops 469762048 | bytes 4194304 | tf_op jit(solution)/shard_map/last_shard/pallas_call | solution.py:281
  16.2 0.1 collective-permute-start.6
  16.3 0.5 %collective-permute-start.5 = (bf16[24,4096]{1,0:T(8,128)(2,1)S(1)}, bf16[24,4096]{1,0:T(8,128)(2,1)S(1)}, u32[]{:S(2)}, u32[]{:S(2)}) collective-permute-start(bf16[24,4096]{1,0:T(8,128)(2,1)S(1)} %get-tuple-element.18), channel_id=1, source_target_pairs={{0,1},{1,0},{2,3},{3,2},{4,5},{5,4},{6,7},{7,6},{8,9},{9,8},{10,11... | collective-permute-start | bytes 589832 | tf_op jit(solution)/shard_map/ppermute | solution.py:223
  16.8 0.9 %collective-permute-done.6.arrived = bf16[24,4096]{1,0:T(8,128)(2,1)S(1)} collective-permute-done((bf16[24,4096]{1,0:T(8,128)(2,1)S(1)}, bf16[24,4096]{1,0:T(8,128)(2,1)S(1)}, u32[]{:S(2)}, u32[]{:S(2)}) %collective-permute-start.6) | collective-permute-done | bytes 196640 | tf_op jit(solution)/shard_map/ppermute | solution.py:223
  17.8 1.7 %collective-permute-start.7 = (bf16[24,4096]{1,0:T(8,128)(2,1)S(1)}, bf16[24,4096]{1,0:T(8,128)(2,1)S(1)}, u32[]{:S(2)}, u32[]{:S(2)}) collective-permute-start(bf16[24,4096]{1,0:T(8,128)(2,1)S(1)} %join_cores.1), channel_id=1, source_target_pairs={{0,2},{1,3},{2,0},{3,1},{4,6},{5,7},{6,4},{7,5},{8,10},{9,11},{10,... | collective-permute-start | bytes 589832 | tf_op jit(solution)/shard_map/ppermute | solution.py:223
  19.5 0.0 collective-permute-done.5.arrived
  19.5 5.3 %collective-permute-done.7.joined = bf16[24,4096]{1,0:T(8,128)(2,1)S(1)} collective-permute-done((bf16[24,4096]{1,0:T(8,128)(2,1)S(1)}, bf16[24,4096]{1,0:T(8,128)(2,1)S(1)}, u32[]{:S(2)}, u32[]{:S(2)}) %collective-permute-start.7) | collective-permute-done | bytes 196640 | tf_op jit(solution)/shard_map/ppermute | solution.py:223
  24.8 0.7 %add_layers.1 = bf16[24,4096]{1,0:T(8,128)(2,1)} custom-call(f32[24,4096]{1,0:T(8,128)S(1)} %get-tuple-element.17.own, bf16[24,4096]{1,0:T(8,128)(2,1)S(1)} %collective-permute-done.5.arrived, bf16[24,4096]{1,0:T(8,128)(2,1)S(1)} %collective-permute-done.7.joined), custom_call_target="tpu_custom_call" | custom-call | flops 196608 | bytes 1048576 | tf_op jit(solution)/shard_map/add_layers/pallas_call | solution.py:296
  (7 shorter events, 0.1 us)
Async XLA Ops:
  0.0 8.7 %copy-start = (s32[1,1,1,768]{3,2,1,0:T(1,128)S(1)}, s32[1,1,1,768]{3,2,1,0:T(1,128)}, u32[]{:S(2)}) copy-start(s32[1,1,1,768]{3,2,1,0:T(1,128)} %param.6) | copy-start | bytes 9220
  0.0 8.7 %copy-start.1 = (s32[1,1,1,768]{3,2,1,0:T(1,128)S(1)}, s32[1,1,1,768]{3,2,1,0:T(1,128)}, u32[]{:S(2)}) copy-start(s32[1,1,1,768]{3,2,1,0:T(1,128)} %param.7) | copy-start | bytes 9220
  0.0 10.8 %collective-permute-start.2 = (bf16[16,4096]{1,0:T(8,128)(2,1)}, bf16[16,4096]{1,0:T(8,128)(2,1)S(1)}, u32[]{:S(2)}, u32[]{:S(2)}) collective-permute-start(bf16[16,4096]{1,0:T(8,128)(2,1)} %bitcast.7), channel_id=1, source_target_pairs={{0,16},{8,24},{16,0},{24,8},{1,17},{9,25},{17,1},{25,9},{2,18},{10... | collective-permute-start | bytes 393224 | tf_op jit(solution)/shard_map/ppermute | solution.py:223
  4.0 0.9 %copy-start.2 = (bf16[1,1,1,16,4096]{4,3,2,1,0:T(8,128)(2,1)S(1)}, bf16[1,1,1,16,4096]{4,3,2,1,0:T(8,128)(2,1)}, u32[]{:S(2)}) copy-start(bf16[1,1,1,16,4096]{4,3,2,1,0:T(8,128)(2,1)} %param.5) | copy-start | bytes 393220
  5.0 1.7 %copy-start.3 = (bf16[1,1,1,8,4096]{4,3,2,1,0:T(8,128)(2,1)S(1)}, bf16[1,1,1,8,4096]{4,3,2,1,0:T(8,128)(2,1)}, u32[]{:S(2)}) copy-start(bf16[1,1,1,8,4096]{4,3,2,1,0:T(8,128)(2,1)} %param.4) | copy-start | bytes 196612
  5.0 7.0 %collective-permute-start.1 = (bf16[16,4096]{1,0:T(8,128)(2,1)S(1)}, bf16[16,4096]{1,0:T(8,128)(2,1)S(1)}, u32[]{:S(2)}, u32[]{:S(2)}) collective-permute-start(bf16[16,4096]{1,0:T(8,128)(2,1)S(1)} %get-tuple-element.13.refs_2_), channel_id=1, source_target_pairs={{0,8},{8,0},{16,24},{24,16},{1,9},{9,1},{17,25},{25,17},{2,10},{10... | collective-permute-start | bytes 393224 | tf_op jit(solution)/shard_map/ppermute | solution.py:223
  6.6 5.4 %collective-permute-start = (bf16[8,4096]{1,0:T(8,128)(2,1)S(1)}, bf16[8,4096]{1,0:T(8,128)(2,1)S(1)}, u32[]{:S(2)}, u32[]{:S(2)}) collective-permute-start(bf16[8,4096]{1,0:T(8,128)(2,1)S(1)} %bitcast.9), channel_id=1, source_target_pairs={{0,4},{4,0},{1,5},{5,1},{2,6},{6,2},{3,7},{7,3},{8,12},{12,8},{9,1... | collective-permute-start | bytes 196616 | tf_op jit(solution)/shard_map/ppermute | solution.py:223
  8.1 6.8 %collective-permute-start.4 = (bf16[8,4096]{1,0:T(8,128)(2,1)S(1)}, bf16[8,4096]{1,0:T(8,128)(2,1)S(1)}, u32[]{:S(2)}, u32[]{:S(2)}) collective-permute-start(bf16[8,4096]{1,0:T(8,128)(2,1)S(1)} %get-tuple-element.16), channel_id=1, source_target_pairs={{0,24},{8,16},{16,8},{24,0},{1,25},{9,17},{17,9},{25,1},{2,26},{10... | collective-permute-start | bytes 196616 | tf_op jit(solution)/shard_map/ppermute | solution.py:223
  10.9 4.3 %collective-permute-start.3 = (bf16[8,4096]{1,0:T(8,128)(2,1)S(1)}, bf16[8,4096]{1,0:T(8,128)(2,1)S(1)}, u32[]{:S(2)}, u32[]{:S(2)}) collective-permute-start(bf16[8,4096]{1,0:T(8,128)(2,1)S(1)} %lower.1), channel_id=1, source_target_pairs={{0,8},{8,0},{16,24},{24,16},{1,9},{9,1},{17,25},{25,17},{2,10},{10... | collective-permute-start | bytes 196616 | tf_op jit(solution)/shard_map/ppermute | solution.py:223
  16.2 1.5 %collective-permute-start.6 = (bf16[24,4096]{1,0:T(8,128)(2,1)S(1)}, bf16[24,4096]{1,0:T(8,128)(2,1)S(1)}, u32[]{:S(2)}, u32[]{:S(2)}) collective-permute-start(bf16[24,4096]{1,0:T(8,128)(2,1)S(1)} %get-tuple-element.20), channel_id=1, source_target_pairs={{0,1},{1,0},{2,3},{3,2},{4,5},{5,4},{6,7},{7,6},{8,9},{9,8},{10,11... | collective-permute-start | bytes 589832 | tf_op jit(solution)/shard_map/ppermute | solution.py:223
  16.3 3.2 %collective-permute-start.5 = (bf16[24,4096]{1,0:T(8,128)(2,1)S(1)}, bf16[24,4096]{1,0:T(8,128)(2,1)S(1)}, u32[]{:S(2)}, u32[]{:S(2)}) collective-permute-start(bf16[24,4096]{1,0:T(8,128)(2,1)S(1)} %get-tuple-element.18), channel_id=1, source_target_pairs={{0,1},{1,0},{2,3},{3,2},{4,5},{5,4},{6,7},{7,6},{8,9},{9,8},{10,11... | collective-permute-start | bytes 589832 | tf_op jit(solution)/shard_map/ppermute | solution.py:223
  17.8 7.0 %collective-permute-start.7 = (bf16[24,4096]{1,0:T(8,128)(2,1)S(1)}, bf16[24,4096]{1,0:T(8,128)(2,1)S(1)}, u32[]{:S(2)}, u32[]{:S(2)}) collective-permute-start(bf16[24,4096]{1,0:T(8,128)(2,1)S(1)} %join_cores.1), channel_id=1, source_target_pairs={{0,2},{1,3},{2,0},{3,1},{4,6},{5,7},{6,4},{7,5},{8,10},{9,11},{10,... | collective-permute-start | bytes 589832 | tf_op jit(solution)/shard_map/ppermute | solution.py:223

commit v3 on v2

--- a/solution.py
+++ b/solution.py
@@ -53,13 +53,9 @@
         pl.loop(0, count)(body)
 
 
-def stage_kernel(b_ref, out, upper):
-    out[...] = b_ref[...]
-    upper[...] = b_ref[upper.shape[0]:, :]
-
-
-def lower_kernel(b_ref, out):
-    out[...] = b_ref[:out.shape[0], :]
+def stage_kernel(*refs):
+    for ref, out in zip(refs[:len(refs) // 2], refs[len(refs) // 2:]):
+        out[...] = ref[...]
 
 
 def counts_kernel(swap, left_tiles, left_each, right_each, a_slots, b_slots, sel):
@@ -153,40 +149,47 @@
         )
 
 
-def first_kernel(groups, n_left, sel, *refs):
+def own_kernel(groups, n_left, sel, *refs):
     shards = sum(groups)
     a_refs, b_refs = refs[:n_left], refs[n_left:n_left + shards]
     acc, a_lines, raw, prod = refs[n_left + shards:]
     left_lines(a_refs, a_lines)
-    pairs = b_refs[0].shape[0] * a_lines.shape[0] // LINES
-    shard = 0
+    add_shards(0, groups, sel, a_lines, b_refs, None, acc, raw, prod)
+
+
+def more_kernel(start, sel, a_lines, acc, b_ref, out, raw, prod):
+    add_shards(start, (1,), sel, a_lines, (b_ref,), acc, out, raw, prod)
+
+
+def add_shards(start, groups, sel, a_lines, b_refs, acc, out, raw, prod):
+    each = a_lines.shape[0] // LINES
+    taken = 0
     for count in groups:
-        start = shard
-        for i in range(count):
-            all_products(a_lines, b_refs[shard], raw, prod, i * pairs)
-            shard += 1
+        done = 0
+        before = out if taken else acc
+        for b_ref in b_refs[taken:taken + count]:
+            all_products(a_lines, b_ref, raw, prod, done)
+            done += b_ref.shape[0] * each
 
         def put(columns, value):
-            acc[:, columns] = value if start == 0 else acc[:, columns] + value
-
-        chosen_sums(sel, start * pairs, count * pairs, prod, put)
-
-
-def last_kernel(start, n_parts, sel, a_lines, acc, *refs):
-    b_refs, (own, far, cross, near, raw, prod) = refs[:n_parts], refs[n_parts:]
-    each = a_lines.shape[0] // LINES
+            out[:, columns] = value if before is None else value + before[:, columns]
+
+        chosen_sums(sel, start, done, prod, put)
+        taken += count
+        start += done
+
+
+def last_kernel(start, sel, a_lines, acc, b_ref, own, far, cross, near, raw, prod):
+    pairs = b_ref.shape[0] * a_lines.shape[0] // LINES
     owned = own.shape[0]
-    done = 0
-    for b_ref in b_refs:
-        all_products(a_lines, b_ref, raw, prod, done)
-        done += b_ref.shape[0] * each
+    all_products(a_lines, b_ref, raw, prod, 0)
 
     def put(columns, value):
         value = value + acc[:, columns]
         for i, out in enumerate((own, far, cross, near)):
             out[:, columns] = value[i * owned:(i + 1) * owned].astype(out.dtype)
 
-    chosen_sums(sel, start, done, prod, put)
+    chosen_sums(sel, start, pairs, prod, put)
 
 
 def join_kernel(far, arrived, out):
@@ -241,18 +244,9 @@
         a_parts = [a_local, exchange(a_local, "col", 1)]
     else:
         a_parts = [lax.all_gather(a_local, "col", axis=0, tiled=True)]
-    upper = right_each // 2
-    b_here, b_upper = call(
-        stage_kernel,
-        [shape(b_local.shape, BF16), shape((upper, FLAT), BF16)],
-        [],
-        1,
-        "stage",
-        STAGE_FLOPS,
-        MIB,
-    )(b_local)
-    b_near = exchange(b_here, "row", 1)
-    last_upper = exchange(b_upper, "row", 3)
+    (b_here,) = call(stage_kernel, [shape(b_local.shape, BF16)], [], 1, "stage", STAGE_FLOPS, MIB)(b_local)
+    b_near = exchange(b_local, "row", 1)
+    b_last = exchange(b_here, "row", 3)
     (sel,) = call(
         functools.partial(counts_kernel, cols == 2, left_tiles, left_each, right_each),
         [shape((tiles, rows * pairs), BF16)],
@@ -262,31 +256,38 @@
         2 * tiles * tiles * TASKS * TASKS,
         MIB,
     )(a_index, b_index)
-    (b_lower,) = call(lower_kernel, [shape((right_each - upper, FLAT), BF16)], [], 1, "lower", upper * FLAT, MIB)(b_far)
-    last_lower = exchange(b_lower, "row", 1)
-
-    groups = (3,) if pairs * FLAT * 2 < 4 * MIB else (1, 1, 1)
+
+    groups = (2,) if pairs * FLAT * 2 < 4 * MIB else (1, 1)
     raw = shape((right_each * LINES, LANES), F32)
-    half_raw = shape((upper * LINES, LANES), F32)
+    one = shape((LINES, pairs, LANES), BF16)
     shard_flops = 2 * pairs * LINES * LANES * LANES + 2 * pairs * tiles * FLAT
     acc, a_lines = call(
-        functools.partial(first_kernel, groups, len(a_parts)),
+        functools.partial(own_kernel, groups, len(a_parts)),
         [shape((tiles, FLAT), F32), shape((left_tiles * LINES, LANES), BF16)],
         [raw, shape((LINES, max(groups) * pairs, LANES), BF16)],
-        4 + len(a_parts),
+        3 + len(a_parts),
         "own_and_near",
-        3 * shard_flops,
-        12 * MIB,
-    )(sel, *a_parts, b_here, b_near, b_far)
+        2 * shard_flops,
+        8 * MIB,
+    )(sel, *a_parts, b_here, b_near)
+    (acc,) = call(
+        functools.partial(more_kernel, 2 * pairs),
+        [shape((tiles, FLAT), F32)],
+        [raw, one],
+        4,
+        "far_shard",
+        shard_flops,
+        4 * MIB,
+    )(sel, a_lines, acc, b_far)
     own, far, cross, near = call(
-        functools.partial(last_kernel, 3 * pairs, 2),
+        functools.partial(last_kernel, 3 * pairs),
         [shape((owned, FLAT), F32)] * 2 + [shape((owned, FLAT), BF16)] * 2,
-        [half_raw, shape((LINES, pairs, LANES), BF16)],
-        5,
+        [raw, one],
+        4,
         "last_shard",
         shard_flops,
         4 * MIB,
-    )(sel, a_lines, acc, last_lower, last_upper)
+    )(sel, a_lines, acc, b_last)
 
     arrived_cross = exchange(cross, "layer", 1)
     arrived_near = exchange(near, "layer", 1)

time: 25.7 us -> 25.5 us (level)
  starting transfers between devices: 11.1 us -> 9.55 us
  waiting for transfers between devices: 7.9 us -> 9.07 us
    ppermute x8 -> x7, starting transfers between devices: 11.1 us -> 9.55 us  [exchange(): return lax.ppermute(x, axis, [(i, i ^ q) for i in range(size)])]
    ppermute x8 -> x7, waiting for transfers between devices: 7.9 us -> 9.07 us  [exchange(): return lax.ppermute(x, axis, [(i, i ^ q) for i in range(size)])]
  transfers between devices with their start and end apart: 8 -> 7, of which waited for: 4 -> 5; matrix products, arithmetic and copies ran while one was open for 0% -> 0% of each run, Pallas kernels for 14% -> 15%
where the time goes in v3:
time: 25.5 us; the launch traced here: 25.3 us
  starting transfers between devices  9.55 us (37%)
  waiting for transfers between devices  9.07 us (36%)
  Pallas kernels  5.73 us (22%)
  local copies, waits for them, and re-layouts  0.91 us (4%)
    ppermute x7, starting transfers between devices, exchange(): return lax.ppermute(x, axis, [(i, i ^ q) for i in range(size)])  9.55 us
    ppermute x7, waiting for transfers between devices, exchange(): return lax.ppermute(x, axis, [(i, i ^ q) for i in range(size)])  9.07 us
    pallas_call x1, Pallas kernels, shards(): call(functools.partial(own_kernel, groups, len(a_parts)), [shape((tiles,...  2.01 us
    pallas_call x1, Pallas kernels, shards(): call(functools.partial(more_kernel, 2 * pairs), [shape((tiles, FLAT), F32...  1.1 us
    pallas_call x1, Pallas kernels, shards(): call(functools.partial(last_kernel, 3 * pairs), [shape((owned, FLAT), F32...  1.1 us
    unnamed x8, local copies, waits for them, and re-layouts  0.91 us
    pallas_call x1, Pallas kernels, shards(): call(add_kernel, [shape((owned, FLAT), BF16)], [], 3, 'add_layers', 2 * o...  0.74 us
    pallas_call x1, Pallas kernels, shards(): call(functools.partial(counts_kernel, cols == 2, left_tiles, left_each, r...  0.73 us
  transfers between devices with their start and end apart: 7, of which 5 were waited for; matrix products, arithmetic and copies ran while one was open for 0% of the time, Pallas kernels for 15%

profile of v3, /device:TPU:0, one launch (start us, length us, event | category | flops | bytes accessed | tf_op | source)
XLA Modules:
  0.0 25.3 jit_solution(14794509049959896637)
XLA Ops:
  0.0 4.0 %collective-permute-start.2 = (bf16[16,4096]{1,0:T(8,128)(2,1)}, bf16[16,4096]{1,0:T(8,128)(2,1)S(1)}, u32[]{:S(2)}, u32[]{:S(2)}) collective-permute-start(bf16[16,4096]{1,0:T(8,128)(2,1)} %bitcast.7), channel_id=1, source_target_pairs={{0,16},{8,24},{16,0},{24,8},{1,17},{9,25},{17,1},{25,9},{2,18},{10... | collective-permute-start | bytes 393224 | tf_op jit(solution)/shard_map/ppermute | solution.py:226
  4.0 1.6 %collective-permute-start.1 = (bf16[16,4096]{1,0:T(8,128)(2,1)}, bf16[16,4096]{1,0:T(8,128)(2,1)S(1)}, u32[]{:S(2)}, u32[]{:S(2)}) collective-permute-start(bf16[16,4096]{1,0:T(8,128)(2,1)} %bitcast.8), channel_id=1, source_target_pairs={{0,8},{8,0},{16,24},{24,16},{1,9},{9,1},{17,25},{25,17},{2,10},{10... | collective-permute-start | bytes 393224 | tf_op jit(solution)/shard_map/ppermute | solution.py:226
  5.6 0.0 copy-start
  5.6 1.5 %collective-permute-start = (bf16[8,4096]{1,0:T(8,128)(2,1)}, bf16[8,4096]{1,0:T(8,128)(2,1)S(1)}, u32[]{:S(2)}, u32[]{:S(2)}) collective-permute-start(bf16[8,4096]{1,0:T(8,128)(2,1)} %bitcast.10), channel_id=1, source_target_pairs={{0,4},{4,0},{1,5},{5,1},{2,6},{6,2},{3,7},{7,3},{8,12},{12,8},{9,1... | collective-permute-start | bytes 196616 | tf_op jit(solution)/shard_map/ppermute | solution.py:226
  7.1 0.9 %copy-done.2 = bf16[1,1,1,16,4096]{4,3,2,1,0:T(8,128)(2,1)S(1)} copy-done((bf16[1,1,1,16,4096]{4,3,2,1,0:T(8,128)(2,1)S(1)}, bf16[1,1,1,16,4096]{4,3,2,1,0:T(8,128)(2,1)}, u32[]{:S(2)}) %copy-start.2) | copy-done | bytes 131096
  8.0 0.3 %collective-permute-start.3 = (bf16[16,4096]{1,0:T(8,128)(2,1)S(1)}, bf16[16,4096]{1,0:T(8,128)(2,1)S(1)}, u32[]{:S(2)}, u32[]{:S(2)}) collective-permute-start(bf16[16,4096]{1,0:T(8,128)(2,1)S(1)} %stage.1.refs_2_), channel_id=1, source_target_pairs={{0,24},{8,16},{16,8},{24,0},{1,25},{9,17},{17,9},{25,1},{2,26},{10... | collective-permute-start | bytes 393224 | tf_op jit(solution)/shard_map/ppermute | solution.py:226
  8.3 0.0 copy-done
  8.3 0.0 copy-done.1
  8.3 0.7 %counts.1.sel = bf16[96,1024]{1,0:T(8,128)(2,1)S(1)} custom-call(s32[1,768]{1,0:T(1,128)S(1)} %bitcast.5, s32[1,768]{1,0:T(1,128)S(1)} %bitcast.6), custom_call_target="tpu_custom_call" | custom-call | flops 1179648 | bytes 1048576 | tf_op jit(solution)/shard_map/counts/pallas_call | solution.py:250
  9.1 1.0 %collective-permute-done.refs_1_ = bf16[8,4096]{1,0:T(8,128)(2,1)S(1)} collective-permute-done((bf16[8,4096]{1,0:T(8,128)(2,1)}, bf16[8,4096]{1,0:T(8,128)(2,1)S(1)}, u32[]{:S(2)}, u32[]{:S(2)}) %collective-permute-start) | collective-permute-done | bytes 65568 | tf_op jit(solution)/shard_map/ppermute | solution.py:226
  10.1 1.0 %collective-permute-done.1.refs_3_ = bf16[16,4096]{1,0:T(8,128)(2,1)S(1)} collective-permute-done((bf16[16,4096]{1,0:T(8,128)(2,1)}, bf16[16,4096]{1,0:T(8,128)(2,1)S(1)}, u32[]{:S(2)}, u32[]{:S(2)}) %collective-permute-start.1) | collective-permute-done | bytes 131104 | tf_op jit(solution)/shard_map/ppermute | solution.py:226
  11.1 0.0 copy-done.3
  11.1 2.0 %own_and_near.1 = (f32[96,4096]{1,0:T(8,128)S(1)}, bf16[512,128]{1,0:T(8,128)(2,1)S(1)}) custom-call(bf16[96,1024]{1,0:T(8,128)(2,1)S(1)} %counts.1.sel, bf16[8,4096]{1,0:T(8,128)(2,1)S(1)} %bitcast.11, bf16[8,4096]{1,0:T(8,128)(2,1)S(1)} %collective-permute-done.refs_1_, bf16[16,4096]{1,0:T(8,128)(2,1)S(1)} %stage.1.refs_2_, ...), custom_call_target="tpu_custom_call" | custom-call | flops 939524096 | bytes 8388608 | tf_op jit(solution)/shard_map/own_and_near/pallas_call | solution.py:264
  13.1 0.0 collective-permute-done.2.b_ref
  13.1 1.1 %far_shard.1.acc = f32[96,4096]{1,0:T(8,128)S(1)} custom-call(bf16[96,1024]{1,0:T(8,128)(2,1)S(1)} %counts.1.sel, bf16[512,128]{1,0:T(8,128)(2,1)S(1)} %get-tuple-element.11.a_lines, f32[96,4096]{1,0:T(8,128)S(1)} %get-tuple-element.12.acc, bf16[16,4096]{1,0:T(8,128)(2,1)S(1)} %collective-permute-done.2.b_ref), custom_call_target="tpu_custom_call" | custom-call | flops 469762048 | bytes 4194304 | tf_op jit(solution)/shard_map/far_shard/pallas_call | solution.py:273
  14.2 0.7 %collective-permute-done.3.b_ref = bf16[16,4096]{1,0:T(8,128)(2,1)S(1)} collective-permute-done((bf16[16,4096]{1,0:T(8,128)(2,1)S(1)}, bf16[16,4096]{1,0:T(8,128)(2,1)S(1)}, u32[]{:S(2)}, u32[]{:S(2)}) %collective-permute-start.3) | collective-permute-done | bytes 131104 | tf_op jit(solution)/shard_map/ppermute | solution.py:226
  14.9 1.1 %last_shard.1 = (f32[24,4096]{1,0:T(8,128)S(1)}, f32[24,4096]{1,0:T(8,128)S(1)}, bf16[24,4096]{1,0:T(8,128)(2,1)S(1)}, bf16[24,4096]{1,0:T(8,128)(2,1)S(1)}) custom-call(bf16[96,1024]{1,0:T(8,128)(2,1)S(1)} %counts.1.sel, bf16[512,128]{1,0:T(8,128)(2,1)S(1)} %get-tuple-element.11.a_lines, f32[96,4096]{1,0:T(8,128)S(1)} %far_shard.1.acc, ...), custom_call_target="tpu_custom_call" | custom-call | flops 469762048 | bytes 4194304 | tf_op jit(solution)/shard_map/last_shard/pallas_call | solution.py:282
  16.0 0.1 collective-permute-start.5
  16.1 0.5 %collective-permute-start.4 = (bf16[24,4096]{1,0:T(8,128)(2,1)S(1)}, bf16[24,4096]{1,0:T(8,128)(2,1)S(1)}, u32[]{:S(2)}, u32[]{:S(2)}) collective-permute-start(bf16[24,4096]{1,0:T(8,128)(2,1)S(1)} %get-tuple-element.14), channel_id=1, source_target_pairs={{0,1},{1,0},{2,3},{3,2},{4,5},{5,4},{6,7},{7,6},{8,9},{9,8},{10,11... | collective-permute-start | bytes 589832 | tf_op jit(solution)/shard_map/ppermute | solution.py:226
  16.6 0.9 %collective-permute-done.5.arrived = bf16[24,4096]{1,0:T(8,128)(2,1)S(1)} collective-permute-done((bf16[24,4096]{1,0:T(8,128)(2,1)S(1)}, bf16[24,4096]{1,0:T(8,128)(2,1)S(1)}, u32[]{:S(2)}, u32[]{:S(2)}) %collective-permute-start.5) | collective-permute-done | bytes 196640 | tf_op jit(solution)/shard_map/ppermute | solution.py:226
  17.6 1.6 %collective-permute-start.6 = (bf16[24,4096]{1,0:T(8,128)(2,1)S(1)}, bf16[24,4096]{1,0:T(8,128)(2,1)S(1)}, u32[]{:S(2)}, u32[]{:S(2)}) collective-permute-start(bf16[24,4096]{1,0:T(8,128)(2,1)S(1)} %join_cores.1), channel_id=1, source_target_pairs={{0,2},{1,3},{2,0},{3,1},{4,6},{5,7},{6,4},{7,5},{8,10},{9,11},{10,... | collective-permute-start | bytes 589832 | tf_op jit(solution)/shard_map/ppermute | solution.py:226
  19.2 0.0 collective-permute-done.4.arrived
  19.2 5.4 %collective-permute-done.6.joined = bf16[24,4096]{1,0:T(8,128)(2,1)S(1)} collective-permute-done((bf16[24,4096]{1,0:T(8,128)(2,1)S(1)}, bf16[24,4096]{1,0:T(8,128)(2,1)S(1)}, u32[]{:S(2)}, u32[]{:S(2)}) %collective-permute-start.6) | collective-permute-done | bytes 196640 | tf_op jit(solution)/shard_map/ppermute | solution.py:226
  24.6 0.7 %add_layers.1 = bf16[24,4096]{1,0:T(8,128)(2,1)} custom-call(f32[24,4096]{1,0:T(8,128)S(1)} %get-tuple-element.13.own, bf16[24,4096]{1,0:T(8,128)(2,1)S(1)} %collective-permute-done.4.arrived, bf16[24,4096]{1,0:T(8,128)(2,1)S(1)} %collective-permute-done.6.joined), custom_call_target="tpu_custom_call" | custom-call | flops 196608 | bytes 1048576 | tf_op jit(solution)/shard_map/add_layers/pallas_call | solution.py:297
  (5 shorter events, 0.1 us)
Async XLA Ops:
  0.0 13.1 %collective-permute-start.2 = (bf16[16,4096]{1,0:T(8,128)(2,1)}, bf16[16,4096]{1,0:T(8,128)(2,1)S(1)}, u32[]{:S(2)}, u32[]{:S(2)}) collective-permute-start(bf16[16,4096]{1,0:T(8,128)(2,1)} %bitcast.7), channel_id=1, source_target_pairs={{0,16},{8,24},{16,0},{24,8},{1,17},{9,25},{17,1},{25,9},{2,18},{10... | collective-permute-start | bytes 393224 | tf_op jit(solution)/shard_map/ppermute | solution.py:226
  4.0 7.0 %collective-permute-start.1 = (bf16[16,4096]{1,0:T(8,128)(2,1)}, bf16[16,4096]{1,0:T(8,128)(2,1)S(1)}, u32[]{:S(2)}, u32[]{:S(2)}) collective-permute-start(bf16[16,4096]{1,0:T(8,128)(2,1)} %bitcast.8), channel_id=1, source_target_pairs={{0,8},{8,0},{16,24},{24,16},{1,9},{9,1},{17,25},{25,17},{2,10},{10... | collective-permute-start | bytes 393224 | tf_op jit(solution)/shard_map/ppermute | solution.py:226
  5.6 2.7 %copy-start = (s32[1,1,1,768]{3,2,1,0:T(1,128)S(1)}, s32[1,1,1,768]{3,2,1,0:T(1,128)}, u32[]{:S(2)}) copy-start(s32[1,1,1,768]{3,2,1,0:T(1,128)} %param.6) | copy-start | bytes 9220
  5.6 2.7 %copy-start.1 = (s32[1,1,1,768]{3,2,1,0:T(1,128)S(1)}, s32[1,1,1,768]{3,2,1,0:T(1,128)}, u32[]{:S(2)}) copy-start(s32[1,1,1,768]{3,2,1,0:T(1,128)} %param.7) | copy-start | bytes 9220
  5.6 4.5 %collective-permute-start = (bf16[8,4096]{1,0:T(8,128)(2,1)}, bf16[8,4096]{1,0:T(8,128)(2,1)S(1)}, u32[]{:S(2)}, u32[]{:S(2)}) collective-permute-start(bf16[8,4096]{1,0:T(8,128)(2,1)} %bitcast.10), channel_id=1, source_target_pairs={{0,4},{4,0},{1,5},{5,1},{2,6},{6,2},{3,7},{7,3},{8,12},{12,8},{9,1... | collective-permute-start | bytes 196616 | tf_op jit(solution)/shard_map/ppermute | solution.py:226
  7.1 0.9 %copy-start.2 = (bf16[1,1,1,16,4096]{4,3,2,1,0:T(8,128)(2,1)S(1)}, bf16[1,1,1,16,4096]{4,3,2,1,0:T(8,128)(2,1)}, u32[]{:S(2)}) copy-start(bf16[1,1,1,16,4096]{4,3,2,1,0:T(8,128)(2,1)} %param.5) | copy-start | bytes 393220
  8.0 3.1 %copy-start.3 = (bf16[1,1,1,8,4096]{4,3,2,1,0:T(8,128)(2,1)S(1)}, bf16[1,1,1,8,4096]{4,3,2,1,0:T(8,128)(2,1)}, u32[]{:S(2)}) copy-start(bf16[1,1,1,8,4096]{4,3,2,1,0:T(8,128)(2,1)} %param.4) | copy-start | bytes 196612
  8.0 6.9 %collective-permute-start.3 = (bf16[16,4096]{1,0:T(8,128)(2,1)S(1)}, bf16[16,4096]{1,0:T(8,128)(2,1)S(1)}, u32[]{:S(2)}, u32[]{:S(2)}) collective-permute-start(bf16[16,4096]{1,0:T(8,128)(2,1)S(1)} %stage.1.refs_2_), channel_id=1, source_target_pairs={{0,24},{8,16},{16,8},{24,0},{1,25},{9,17},{17,9},{25,1},{2,26},{10... | collective-permute-start | bytes 393224 | tf_op jit(solution)/shard_map/ppermute | solution.py:226
  16.0 1.5 %collective-permute-start.5 = (bf16[24,4096]{1,0:T(8,128)(2,1)S(1)}, bf16[24,4096]{1,0:T(8,128)(2,1)S(1)}, u32[]{:S(2)}, u32[]{:S(2)}) collective-permute-start(bf16[24,4096]{1,0:T(8,128)(2,1)S(1)} %get-tuple-element.16), channel_id=1, source_target_pairs={{0,1},{1,0},{2,3},{3,2},{4,5},{5,4},{6,7},{7,6},{8,9},{9,8},{10,11... | collective-permute-start | bytes 589832 | tf_op jit(solution)/shard_map/ppermute | solution.py:226
  16.1 3.1 %collective-permute-start.4 = (bf16[24,4096]{1,0:T(8,128)(2,1)S(1)}, bf16[24,4096]{1,0:T(8,128)(2,1)S(1)}, u32[]{:S(2)}, u32[]{:S(2)}) collective-permute-start(bf16[24,4096]{1,0:T(8,128)(2,1)S(1)} %get-tuple-element.14), channel_id=1, source_target_pairs={{0,1},{1,0},{2,3},{3,2},{4,5},{5,4},{6,7},{7,6},{8,9},{9,8},{10,11... | collective-permute-start | bytes 589832 | tf_op jit(solution)/shard_map/ppermute | solution.py:226
  17.6 7.0 %collective-permute-start.6 = (bf16[24,4096]{1,0:T(8,128)(2,1)S(1)}, bf16[24,4096]{1,0:T(8,128)(2,1)S(1)}, u32[]{:S(2)}, u32[]{:S(2)}) collective-permute-start(bf16[24,4096]{1,0:T(8,128)(2,1)S(1)} %join_cores.1), channel_id=1, source_target_pairs={{0,2},{1,3},{2,0},{3,1},{4,6},{5,7},{6,4},{7,5},{8,10},{9,11},{10,... | collective-permute-start | bytes 589832 | tf_op jit(solution)/shard_map/ppermute | solution.py:226

commit v4 on v2

--- a/solution.py
+++ b/solution.py
@@ -53,16 +53,17 @@
         pl.loop(0, count)(body)
 
 
-def stage_kernel(b_ref, out, upper):
+def stage_kernel(b_ref, out):
     out[...] = b_ref[...]
-    upper[...] = b_ref[upper.shape[0]:, :]
 
 
 def lower_kernel(b_ref, out):
     out[...] = b_ref[:out.shape[0], :]
 
 
-def counts_kernel(swap, left_tiles, left_each, right_each, a_slots, b_slots, sel):
+def counts_kernel(swap, left_tiles, left_each, right_each, a_slots, b_slots, b_ref, sel, b_out, upper):
+    b_out[...] = b_ref[...]
+    upper[...] = b_ref[upper.shape[0]:, :]
     row, col, layer = lax.axis_index("row"), lax.axis_index("col"), lax.axis_index("layer")
     tiles, pairs = sel.shape
     tasks = tiles * TASKS
@@ -242,26 +243,18 @@
     else:
         a_parts = [lax.all_gather(a_local, "col", axis=0, tiled=True)]
     upper = right_each // 2
-    b_here, b_upper = call(
-        stage_kernel,
-        [shape(b_local.shape, BF16), shape((upper, FLAT), BF16)],
+    (b_staged,) = call(stage_kernel, [shape(b_local.shape, BF16)], [], 1, "stage", STAGE_FLOPS, MIB)(b_local)
+    sel, b_here, b_upper = call(
+        functools.partial(counts_kernel, cols == 2, left_tiles, left_each, right_each),
+        [shape((tiles, rows * pairs), BF16), shape(b_local.shape, BF16), shape((upper, FLAT), BF16)],
         [],
-        1,
-        "stage",
-        STAGE_FLOPS,
-        MIB,
-    )(b_local)
-    b_near = exchange(b_here, "row", 1)
-    last_upper = exchange(b_upper, "row", 3)
-    (sel,) = call(
-        functools.partial(counts_kernel, cols == 2, left_tiles, left_each, right_each),
-        [shape((tiles, rows * pairs), BF16)],
-        [],
-        2,
+        3,
         "counts",
         2 * tiles * tiles * TASKS * TASKS,
         MIB,
-    )(a_index, b_index)
+    )(a_index, b_index, b_staged)
+    b_near = exchange(b_here, "row", 1)
+    last_upper = exchange(b_upper, "row", 3)
     (b_lower,) = call(lower_kernel, [shape((right_each - upper, FLAT), BF16)], [], 1, "lower", upper * FLAT, MIB)(b_far)
     last_lower = exchange(b_lower, "row", 1)
 

time: 25.7 us -> 26.4 us (1.027)
  starting transfers between devices: 11.1 us -> 11.6 us
    ppermute x8, starting transfers between devices: 11.1 us -> 11.6 us  [exchange(): return lax.ppermute(x, axis, [(i, i ^ q) for i in range(size)])]
where the time goes in v4:
time: 26.4 us; the launch traced here: 26.2 us
  starting transfers between devices  11.6 us (44%)
  waiting for transfers between devices  8.06 us (31%)
  Pallas kernels  5.53 us (21%)
  local copies, waits for them, and re-layouts  0.95 us (4%)
    ppermute x8, starting transfers between devices, exchange(): return lax.ppermute(x, axis, [(i, i ^ q) for i in range(size)])  11.6 us
    ppermute x8, waiting for transfers between devices, exchange(): return lax.ppermute(x, axis, [(i, i ^ q) for i in range(size)])  8.06 us
    pallas_call x1, Pallas kernels, shards(): call(functools.partial(first_kernel, groups, len(a_parts)), [shape((tiles...  2.91 us
    pallas_call x1, Pallas kernels, shards(): call(functools.partial(last_kernel, 3 * pairs, 2), [shape((owned, FLAT),...  1.1 us
    unnamed x8, local copies, waits for them, and re-layouts  0.95 us
    pallas_call x1, Pallas kernels, shards(): call(add_kernel, [shape((owned, FLAT), BF16)], [], 3, 'add_layers', 2 * o...  0.74 us
    pallas_call x1, Pallas kernels, shards(): call(functools.partial(counts_kernel, cols == 2, left_tiles, left_each, r...  0.74 us
  transfers between devices with their start and end apart: 8, of which 4 were waited for; matrix products, arithmetic and copies ran while one was open for 0% of the time, Pallas kernels for 14%

profile of v4, /device:TPU:0, one launch (start us, length us, event | category | flops | bytes accessed | tf_op | source)
XLA Modules:
  0.0 26.2 jit_solution(9553084986438642247)
XLA Ops:
  0.0 4.0 %collective-permute-start.2 = (bf16[16,4096]{1,0:T(8,128)(2,1)}, bf16[16,4096]{1,0:T(8,128)(2,1)S(1)}, u32[]{:S(2)}, u32[]{:S(2)}) collective-permute-start(bf16[16,4096]{1,0:T(8,128)(2,1)} %bitcast.7), channel_id=1, source_target_pairs={{0,16},{8,24},{16,0},{24,8},{1,17},{9,25},{17,1},{25,9},{2,18},{10... | collective-permute-start | bytes 393224 | tf_op jit(solution)/shard_map/ppermute | solution.py:224
  4.0 0.9 %copy-done.2 = bf16[1,1,1,16,4096]{4,3,2,1,0:T(8,128)(2,1)S(1)} copy-done((bf16[1,1,1,16,4096]{4,3,2,1,0:T(8,128)(2,1)S(1)}, bf16[1,1,1,16,4096]{4,3,2,1,0:T(8,128)(2,1)}, u32[]{:S(2)}) %copy-start.2) | copy-done | bytes 131096
  5.0 0.0 copy-done
  5.0 0.0 copy-done.1
  5.0 0.7 %counts.1 = (bf16[96,1024]{1,0:T(8,128)(2,1)S(1)}, bf16[16,4096]{1,0:T(8,128)(2,1)S(1)}, bf16[8,4096]{1,0:T(8,128)(2,1)S(1)}) custom-call(s32[1,768]{1,0:T(1,128)S(1)} %bitcast.5, s32[1,768]{1,0:T(1,128)S(1)} %bitcast.6, bf16[16,4096]{1,0:T(8,128)(2,1)S(1)} %stage.1.b_ref), custom_call_target="tpu_custom_call" | custom-call | flops 1179648 | bytes 1048576 | tf_op jit(solution)/shard_map/counts/pallas_call | solution.py:247
  5.8 1.6 %collective-permute-start.1 = (bf16[16,4096]{1,0:T(8,128)(2,1)S(1)}, bf16[16,4096]{1,0:T(8,128)(2,1)S(1)}, u32[]{:S(2)}, u32[]{:S(2)}) collective-permute-start(bf16[16,4096]{1,0:T(8,128)(2,1)S(1)} %get-tuple-element.15.refs_2_), channel_id=1, source_target_pairs={{0,8},{8,0},{16,24},{24,16},{1,9},{9,1},{17,25},{25,17},{2,10},{10... | collective-permute-start | bytes 393224 | tf_op jit(solution)/shard_map/ppermute | solution.py:224
  7.4 0.0 copy-done.3
  7.4 1.5 %collective-permute-start = (bf16[8,4096]{1,0:T(8,128)(2,1)S(1)}, bf16[8,4096]{1,0:T(8,128)(2,1)S(1)}, u32[]{:S(2)}, u32[]{:S(2)}) collective-permute-start(bf16[8,4096]{1,0:T(8,128)(2,1)S(1)} %bitcast.9), channel_id=1, source_target_pairs={{0,4},{4,0},{1,5},{5,1},{2,6},{6,2},{3,7},{7,3},{8,12},{12,8},{9,1... | collective-permute-start | bytes 196616 | tf_op jit(solution)/shard_map/ppermute | solution.py:224
  8.9 0.2 collective-permute-start.4
  9.1 1.6 %collective-permute-done.2.refs_4_.b_ref = bf16[16,4096]{1,0:T(8,128)(2,1)S(1)} collective-permute-done((bf16[16,4096]{1,0:T(8,128)(2,1)}, bf16[16,4096]{1,0:T(8,128)(2,1)S(1)}, u32[]{:S(2)}, u32[]{:S(2)}) %collective-permute-start.2) | collective-permute-done | bytes 131104 | tf_op jit(solution)/shard_map/ppermute | solution.py:224
  10.7 1.7 %collective-permute-start.3 = (bf16[8,4096]{1,0:T(8,128)(2,1)S(1)}, bf16[8,4096]{1,0:T(8,128)(2,1)S(1)}, u32[]{:S(2)}, u32[]{:S(2)}) collective-permute-start(bf16[8,4096]{1,0:T(8,128)(2,1)S(1)} %lower.1), channel_id=1, source_target_pairs={{0,8},{8,0},{16,24},{24,16},{1,9},{9,1},{17,25},{25,17},{2,10},{10... | collective-permute-start | bytes 196616 | tf_op jit(solution)/shard_map/ppermute | solution.py:224
  12.4 0.0 collective-permute-done.refs_1_
  12.4 0.0 collective-permute-done.1.refs_3_
  12.4 2.9 %own_and_near.1 = (f32[96,4096]{1,0:T(8,128)S(1)}, bf16[512,128]{1,0:T(8,128)(2,1)S(1)}) custom-call(bf16[96,1024]{1,0:T(8,128)(2,1)S(1)} %get-tuple-element.14.sel, bf16[8,4096]{1,0:T(8,128)(2,1)S(1)} %bitcast.10, bf16[8,4096]{1,0:T(8,128)(2,1)S(1)} %collective-permute-done.refs_1_, bf16[16,4096]{1,0:T(8,128)(2,1)S(1)} %get-tuple-element.15.refs_2_, ...), custom_call_target="tpu_custom_call" | custom-call | flops 1409286144 | bytes 12582912 | tf_op jit(solution)/shard_map/own_and_near/pallas_call | solution.py:265
  15.3 0.0 collective-permute-done.4.refs_1_
  15.3 0.4 %collective-permute-done.3.refs_0_ = bf16[8,4096]{1,0:T(8,128)(2,1)S(1)} collective-permute-done((bf16[8,4096]{1,0:T(8,128)(2,1)S(1)}, bf16[8,4096]{1,0:T(8,128)(2,1)S(1)}, u32[]{:S(2)}, u32[]{:S(2)}) %collective-permute-start.3) | collective-permute-done | bytes 65568 | tf_op jit(solution)/shard_map/ppermute | solution.py:224
  15.6 1.1 %last_shard.1 = (f32[24,4096]{1,0:T(8,128)S(1)}, f32[24,4096]{1,0:T(8,128)S(1)}, bf16[24,4096]{1,0:T(8,128)(2,1)S(1)}, bf16[24,4096]{1,0:T(8,128)(2,1)S(1)}) custom-call(bf16[96,1024]{1,0:T(8,128)(2,1)S(1)} %get-tuple-element.14.sel, bf16[512,128]{1,0:T(8,128)(2,1)S(1)} %get-tuple-element.16.a_lines, f32[96,4096]{1,0:T(8,128)S(1)} %get-tuple-element.17.acc, ...), custom_call_target="tpu_custom_call" | custom-call | flops 469762048 | bytes 4194304 | tf_op jit(solution)/shard_map/last_shard/pallas_call | solution.py:274
  16.7 0.1 collective-permute-start.6
  16.8 0.5 %collective-permute-start.5 = (bf16[24,4096]{1,0:T(8,128)(2,1)S(1)}, bf16[24,4096]{1,0:T(8,128)(2,1)S(1)}, u32[]{:S(2)}, u32[]{:S(2)}) collective-permute-start(bf16[24,4096]{1,0:T(8,128)(2,1)S(1)} %get-tuple-element.20), channel_id=1, source_target_pairs={{0,1},{1,0},{2,3},{3,2},{4,5},{5,4},{6,7},{7,6},{8,9},{9,8},{10,11... | collective-permute-start | bytes 589832 | tf_op jit(solution)/shard_map/ppermute | solution.py:224
  17.3 0.9 %collective-permute-done.6.arrived = bf16[24,4096]{1,0:T(8,128)(2,1)S(1)} collective-permute-done((bf16[24,4096]{1,0:T(8,128)(2,1)S(1)}, bf16[24,4096]{1,0:T(8,128)(2,1)S(1)}, u32[]{:S(2)}, u32[]{:S(2)}) %collective-permute-start.6) | collective-permute-done | bytes 196640 | tf_op jit(solution)/shard_map/ppermute | solution.py:224
  18.3 2.0 %collective-permute-start.7 = (bf16[24,4096]{1,0:T(8,128)(2,1)S(1)}, bf16[24,4096]{1,0:T(8,128)(2,1)S(1)}, u32[]{:S(2)}, u32[]{:S(2)}) collective-permute-start(bf16[24,4096]{1,0:T(8,128)(2,1)S(1)} %join_cores.1), channel_id=1, source_target_pairs={{0,2},{1,3},{2,0},{3,1},{4,6},{5,7},{6,4},{7,5},{8,10},{9,11},{10,... | collective-permute-start | bytes 589832 | tf_op jit(solution)/shard_map/ppermute | solution.py:224
  20.3 0.0 collective-permute-done.5.arrived
  20.3 5.2 %collective-permute-done.7.joined = bf16[24,4096]{1,0:T(8,128)(2,1)S(1)} collective-permute-done((bf16[24,4096]{1,0:T(8,128)(2,1)S(1)}, bf16[24,4096]{1,0:T(8,128)(2,1)S(1)}, u32[]{:S(2)}, u32[]{:S(2)}) %collective-permute-start.7) | collective-permute-done | bytes 196640 | tf_op jit(solution)/shard_map/ppermute | solution.py:224
  25.5 0.7 %add_layers.1 = bf16[24,4096]{1,0:T(8,128)(2,1)} custom-call(f32[24,4096]{1,0:T(8,128)S(1)} %get-tuple-element.19.own, bf16[24,4096]{1,0:T(8,128)(2,1)S(1)} %collective-permute-done.5.arrived, bf16[24,4096]{1,0:T(8,128)(2,1)S(1)} %collective-permute-done.7.joined), custom_call_target="tpu_custom_call" | custom-call | flops 196608 | bytes 1048576 | tf_op jit(solution)/shard_map/add_layers/pallas_call | solution.py:289
  (7 shorter events, 0.1 us)
Async XLA Ops:
  0.0 5.0 %copy-start = (s32[1,1,1,768]{3,2,1,0:T(1,128)S(1)}, s32[1,1,1,768]{3,2,1,0:T(1,128)}, u32[]{:S(2)}) copy-start(s32[1,1,1,768]{3,2,1,0:T(1,128)} %param.6) | copy-start | bytes 9220
  0.0 5.0 %copy-start.1 = (s32[1,1,1,768]{3,2,1,0:T(1,128)S(1)}, s32[1,1,1,768]{3,2,1,0:T(1,128)}, u32[]{:S(2)}) copy-start(s32[1,1,1,768]{3,2,1,0:T(1,128)} %param.7) | copy-start | bytes 9220
  0.0 10.7 %collective-permute-start.2 = (bf16[16,4096]{1,0:T(8,128)(2,1)}, bf16[16,4096]{1,0:T(8,128)(2,1)S(1)}, u32[]{:S(2)}, u32[]{:S(2)}) collective-permute-start(bf16[16,4096]{1,0:T(8,128)(2,1)} %bitcast.7), channel_id=1, source_target_pairs={{0,16},{8,24},{16,0},{24,8},{1,17},{9,25},{17,1},{25,9},{2,18},{10... | collective-permute-start | bytes 393224 | tf_op jit(solution)/shard_map/ppermute | solution.py:224
  4.0 0.9 %copy-start.2 = (bf16[1,1,1,16,4096]{4,3,2,1,0:T(8,128)(2,1)S(1)}, bf16[1,1,1,16,4096]{4,3,2,1,0:T(8,128)(2,1)}, u32[]{:S(2)}) copy-start(bf16[1,1,1,16,4096]{4,3,2,1,0:T(8,128)(2,1)} %param.5) | copy-start | bytes 393220
  5.0 2.4 %copy-start.3 = (bf16[1,1,1,8,4096]{4,3,2,1,0:T(8,128)(2,1)S(1)}, bf16[1,1,1,8,4096]{4,3,2,1,0:T(8,128)(2,1)}, u32[]{:S(2)}) copy-start(bf16[1,1,1,8,4096]{4,3,2,1,0:T(8,128)(2,1)} %param.4) | copy-start | bytes 196612
  5.8 6.6 %collective-permute-start.1 = (bf16[16,4096]{1,0:T(8,128)(2,1)S(1)}, bf16[16,4096]{1,0:T(8,128)(2,1)S(1)}, u32[]{:S(2)}, u32[]{:S(2)}) collective-permute-start(bf16[16,4096]{1,0:T(8,128)(2,1)S(1)} %get-tuple-element.15.refs_2_), channel_id=1, source_target_pairs={{0,8},{8,0},{16,24},{24,16},{1,9},{9,1},{17,25},{25,17},{2,10},{10... | collective-permute-start | bytes 393224 | tf_op jit(solution)/shard_map/ppermute | solution.py:224
  7.4 5.0 %collective-permute-start = (bf16[8,4096]{1,0:T(8,128)(2,1)S(1)}, bf16[8,4096]{1,0:T(8,128)(2,1)S(1)}, u32[]{:S(2)}, u32[]{:S(2)}) collective-permute-start(bf16[8,4096]{1,0:T(8,128)(2,1)S(1)} %bitcast.9), channel_id=1, source_target_pairs={{0,4},{4,0},{1,5},{5,1},{2,6},{6,2},{3,7},{7,3},{8,12},{12,8},{9,1... | collective-permute-start | bytes 196616 | tf_op jit(solution)/shard_map/ppermute | solution.py:224
  8.9 6.4 %collective-permute-start.4 = (bf16[8,4096]{1,0:T(8,128)(2,1)S(1)}, bf16[8,4096]{1,0:T(8,128)(2,1)S(1)}, u32[]{:S(2)}, u32[]{:S(2)}) collective-permute-start(bf16[8,4096]{1,0:T(8,128)(2,1)S(1)} %get-tuple-element.18), channel_id=1, source_target_pairs={{0,24},{8,16},{16,8},{24,0},{1,25},{9,17},{17,9},{25,1},{2,26},{10... | collective-permute-start | bytes 196616 | tf_op jit(solution)/shard_map/ppermute | solution.py:224
  10.7 5.0 %collective-permute-start.3 = (bf16[8,4096]{1,0:T(8,128)(2,1)S(1)}, bf16[8,4096]{1,0:T(8,128)(2,1)S(1)}, u32[]{:S(2)}, u32[]{:S(2)}) collective-permute-start(bf16[8,4096]{1,0:T(8,128)(2,1)S(1)} %lower.1), channel_id=1, source_target_pairs={{0,8},{8,0},{16,24},{24,16},{1,9},{9,1},{17,25},{25,17},{2,10},{10... | collective-permute-start | bytes 196616 | tf_op jit(solution)/shard_map/ppermute | solution.py:224
  16.7 1.5 %collective-permute-start.6 = (bf16[24,4096]{1,0:T(8,128)(2,1)S(1)}, bf16[24,4096]{1,0:T(8,128)(2,1)S(1)}, u32[]{:S(2)}, u32[]{:S(2)}) collective-permute-start(bf16[24,4096]{1,0:T(8,128)(2,1)S(1)} %get-tuple-element.22), channel_id=1, source_target_pairs={{0,1},{1,0},{2,3},{3,2},{4,5},{5,4},{6,7},{7,6},{8,9},{9,8},{10,11... | collective-permute-start | bytes 589832 | tf_op jit(solution)/shard_map/ppermute | solution.py:224
  16.8 3.5 %collective-permute-start.5 = (bf16[24,4096]{1,0:T(8,128)(2,1)S(1)}, bf16[24,4096]{1,0:T(8,128)(2,1)S(1)}, u32[]{:S(2)}, u32[]{:S(2)}) collective-permute-start(bf16[24,4096]{1,0:T(8,128)(2,1)S(1)} %get-tuple-element.20), channel_id=1, source_target_pairs={{0,1},{1,0},{2,3},{3,2},{4,5},{5,4},{6,7},{7,6},{8,9},{9,8},{10,11... | collective-permute-start | bytes 589832 | tf_op jit(solution)/shard_map/ppermute | solution.py:224
  18.3 7.2 %collective-permute-start.7 = (bf16[24,4096]{1,0:T(8,128)(2,1)S(1)}, bf16[24,4096]{1,0:T(8,128)(2,1)S(1)}, u32[]{:S(2)}, u32[]{:S(2)}) collective-permute-start(bf16[24,4096]{1,0:T(8,128)(2,1)S(1)} %join_cores.1), channel_id=1, source_target_pairs={{0,2},{1,3},{2,0},{3,1},{4,6},{5,7},{6,4},{7,5},{8,10},{9,11},{10,... | collective-permute-start | bytes 589832 | tf_op jit(solution)/shard_map/ppermute | solution.py:224

commit v5 on v3

--- a/solution.py
+++ b/solution.py
@@ -13,6 +13,8 @@
 LANES = 128
 LINES = FLAT // LANES
 ROWS_AT_ONCE = 512
+TILES_AT_ONCE = 4
+LINES_AT_ONCE = 4
 MIB = 1 << 20
 STAGE_FLOPS = 2 * 10**9
 F32, BF16 = jnp.float32, jnp.bfloat16
@@ -23,26 +25,23 @@
     return lax.broadcasted_iota(jnp.int32, shape, axis)
 
 
+def ones_where(hit):
+    return jnp.where(hit, 1.0, 0.0).astype(BF16)
+
+
 def split_inner_order():
     src, dst = iota((LANES, LANES), 0), iota((LANES, LANES), 1)
     half, rest = dst // TILE, dst % TILE
     wanted = half * TILE + 2 * (rest % (TILE // 2)) + rest // (TILE // 2)
-    return jnp.where(src == wanted, 1.0, 0.0).astype(BF16)
+    return ones_where(src == wanted)
 
 
 def twice_on_diagonal(lines):
-    low = iota(lines.shape, 1) < TILE
-    turned = pltpu.roll(lines, TILE, 1)
-    zero = jnp.zeros_like(lines)
-    return jnp.concatenate(
-        [
-            jnp.where(low, lines, zero),
-            jnp.where(low, turned, zero),
-            jnp.where(low, zero, turned),
-            jnp.where(low, zero, lines),
-        ],
-        axis=0,
-    ).astype(BF16)
+    low = ones_where(iota(lines.shape, 1) < TILE)
+    high = ones_where(iota(lines.shape, 1) >= TILE)
+    turned = pltpu.roll(lines, TILE, 1).astype(BF16)
+    lines = lines.astype(BF16)
+    return jnp.concatenate([lines * low, turned * low, turned * high, lines * high], axis=0)
 
 
 def loop(count, few, body):
@@ -119,17 +118,21 @@
     lines_at_once = min(LINES, max(1, ROWS_AT_ONCE // left_tiles))
     rows = lines_at_once * left_tiles
 
-    def pair(p):
+    def some_tiles(p):
         right = jnp.concatenate(
-            [twice_on_diagonal(raw[pl.ds(2 * p + h, LINES, stride=right_tiles), :]) for h in range(2)], axis=1
+            [
+                twice_on_diagonal(raw[pl.ds(p * TILES_AT_ONCE + h, LINES, stride=right_tiles), :])
+                for h in range(TILES_AT_ONCE)
+            ],
+            axis=1,
         )
 
         def some(part):
             at = part * rows if isinstance(part, int) else pl.multiple_of(part * rows, rows)
             got = jnp.dot(a_lines[pl.ds(at, rows), :], right, preferred_element_type=F32).astype(BF16)
             for j in range(lines_at_once):
-                for h in range(2):
-                    to = first + (2 * p + h) * left_tiles
+                for h in range(TILES_AT_ONCE):
+                    to = first + (p * TILES_AT_ONCE + h) * left_tiles
                     to = to if isinstance(to, int) else pl.multiple_of(to, left_tiles)
                     prod[part * lines_at_once + j, pl.ds(to, left_tiles), :] = got[
                         j * left_tiles:(j + 1) * left_tiles, h * LANES:(h + 1) * LANES
@@ -137,14 +140,14 @@
 
         loop(LINES // lines_at_once, 1, some)
 
-    loop(right_tiles // 2, 8 if rows == a_lines.shape[0] else 1, pair)
+    loop(right_tiles // TILES_AT_ONCE, 8 if rows == a_lines.shape[0] else 1, some_tiles)
 
 
 def chosen_sums(sel, first, count, prod, put):
-    for j in range(0, LINES, 2):
-        right = jnp.concatenate([prod[j, :count, :], prod[j + 1, :count, :]], axis=1)
+    for j in range(0, LINES, LINES_AT_ONCE):
+        right = jnp.concatenate([prod[j + i, :count, :] for i in range(LINES_AT_ONCE)], axis=1)
         put(
-            slice(j * LANES, (j + 2) * LANES),
+            slice(j * LANES, (j + LINES_AT_ONCE) * LANES),
             jnp.dot(sel[:, first:first + count], right, preferred_element_type=F32),
         )
 

time: 25.5 us -> 25.5 us (level)
  no operation moved by 1% of the time
where the time goes in v5:
time: 25.5 us; the launch traced here: 25.3 us
  starting transfers between devices  9.55 us (37%)
  waiting for transfers between devices  9.06 us (36%)
  Pallas kernels  5.75 us (23%)
  local copies, waits for them, and re-layouts  0.91 us (4%)
    ppermute x7, starting transfers between devices, exchange(): return lax.ppermute(x, axis, [(i, i ^ q) for i in range(size)])  9.55 us
    ppermute x7, waiting for transfers between devices, exchange(): return lax.ppermute(x, axis, [(i, i ^ q) for i in range(size)])  9.06 us
    pallas_call x1, Pallas kernels, shards(): call(functools.partial(own_kernel, groups, len(a_parts)), [shape((tiles,...  2.01 us
    pallas_call x1, Pallas kernels, shards(): call(functools.partial(more_kernel, 2 * pairs), [shape((tiles, FLAT), F32...  1.11 us
    pallas_call x1, Pallas kernels, shards(): call(functools.partial(last_kernel, 3 * pairs), [shape((owned, FLAT), F32...  1.11 us
    unnamed x8, local copies, waits for them, and re-layouts  0.91 us
    pallas_call x1, Pallas kernels, shards(): call(add_kernel, [shape((owned, FLAT), BF16)], [], 3, 'add_layers', 2 * o...  0.74 us
    pallas_call x1, Pallas kernels, shards(): call(functools.partial(counts_kernel, cols == 2, left_tiles, left_each, r...  0.73 us
  transfers between devices with their start and end apart: 7, of which 5 were waited for; matrix products, arithmetic and copies ran while one was open for 0% of the time, Pallas kernels for 15%

profile of v5, /device:TPU:0, one launch (start us, length us, event | category | flops | bytes accessed | tf_op | source)
XLA Modules:
  0.0 25.3 jit_solution(7910075079084015779)
XLA Ops:
  0.0 4.0 %collective-permute-start.2 = (bf16[16,4096]{1,0:T(8,128)(2,1)}, bf16[16,4096]{1,0:T(8,128)(2,1)S(1)}, u32[]{:S(2)}, u32[]{:S(2)}) collective-permute-start(bf16[16,4096]{1,0:T(8,128)(2,1)} %bitcast.7), channel_id=1, source_target_pairs={{0,16},{8,24},{16,0},{24,8},{1,17},{9,25},{17,1},{25,9},{2,18},{10... | collective-permute-start | bytes 393224 | tf_op jit(solution)/shard_map/ppermute | solution.py:229
  4.0 1.6 %collective-permute-start.1 = (bf16[16,4096]{1,0:T(8,128)(2,1)}, bf16[16,4096]{1,0:T(8,128)(2,1)S(1)}, u32[]{:S(2)}, u32[]{:S(2)}) collective-permute-start(bf16[16,4096]{1,0:T(8,128)(2,1)} %bitcast.8), channel_id=1, source_target_pairs={{0,8},{8,0},{16,24},{24,16},{1,9},{9,1},{17,25},{25,17},{2,10},{10... | collective-permute-start | bytes 393224 | tf_op jit(solution)/shard_map/ppermute | solution.py:229
  5.6 0.0 copy-start
  5.6 1.5 %collective-permute-start = (bf16[8,4096]{1,0:T(8,128)(2,1)}, bf16[8,4096]{1,0:T(8,128)(2,1)S(1)}, u32[]{:S(2)}, u32[]{:S(2)}) collective-permute-start(bf16[8,4096]{1,0:T(8,128)(2,1)} %bitcast.10), channel_id=1, source_target_pairs={{0,4},{4,0},{1,5},{5,1},{2,6},{6,2},{3,7},{7,3},{8,12},{12,8},{9,1... | collective-permute-start | bytes 196616 | tf_op jit(solution)/shard_map/ppermute | solution.py:229
  7.1 0.9 %copy-done.2 = bf16[1,1,1,16,4096]{4,3,2,1,0:T(8,128)(2,1)S(1)} copy-done((bf16[1,1,1,16,4096]{4,3,2,1,0:T(8,128)(2,1)S(1)}, bf16[1,1,1,16,4096]{4,3,2,1,0:T(8,128)(2,1)}, u32[]{:S(2)}) %copy-start.2) | copy-done | bytes 131096
  8.0 0.3 %collective-permute-start.3 = (bf16[16,4096]{1,0:T(8,128)(2,1)S(1)}, bf16[16,4096]{1,0:T(8,128)(2,1)S(1)}, u32[]{:S(2)}, u32[]{:S(2)}) collective-permute-start(bf16[16,4096]{1,0:T(8,128)(2,1)S(1)} %stage.1.refs_2_), channel_id=1, source_target_pairs={{0,24},{8,16},{16,8},{24,0},{1,25},{9,17},{17,9},{25,1},{2,26},{10... | collective-permute-start | bytes 393224 | tf_op jit(solution)/shard_map/ppermute | solution.py:229
  8.3 0.0 copy-done
  8.3 0.0 copy-done.1
  8.3 0.7 %counts.1.sel = bf16[96,1024]{1,0:T(8,128)(2,1)S(1)} custom-call(s32[1,768]{1,0:T(1,128)S(1)} %bitcast.5, s32[1,768]{1,0:T(1,128)S(1)} %bitcast.6), custom_call_target="tpu_custom_call" | custom-call | flops 1179648 | bytes 1048576 | tf_op jit(solution)/shard_map/counts/pallas_call | solution.py:253
  9.1 1.0 %collective-permute-done.refs_1_ = bf16[8,4096]{1,0:T(8,128)(2,1)S(1)} collective-permute-done((bf16[8,4096]{1,0:T(8,128)(2,1)}, bf16[8,4096]{1,0:T(8,128)(2,1)S(1)}, u32[]{:S(2)}, u32[]{:S(2)}) %collective-permute-start) | collective-permute-done | bytes 65568 | tf_op jit(solution)/shard_map/ppermute | solution.py:229
  10.1 1.0 %collective-permute-done.1.refs_3_ = bf16[16,4096]{1,0:T(8,128)(2,1)S(1)} collective-permute-done((bf16[16,4096]{1,0:T(8,128)(2,1)}, bf16[16,4096]{1,0:T(8,128)(2,1)S(1)}, u32[]{:S(2)}, u32[]{:S(2)}) %collective-permute-start.1) | collective-permute-done | bytes 131104 | tf_op jit(solution)/shard_map/ppermute | solution.py:229
  11.1 0.0 copy-done.3
  11.1 2.0 %own_and_near.1 = (f32[96,4096]{1,0:T(8,128)S(1)}, bf16[512,128]{1,0:T(8,128)(2,1)S(1)}) custom-call(bf16[96,1024]{1,0:T(8,128)(2,1)S(1)} %counts.1.sel, bf16[8,4096]{1,0:T(8,128)(2,1)S(1)} %bitcast.11, bf16[8,4096]{1,0:T(8,128)(2,1)S(1)} %collective-permute-done.refs_1_, bf16[16,4096]{1,0:T(8,128)(2,1)S(1)} %stage.1.refs_2_, ...), custom_call_target="tpu_custom_call" | custom-call | flops 939524096 | bytes 8388608 | tf_op jit(solution)/shard_map/own_and_near/pallas_call | solution.py:267
  13.1 0.0 collective-permute-done.2.b_ref
  13.1 1.1 %far_shard.1.acc = f32[96,4096]{1,0:T(8,128)S(1)} custom-call(bf16[96,1024]{1,0:T(8,128)(2,1)S(1)} %counts.1.sel, bf16[512,128]{1,0:T(8,128)(2,1)S(1)} %get-tuple-element.11.a_lines, f32[96,4096]{1,0:T(8,128)S(1)} %get-tuple-element.12.acc, bf16[16,4096]{1,0:T(8,128)(2,1)S(1)} %collective-permute-done.2.b_ref), custom_call_target="tpu_custom_call" | custom-call | flops 469762048 | bytes 4194304 | tf_op jit(solution)/shard_map/far_shard/pallas_call | solution.py:276
  14.2 0.7 %collective-permute-done.3.b_ref = bf16[16,4096]{1,0:T(8,128)(2,1)S(1)} collective-permute-done((bf16[16,4096]{1,0:T(8,128)(2,1)S(1)}, bf16[16,4096]{1,0:T(8,128)(2,1)S(1)}, u32[]{:S(2)}, u32[]{:S(2)}) %collective-permute-start.3) | collective-permute-done | bytes 131104 | tf_op jit(solution)/shard_map/ppermute | solution.py:229
  14.9 1.1 %last_shard.1 = (f32[24,4096]{1,0:T(8,128)S(1)}, f32[24,4096]{1,0:T(8,128)S(1)}, bf16[24,4096]{1,0:T(8,128)(2,1)S(1)}, bf16[24,4096]{1,0:T(8,128)(2,1)S(1)}) custom-call(bf16[96,1024]{1,0:T(8,128)(2,1)S(1)} %counts.1.sel, bf16[512,128]{1,0:T(8,128)(2,1)S(1)} %get-tuple-element.11.a_lines, f32[96,4096]{1,0:T(8,128)S(1)} %far_shard.1.acc, ...), custom_call_target="tpu_custom_call" | custom-call | flops 469762048 | bytes 4194304 | tf_op jit(solution)/shard_map/last_shard/pallas_call | solution.py:285
  16.0 0.1 collective-permute-start.5
  16.1 0.5 %collective-permute-start.4 = (bf16[24,4096]{1,0:T(8,128)(2,1)S(1)}, bf16[24,4096]{1,0:T(8,128)(2,1)S(1)}, u32[]{:S(2)}, u32[]{:S(2)}) collective-permute-start(bf16[24,4096]{1,0:T(8,128)(2,1)S(1)} %get-tuple-element.14), channel_id=1, source_target_pairs={{0,1},{1,0},{2,3},{3,2},{4,5},{5,4},{6,7},{7,6},{8,9},{9,8},{10,11... | collective-permute-start | bytes 589832 | tf_op jit(solution)/shard_map/ppermute | solution.py:229
  16.6 0.9 %collective-permute-done.5.arrived = bf16[24,4096]{1,0:T(8,128)(2,1)S(1)} collective-permute-done((bf16[24,4096]{1,0:T(8,128)(2,1)S(1)}, bf16[24,4096]{1,0:T(8,128)(2,1)S(1)}, u32[]{:S(2)}, u32[]{:S(2)}) %collective-permute-start.5) | collective-permute-done | bytes 196640 | tf_op jit(solution)/shard_map/ppermute | solution.py:229
  17.6 1.6 %collective-permute-start.6 = (bf16[24,4096]{1,0:T(8,128)(2,1)S(1)}, bf16[24,4096]{1,0:T(8,128)(2,1)S(1)}, u32[]{:S(2)}, u32[]{:S(2)}) collective-permute-start(bf16[24,4096]{1,0:T(8,128)(2,1)S(1)} %join_cores.1), channel_id=1, source_target_pairs={{0,2},{1,3},{2,0},{3,1},{4,6},{5,7},{6,4},{7,5},{8,10},{9,11},{10,... | collective-permute-start | bytes 589832 | tf_op jit(solution)/shard_map/ppermute | solution.py:229
  19.2 0.0 collective-permute-done.4.arrived
  19.2 5.4 %collective-permute-done.6.joined = bf16[24,4096]{1,0:T(8,128)(2,1)S(1)} collective-permute-done((bf16[24,4096]{1,0:T(8,128)(2,1)S(1)}, bf16[24,4096]{1,0:T(8,128)(2,1)S(1)}, u32[]{:S(2)}, u32[]{:S(2)}) %collective-permute-start.6) | collective-permute-done | bytes 196640 | tf_op jit(solution)/shard_map/ppermute | solution.py:229
  24.6 0.7 %add_layers.1 = bf16[24,4096]{1,0:T(8,128)(2,1)} custom-call(f32[24,4096]{1,0:T(8,128)S(1)} %get-tuple-element.13.own, bf16[24,4096]{1,0:T(8,128)(2,1)S(1)} %collective-permute-done.4.arrived, bf16[24,4096]{1,0:T(8,128)(2,1)S(1)} %collective-permute-done.6.joined), custom_call_target="tpu_custom_call" | custom-call | flops 196608 | bytes 1048576 | tf_op jit(solution)/shard_map/add_layers/pallas_call | solution.py:300
  (5 shorter events, 0.1 us)
Async XLA Ops:
  0.0 13.1 %collective-permute-start.2 = (bf16[16,4096]{1,0:T(8,128)(2,1)}, bf16[16,4096]{1,0:T(8,128)(2,1)S(1)}, u32[]{:S(2)}, u32[]{:S(2)}) collective-permute-start(bf16[16,4096]{1,0:T(8,128)(2,1)} %bitcast.7), channel_id=1, source_target_pairs={{0,16},{8,24},{16,0},{24,8},{1,17},{9,25},{17,1},{25,9},{2,18},{10... | collective-permute-start | bytes 393224 | tf_op jit(solution)/shard_map/ppermute | solution.py:229
  4.0 7.0 %collective-permute-start.1 = (bf16[16,4096]{1,0:T(8,128)(2,1)}, bf16[16,4096]{1,0:T(8,128)(2,1)S(1)}, u32[]{:S(2)}, u32[]{:S(2)}) collective-permute-start(bf16[16,4096]{1,0:T(8,128)(2,1)} %bitcast.8), channel_id=1, source_target_pairs={{0,8},{8,0},{16,24},{24,16},{1,9},{9,1},{17,25},{25,17},{2,10},{10... | collective-permute-start | bytes 393224 | tf_op jit(solution)/shard_map/ppermute | solution.py:229
  5.6 2.7 %copy-start = (s32[1,1,1,768]{3,2,1,0:T(1,128)S(1)}, s32[1,1,1,768]{3,2,1,0:T(1,128)}, u32[]{:S(2)}) copy-start(s32[1,1,1,768]{3,2,1,0:T(1,128)} %param.6) | copy-start | bytes 9220
  5.6 2.7 %copy-start.1 = (s32[1,1,1,768]{3,2,1,0:T(1,128)S(1)}, s32[1,1,1,768]{3,2,1,0:T(1,128)}, u32[]{:S(2)}) copy-start(s32[1,1,1,768]{3,2,1,0:T(1,128)} %param.7) | copy-start | bytes 9220
  5.6 4.5 %collective-permute-start = (bf16[8,4096]{1,0:T(8,128)(2,1)}, bf16[8,4096]{1,0:T(8,128)(2,1)S(1)}, u32[]{:S(2)}, u32[]{:S(2)}) collective-permute-start(bf16[8,4096]{1,0:T(8,128)(2,1)} %bitcast.10), channel_id=1, source_target_pairs={{0,4},{4,0},{1,5},{5,1},{2,6},{6,2},{3,7},{7,3},{8,12},{12,8},{9,1... | collective-permute-start | bytes 196616 | tf_op jit(solution)/shard_map/ppermute | solution.py:229
  7.1 0.9 %copy-start.2 = (bf16[1,1,1,16,4096]{4,3,2,1,0:T(8,128)(2,1)S(1)}, bf16[1,1,1,16,4096]{4,3,2,1,0:T(8,128)(2,1)}, u32[]{:S(2)}) copy-start(bf16[1,1,1,16,4096]{4,3,2,1,0:T(8,128)(2,1)} %param.5) | copy-start | bytes 393220
  8.0 3.1 %copy-start.3 = (bf16[1,1,1,8,4096]{4,3,2,1,0:T(8,128)(2,1)S(1)}, bf16[1,1,1,8,4096]{4,3,2,1,0:T(8,128)(2,1)}, u32[]{:S(2)}) copy-start(bf16[1,1,1,8,4096]{4,3,2,1,0:T(8,128)(2,1)} %param.4) | copy-start | bytes 196612
  8.0 6.9 %collective-permute-start.3 = (bf16[16,4096]{1,0:T(8,128)(2,1)S(1)}, bf16[16,4096]{1,0:T(8,128)(2,1)S(1)}, u32[]{:S(2)}, u32[]{:S(2)}) collective-permute-start(bf16[16,4096]{1,0:T(8,128)(2,1)S(1)} %stage.1.refs_2_), channel_id=1, source_target_pairs={{0,24},{8,16},{16,8},{24,0},{1,25},{9,17},{17,9},{25,1},{2,26},{10... | collective-permute-start | bytes 393224 | tf_op jit(solution)/shard_map/ppermute | solution.py:229
  16.0 1.5 %collective-permute-start.5 = (bf16[24,4096]{1,0:T(8,128)(2,1)S(1)}, bf16[24,4096]{1,0:T(8,128)(2,1)S(1)}, u32[]{:S(2)}, u32[]{:S(2)}) collective-permute-start(bf16[24,4096]{1,0:T(8,128)(2,1)S(1)} %get-tuple-element.16), channel_id=1, source_target_pairs={{0,1},{1,0},{2,3},{3,2},{4,5},{5,4},{6,7},{7,6},{8,9},{9,8},{10,11... | collective-permute-start | bytes 589832 | tf_op jit(solution)/shard_map/ppermute | solution.py:229
  16.1 3.1 %collective-permute-start.4 = (bf16[24,4096]{1,0:T(8,128)(2,1)S(1)}, bf16[24,4096]{1,0:T(8,128)(2,1)S(1)}, u32[]{:S(2)}, u32[]{:S(2)}) collective-permute-start(bf16[24,4096]{1,0:T(8,128)(2,1)S(1)} %get-tuple-element.14), channel_id=1, source_target_pairs={{0,1},{1,0},{2,3},{3,2},{4,5},{5,4},{6,7},{7,6},{8,9},{9,8},{10,11... | collective-permute-start | bytes 589832 | tf_op jit(solution)/shard_map/ppermute | solution.py:229
  17.6 7.0 %collective-permute-start.6 = (bf16[24,4096]{1,0:T(8,128)(2,1)S(1)}, bf16[24,4096]{1,0:T(8,128)(2,1)S(1)}, u32[]{:S(2)}, u32[]{:S(2)}) collective-permute-start(bf16[24,4096]{1,0:T(8,128)(2,1)S(1)} %join_cores.1), channel_id=1, source_target_pairs={{0,2},{1,3},{2,0},{3,1},{4,6},{5,7},{6,4},{7,5},{8,10},{9,11},{10,... | collective-permute-start | bytes 589832 | tf_op jit(solution)/shard_map/ppermute | solution.py:229

commit v6 on v5

--- a/solution.py
+++ b/solution.py
@@ -16,6 +16,7 @@
 TILES_AT_ONCE = 4
 LINES_AT_ONCE = 4
 MIB = 1 << 20
+OWN_FLOPS = 500 * 10**6
 STAGE_FLOPS = 2 * 10**9
 F32, BF16 = jnp.float32, jnp.bfloat16
 OWNER_ORDER = (0, 2, 3, 1)
@@ -52,9 +53,13 @@
         pl.loop(0, count)(body)
 
 
-def stage_kernel(*refs):
-    for ref, out in zip(refs[:len(refs) // 2], refs[len(refs) // 2:]):
-        out[...] = ref[...]
+def stage_kernel(b_ref, out, straight):
+    out[...] = b_ref[...]
+    straight[...] = b_ref[:, b_ref.shape[1] - straight.shape[1]:]
+
+
+def first_columns_kernel(b_ref, out):
+    out[...] = b_ref[:, :out.shape[1]]
 
 
 def counts_kernel(swap, left_tiles, left_each, right_each, a_slots, b_slots, sel):
@@ -110,11 +115,12 @@
         a_lines[i * left_tiles:(i + lines_at_once) * left_tiles, :] = got.astype(BF16)
 
 
-def all_products(a_lines, b_ref, raw, prod, first):
-    right_tiles = b_ref.shape[0]
+def all_products(a_lines, b_refs, raw, prod, first):
+    right_tiles = b_refs[0].shape[0]
     left_tiles = a_lines.shape[0] // LINES
-    for i in range(LINES):
-        raw[i * right_tiles:(i + 1) * right_tiles, :] = b_ref[:, i * LANES:(i + 1) * LANES].astype(F32)
+    blocks = [(b_ref, i) for b_ref in b_refs for i in range(0, b_ref.shape[1], LANES)]
+    for line, (b_ref, i) in enumerate(blocks):
+        raw[line * right_tiles:(line + 1) * right_tiles, :] = b_ref[:, i:i + LANES].astype(F32)
     lines_at_once = min(LINES, max(1, ROWS_AT_ONCE // left_tiles))
     rows = lines_at_once * left_tiles
 
@@ -160,8 +166,9 @@
     add_shards(0, groups, sel, a_lines, b_refs, None, acc, raw, prod)
 
 
-def more_kernel(start, sel, a_lines, acc, b_ref, out, raw, prod):
-    add_shards(start, (1,), sel, a_lines, (b_ref,), acc, out, raw, prod)
+def more_kernel(start, groups, sel, a_lines, acc, *refs):
+    b_refs, (out, raw, prod) = refs[:-3], refs[-3:]
+    add_shards(start, groups, sel, a_lines, b_refs, acc, out, raw, prod)
 
 
 def add_shards(start, groups, sel, a_lines, b_refs, acc, out, raw, prod):
@@ -171,7 +178,7 @@
         done = 0
         before = out if taken else acc
         for b_ref in b_refs[taken:taken + count]:
-            all_products(a_lines, b_ref, raw, prod, done)
+            all_products(a_lines, [b_ref], raw, prod, done)
             done += b_ref.shape[0] * each
 
         def put(columns, value):
@@ -182,10 +189,10 @@
         start += done
 
 
-def last_kernel(start, sel, a_lines, acc, b_ref, own, far, cross, near, raw, prod):
-    pairs = b_ref.shape[0] * a_lines.shape[0] // LINES
+def last_kernel(start, sel, a_lines, acc, b_sent_on, b_straight, own, far, cross, near, raw, prod):
+    pairs = b_straight.shape[0] * a_lines.shape[0] // LINES
     owned = own.shape[0]
-    all_products(a_lines, b_ref, raw, prod, 0)
+    all_products(a_lines, [b_sent_on, b_straight], raw, prod, 0)
 
     def put(columns, value):
         value = value + acc[:, columns]
@@ -247,9 +254,22 @@
         a_parts = [a_local, exchange(a_local, "col", 1)]
     else:
         a_parts = [lax.all_gather(a_local, "col", axis=0, tiled=True)]
-    (b_here,) = call(stage_kernel, [shape(b_local.shape, BF16)], [], 1, "stage", STAGE_FLOPS, MIB)(b_local)
+    sent_on = FLAT // 4
+    b_here, b_straight = call(
+        stage_kernel,
+        [shape(b_local.shape, BF16), shape((right_each, FLAT - sent_on), BF16)],
+        [],
+        1,
+        "stage",
+        STAGE_FLOPS,
+        MIB,
+    )(b_local)
     b_near = exchange(b_local, "row", 1)
-    b_last = exchange(b_here, "row", 3)
+    last_straight = exchange(b_straight, "row", 3)
+    (b_first,) = call(
+        first_columns_kernel, [shape((right_each, sent_on), BF16)], [], 1, "first_columns", FLAT, MIB
+    )(b_far)
+    last_sent_on = exchange(b_first, "row", 1)
     (sel,) = call(
         functools.partial(counts_kernel, cols == 2, left_tiles, left_each, right_each),
         [shape((tiles, rows * pairs), BF16)],
@@ -265,32 +285,32 @@
     one = shape((LINES, pairs, LANES), BF16)
     shard_flops = 2 * pairs * LINES * LANES * LANES + 2 * pairs * tiles * FLAT
     acc, a_lines = call(
-        functools.partial(own_kernel, groups, len(a_parts)),
+        functools.partial(own_kernel, (1,), len(a_parts)),
         [shape((tiles, FLAT), F32), shape((left_tiles * LINES, LANES), BF16)],
+        [raw, one],
+        2 + len(a_parts),
+        "own_shard",
+        OWN_FLOPS,
+        4 * MIB,
+    )(sel, *a_parts, b_here)
+    (acc,) = call(
+        functools.partial(more_kernel, pairs, groups),
+        [shape((tiles, FLAT), F32)],
         [raw, shape((LINES, max(groups) * pairs, LANES), BF16)],
-        3 + len(a_parts),
-        "own_and_near",
+        5,
+        "near_and_far",
         2 * shard_flops,
         8 * MIB,
-    )(sel, *a_parts, b_here, b_near)
-    (acc,) = call(
-        functools.partial(more_kernel, 2 * pairs),
-        [shape((tiles, FLAT), F32)],
-        [raw, one],
-        4,
-        "far_shard",
-        shard_flops,
-        4 * MIB,
-    )(sel, a_lines, acc, b_far)
+    )(sel, a_lines, acc, b_near, b_far)
     own, far, cross, near = call(
         functools.partial(last_kernel, 3 * pairs),
         [shape((owned, FLAT), F32)] * 2 + [shape((owned, FLAT), BF16)] * 2,
         [raw, one],
-        4,
+        5,
         "last_shard",
         shard_flops,
         4 * MIB,
-    )(sel, a_lines, acc, b_last)
+    )(sel, a_lines, acc, last_sent_on, last_straight)
 
     arrived_cross = exchange(cross, "layer", 1)
     arrived_near = exchange(near, "layer", 1)

time: 25.5 us -> 25.8 us (1.012)
  starting transfers between devices: 9.55 us -> 10.7 us
  waiting for transfers between devices: 9.06 us -> 8.25 us
    ppermute x7 -> x8, starting transfers between devices: 9.55 us -> 10.7 us  [exchange(): return lax.ppermute(x, axis, [(i, i ^ q) for i in range(size)])]
    ppermute x7 -> x8, waiting for transfers between devices: 9.06 us -> 8.25 us  [exchange(): return lax.ppermute(x, axis, [(i, i ^ q) for i in range(size)])]
    pallas_call x3 -> x4, Pallas kernels: 3.14 us -> 3.14 us  [the longest x1 1.97 us: shards(): call(functools.partial(more_kernel, pairs, groups), [shape((tiles, FLAT),...]
  transfers between devices with their start and end apart: 7 -> 8, of which waited for: 5 -> 5; matrix products, arithmetic and copies ran while one was open for 0% -> 0% of each run, Pallas kernels for 15% -> 15%
where the time goes in v6:
time: 25.8 us; the launch traced here: 25.7 us
  starting transfers between devices  10.7 us (41%)
  waiting for transfers between devices  8.25 us (32%)
  Pallas kernels  5.75 us (22%)
  local copies, waits for them, and re-layouts  0.91 us (4%)
    ppermute x8, starting transfers between devices, exchange(): return lax.ppermute(x, axis, [(i, i ^ q) for i in range(size)])  10.7 us
    ppermute x8, waiting for transfers between devices, exchange(): return lax.ppermute(x, axis, [(i, i ^ q) for i in range(size)])  8.25 us
    pallas_call x1, Pallas kernels, shards(): call(functools.partial(more_kernel, pairs, groups), [shape((tiles, FLAT),...  1.97 us
    pallas_call x1, Pallas kernels, shards(): call(functools.partial(own_kernel, (1,), len(a_parts)), [shape((tiles, FL...  1.15 us
    pallas_call x1, Pallas kernels, shards(): call(functools.partial(last_kernel, 3 * pairs), [shape((owned, FLAT), F32...  1.11 us
    unnamed x8, local copies, waits for them, and re-layouts  0.91 us
    pallas_call x1, Pallas kernels, shards(): call(add_kernel, [shape((owned, FLAT), BF16)], [], 3, 'add_layers', 2 * o...  0.74 us
    pallas_call x1, Pallas kernels, shards(): call(functools.partial(counts_kernel, cols == 2, left_tiles, left_each, r...  0.73 us
  transfers between devices with their start and end apart: 8, of which 5 were waited for; matrix products, arithmetic and copies ran while one was open for 0% of the time, Pallas kernels for 15%

profile of v6, /device:TPU:0, one launch (start us, length us, event | category | flops | bytes accessed | tf_op | source)
XLA Modules:
  0.0 25.7 jit_solution(8182584420536973352)
XLA Ops:
  0.0 4.0 %collective-permute-start.2 = (bf16[16,4096]{1,0:T(8,128)(2,1)}, bf16[16,4096]{1,0:T(8,128)(2,1)S(1)}, u32[]{:S(2)}, u32[]{:S(2)}) collective-permute-start(bf16[16,4096]{1,0:T(8,128)(2,1)} %bitcast.7), channel_id=1, source_target_pairs={{0,16},{8,24},{16,0},{24,8},{1,17},{9,25},{17,1},{25,9},{2,18},{10... | collective-permute-start | bytes 393224 | tf_op jit(solution)/shard_map/ppermute | solution.py:236
  4.0 1.6 %collective-permute-start.1 = (bf16[16,4096]{1,0:T(8,128)(2,1)}, bf16[16,4096]{1,0:T(8,128)(2,1)S(1)}, u32[]{:S(2)}, u32[]{:S(2)}) collective-permute-start(bf16[16,4096]{1,0:T(8,128)(2,1)} %bitcast.8), channel_id=1, source_target_pairs={{0,8},{8,0},{16,24},{24,16},{1,9},{9,1},{17,25},{25,17},{2,10},{10... | collective-permute-start | bytes 393224 | tf_op jit(solution)/shard_map/ppermute | solution.py:236
  5.6 1.5 %collective-permute-start = (bf16[8,4096]{1,0:T(8,128)(2,1)}, bf16[8,4096]{1,0:T(8,128)(2,1)S(1)}, u32[]{:S(2)}, u32[]{:S(2)}) collective-permute-start(bf16[8,4096]{1,0:T(8,128)(2,1)} %bitcast.10), channel_id=1, source_target_pairs={{0,4},{4,0},{1,5},{5,1},{2,6},{6,2},{3,7},{7,3},{8,12},{12,8},{9,1... | collective-permute-start | bytes 196616 | tf_op jit(solution)/shard_map/ppermute | solution.py:236
  7.1 0.9 %copy-done.2 = bf16[1,1,1,16,4096]{4,3,2,1,0:T(8,128)(2,1)S(1)} copy-done((bf16[1,1,1,16,4096]{4,3,2,1,0:T(8,128)(2,1)S(1)}, bf16[1,1,1,16,4096]{4,3,2,1,0:T(8,128)(2,1)}, u32[]{:S(2)}) %copy-start.2) | copy-done | bytes 131096
  8.0 0.3 %collective-permute-start.4 = (bf16[16,3072]{1,0:T(8,128)(2,1)S(1)}, bf16[16,3072]{1,0:T(8,128)(2,1)S(1)}, u32[]{:S(2)}, u32[]{:S(2)}) collective-permute-start(bf16[16,3072]{1,0:T(8,128)(2,1)S(1)} %get-tuple-element.16), channel_id=1, source_target_pairs={{0,24},{8,16},{16,8},{24,0},{1,25},{9,17},{17,9},{25,1},{2,26},{10... | collective-permute-start | bytes 294920 | tf_op jit(solution)/shard_map/ppermute | solution.py:236
  8.3 0.0 copy-done
  8.3 0.0 copy-done.1
  8.3 0.7 %counts.1.sel = bf16[96,1024]{1,0:T(8,128)(2,1)S(1)} custom-call(s32[1,768]{1,0:T(1,128)S(1)} %bitcast.5, s32[1,768]{1,0:T(1,128)S(1)} %bitcast.6), custom_call_target="tpu_custom_call" | custom-call | flops 1179648 | bytes 1048576 | tf_op jit(solution)/shard_map/counts/pallas_call | solution.py:273
  9.1 1.0 %collective-permute-done.refs_1_ = bf16[8,4096]{1,0:T(8,128)(2,1)S(1)} collective-permute-done((bf16[8,4096]{1,0:T(8,128)(2,1)}, bf16[8,4096]{1,0:T(8,128)(2,1)S(1)}, u32[]{:S(2)}, u32[]{:S(2)}) %collective-permute-start) | collective-permute-done | bytes 65568 | tf_op jit(solution)/shard_map/ppermute | solution.py:236
  10.1 1.1 %own_shard.1 = (f32[96,4096]{1,0:T(8,128)S(1)}, bf16[512,128]{1,0:T(8,128)(2,1)S(1)}) custom-call(bf16[96,1024]{1,0:T(8,128)(2,1)S(1)} %counts.1.sel, bf16[8,4096]{1,0:T(8,128)(2,1)S(1)} %bitcast.11, bf16[8,4096]{1,0:T(8,128)(2,1)S(1)} %collective-permute-done.refs_1_, bf16[16,4096]{1,0:T(8,128)(2,1)S(1)} %get-tuple-element.13.refs_2_), custom_call_target="tpu_custom_call" | custom-call | flops 500000000 | bytes 4194304 | tf_op jit(solution)/shard_map/own_shard/pallas_call | solution.py:287
  11.2 0.0 collective-permute-done.2.refs_1_.b_ref
  11.3 1.1 %collective-permute-start.3 = (bf16[16,1024]{1,0:T(8,128)(2,1)S(1)}, bf16[16,1024]{1,0:T(8,128)(2,1)S(1)}, u32[]{:S(2)}, u32[]{:S(2)}) collective-permute-start(bf16[16,1024]{1,0:T(8,128)(2,1)S(1)} %first_columns.1), channel_id=1, source_target_pairs={{0,8},{8,0},{16,24},{24,16},{1,9},{9,1},{17,25},{25,17},{2,10},{10... | collective-permute-start | bytes 98312 | tf_op jit(solution)/shard_map/ppermute | solution.py:236
  12.4 0.0 collective-permute-done.1.refs_0_
  12.4 2.0 %near_and_far.1.acc = f32[96,4096]{1,0:T(8,128)S(1)} custom-call(bf16[96,1024]{1,0:T(8,128)(2,1)S(1)} %counts.1.sel, bf16[512,128]{1,0:T(8,128)(2,1)S(1)} %get-tuple-element.14.a_lines, f32[96,4096]{1,0:T(8,128)S(1)} %get-tuple-element.15.acc, bf16[16,4096]{1,0:T(8,128)(2,1)S(1)} %collective-permute-done.1.refs_0_, ...), custom_call_target="tpu_custom_call" | custom-call | flops 939524096 | bytes 8388608 | tf_op jit(solution)/shard_map/near_and_far/pallas_call | solution.py:296
  14.4 0.3 %collective-permute-done.4.b_straight = bf16[16,3072]{1,0:T(8,128)(2,1)S(1)} collective-permute-done((bf16[16,3072]{1,0:T(8,128)(2,1)S(1)}, bf16[16,3072]{1,0:T(8,128)(2,1)S(1)}, u32[]{:S(2)}, u32[]{:S(2)}) %collective-permute-start.4) | collective-permute-done | bytes 98336 | tf_op jit(solution)/shard_map/ppermute | solution.py:236
  14.6 0.6 %collective-permute-done.3.b_sent_on = bf16[16,1024]{1,0:T(8,128)(2,1)S(1)} collective-permute-done((bf16[16,1024]{1,0:T(8,128)(2,1)S(1)}, bf16[16,1024]{1,0:T(8,128)(2,1)S(1)}, u32[]{:S(2)}, u32[]{:S(2)}) %collective-permute-start.3) | collective-permute-done | bytes 32800 | tf_op jit(solution)/shard_map/ppermute | solution.py:236
  15.3 1.1 %last_shard.1 = (f32[24,4096]{1,0:T(8,128)S(1)}, f32[24,4096]{1,0:T(8,128)S(1)}, bf16[24,4096]{1,0:T(8,128)(2,1)S(1)}, bf16[24,4096]{1,0:T(8,128)(2,1)S(1)}) custom-call(bf16[96,1024]{1,0:T(8,128)(2,1)S(1)} %counts.1.sel, bf16[512,128]{1,0:T(8,128)(2,1)S(1)} %get-tuple-element.14.a_lines, f32[96,4096]{1,0:T(8,128)S(1)} %near_and_far.1.acc, ...), custom_call_target="tpu_custom_call" | custom-call | flops 469762048 | bytes 4194304 | tf_op jit(solution)/shard_map/last_shard/pallas_call | solution.py:305
  16.4 0.1 collective-permute-start.6
  16.4 0.5 %collective-permute-start.5 = (bf16[24,4096]{1,0:T(8,128)(2,1)S(1)}, bf16[24,4096]{1,0:T(8,128)(2,1)S(1)}, u32[]{:S(2)}, u32[]{:S(2)}) collective-permute-start(bf16[24,4096]{1,0:T(8,128)(2,1)S(1)} %get-tuple-element.18), channel_id=1, source_target_pairs={{0,1},{1,0},{2,3},{3,2},{4,5},{5,4},{6,7},{7,6},{8,9},{9,8},{10,11... | collective-permute-start | bytes 589832 | tf_op jit(solution)/shard_map/ppermute | solution.py:236
  16.9 0.9 %collective-permute-done.6.arrived = bf16[24,4096]{1,0:T(8,128)(2,1)S(1)} collective-permute-done((bf16[24,4096]{1,0:T(8,128)(2,1)S(1)}, bf16[24,4096]{1,0:T(8,128)(2,1)S(1)}, u32[]{:S(2)}, u32[]{:S(2)}) %collective-permute-start.6) | collective-permute-done | bytes 196640 | tf_op jit(solution)/shard_map/ppermute | solution.py:236
  17.9 1.6 %collective-permute-start.7 = (bf16[24,4096]{1,0:T(8,128)(2,1)S(1)}, bf16[24,4096]{1,0:T(8,128)(2,1)S(1)}, u32[]{:S(2)}, u32[]{:S(2)}) collective-permute-start(bf16[24,4096]{1,0:T(8,128)(2,1)S(1)} %join_cores.1), channel_id=1, source_target_pairs={{0,2},{1,3},{2,0},{3,1},{4,6},{5,7},{6,4},{7,5},{8,10},{9,11},{10,... | collective-permute-start | bytes 589832 | tf_op jit(solution)/shard_map/ppermute | solution.py:236
  19.5 0.0 collective-permute-done.5.arrived
  19.5 5.4 %collective-permute-done.7.joined = bf16[24,4096]{1,0:T(8,128)(2,1)S(1)} collective-permute-done((bf16[24,4096]{1,0:T(8,128)(2,1)S(1)}, bf16[24,4096]{1,0:T(8,128)(2,1)S(1)}, u32[]{:S(2)}, u32[]{:S(2)}) %collective-permute-start.7) | collective-permute-done | bytes 196640 | tf_op jit(solution)/shard_map/ppermute | solution.py:236
  24.9 0.7 %add_layers.1 = bf16[24,4096]{1,0:T(8,128)(2,1)} custom-call(f32[24,4096]{1,0:T(8,128)S(1)} %get-tuple-element.17.own, bf16[24,4096]{1,0:T(8,128)(2,1)S(1)} %collective-permute-done.5.arrived, bf16[24,4096]{1,0:T(8,128)(2,1)S(1)} %collective-permute-done.7.joined), custom_call_target="tpu_custom_call" | custom-call | flops 196608 | bytes 1048576 | tf_op jit(solution)/shard_map/add_layers/pallas_call | solution.py:320
  (8 shorter events, 0.1 us)
Async XLA Ops:
  0.0 11.3 %collective-permute-start.2 = (bf16[16,4096]{1,0:T(8,128)(2,1)}, bf16[16,4096]{1,0:T(8,128)(2,1)S(1)}, u32[]{:S(2)}, u32[]{:S(2)}) collective-permute-start(bf16[16,4096]{1,0:T(8,128)(2,1)} %bitcast.7), channel_id=1, source_target_pairs={{0,16},{8,24},{16,0},{24,8},{1,17},{9,25},{17,1},{25,9},{2,18},{10... | collective-permute-start | bytes 393224 | tf_op jit(solution)/shard_map/ppermute | solution.py:236
  4.0 8.3 %collective-permute-start.1 = (bf16[16,4096]{1,0:T(8,128)(2,1)}, bf16[16,4096]{1,0:T(8,128)(2,1)S(1)}, u32[]{:S(2)}, u32[]{:S(2)}) collective-permute-start(bf16[16,4096]{1,0:T(8,128)(2,1)} %bitcast.8), channel_id=1, source_target_pairs={{0,8},{8,0},{16,24},{24,16},{1,9},{9,1},{17,25},{25,17},{2,10},{10... | collective-permute-start | bytes 393224 | tf_op jit(solution)/shard_map/ppermute | solution.py:236
  5.6 2.7 %copy-start = (s32[1,1,1,768]{3,2,1,0:T(1,128)S(1)}, s32[1,1,1,768]{3,2,1,0:T(1,128)}, u32[]{:S(2)}) copy-start(s32[1,1,1,768]{3,2,1,0:T(1,128)} %param.6) | copy-start | bytes 9220
  5.6 2.7 %copy-start.1 = (s32[1,1,1,768]{3,2,1,0:T(1,128)S(1)}, s32[1,1,1,768]{3,2,1,0:T(1,128)}, u32[]{:S(2)}) copy-start(s32[1,1,1,768]{3,2,1,0:T(1,128)} %param.7) | copy-start | bytes 9220
  5.6 4.5 %collective-permute-start = (bf16[8,4096]{1,0:T(8,128)(2,1)}, bf16[8,4096]{1,0:T(8,128)(2,1)S(1)}, u32[]{:S(2)}, u32[]{:S(2)}) collective-permute-start(bf16[8,4096]{1,0:T(8,128)(2,1)} %bitcast.10), channel_id=1, source_target_pairs={{0,4},{4,0},{1,5},{5,1},{2,6},{6,2},{3,7},{7,3},{8,12},{12,8},{9,1... | collective-permute-start | bytes 196616 | tf_op jit(solution)/shard_map/ppermute | solution.py:236
  7.1 0.9 %copy-start.2 = (bf16[1,1,1,16,4096]{4,3,2,1,0:T(8,128)(2,1)S(1)}, bf16[1,1,1,16,4096]{4,3,2,1,0:T(8,128)(2,1)}, u32[]{:S(2)}) copy-start(bf16[1,1,1,16,4096]{4,3,2,1,0:T(8,128)(2,1)} %param.5) | copy-start | bytes 393220
  8.0 2.1 %copy-start.3 = (bf16[1,1,1,8,4096]{4,3,2,1,0:T(8,128)(2,1)S(1)}, bf16[1,1,1,8,4096]{4,3,2,1,0:T(8,128)(2,1)}, u32[]{:S(2)}) copy-start(bf16[1,1,1,8,4096]{4,3,2,1,0:T(8,128)(2,1)} %param.4) | copy-start | bytes 196612
  8.0 6.6 %collective-permute-start.4 = (bf16[16,3072]{1,0:T(8,128)(2,1)S(1)}, bf16[16,3072]{1,0:T(8,128)(2,1)S(1)}, u32[]{:S(2)}, u32[]{:S(2)}) collective-permute-start(bf16[16,3072]{1,0:T(8,128)(2,1)S(1)} %get-tuple-element.16), channel_id=1, source_target_pairs={{0,24},{8,16},{16,8},{24,0},{1,25},{9,17},{17,9},{25,1},{2,26},{10... | collective-permute-start | bytes 294920 | tf_op jit(solution)/shard_map/ppermute | solution.py:236
  11.3 4.0 %collective-permute-start.3 = (bf16[16,1024]{1,0:T(8,128)(2,1)S(1)}, bf16[16,1024]{1,0:T(8,128)(2,1)S(1)}, u32[]{:S(2)}, u32[]{:S(2)}) collective-permute-start(bf16[16,1024]{1,0:T(8,128)(2,1)S(1)} %first_columns.1), channel_id=1, source_target_pairs={{0,8},{8,0},{16,24},{24,16},{1,9},{9,1},{17,25},{25,17},{2,10},{10... | collective-permute-start | bytes 98312 | tf_op jit(solution)/shard_map/ppermute | solution.py:236
  16.4 1.5 %collective-permute-start.6 = (bf16[24,4096]{1,0:T(8,128)(2,1)S(1)}, bf16[24,4096]{1,0:T(8,128)(2,1)S(1)}, u32[]{:S(2)}, u32[]{:S(2)}) collective-permute-start(bf16[24,4096]{1,0:T(8,128)(2,1)S(1)} %get-tuple-element.20), channel_id=1, source_target_pairs={{0,1},{1,0},{2,3},{3,2},{4,5},{5,4},{6,7},{7,6},{8,9},{9,8},{10,11... | collective-permute-start | bytes 589832 | tf_op jit(solution)/shard_map/ppermute | solution.py:236
  16.4 3.1 %collective-permute-start.5 = (bf16[24,4096]{1,0:T(8,128)(2,1)S(1)}, bf16[24,4096]{1,0:T(8,128)(2,1)S(1)}, u32[]{:S(2)}, u32[]{:S(2)}) collective-permute-start(bf16[24,4096]{1,0:T(8,128)(2,1)S(1)} %get-tuple-element.18), channel_id=1, source_target_pairs={{0,1},{1,0},{2,3},{3,2},{4,5},{5,4},{6,7},{7,6},{8,9},{9,8},{10,11... | collective-permute-start | bytes 589832 | tf_op jit(solution)/shard_map/ppermute | solution.py:236
  17.9 7.0 %collective-permute-start.7 = (bf16[24,4096]{1,0:T(8,128)(2,1)S(1)}, bf16[24,4096]{1,0:T(8,128)(2,1)S(1)}, u32[]{:S(2)}, u32[]{:S(2)}) collective-permute-start(bf16[24,4096]{1,0:T(8,128)(2,1)S(1)} %join_cores.1), channel_id=1, source_target_pairs={{0,2},{1,3},{2,0},{3,1},{4,6},{5,7},{6,4},{7,5},{8,10},{9,11},{10,... | collective-permute-start | bytes 589832 | tf_op jit(solution)/shard_map/ppermute | solution.py:236

commit v7 on v5

--- a/solution.py
+++ b/solution.py
@@ -110,12 +110,13 @@
         a_lines[i * left_tiles:(i + lines_at_once) * left_tiles, :] = got.astype(BF16)
 
 
-def all_products(a_lines, b_ref, raw, prod, first):
+def all_products(a_lines, b_ref, raw, prod, first, first_line=0):
     right_tiles = b_ref.shape[0]
     left_tiles = a_lines.shape[0] // LINES
     for i in range(LINES):
         raw[i * right_tiles:(i + 1) * right_tiles, :] = b_ref[:, i * LANES:(i + 1) * LANES].astype(F32)
-    lines_at_once = min(LINES, max(1, ROWS_AT_ONCE // left_tiles))
+    lines = prod.shape[0]
+    lines_at_once = min(lines, max(1, ROWS_AT_ONCE // left_tiles))
     rows = lines_at_once * left_tiles
 
     def some_tiles(p):
@@ -128,7 +129,8 @@
         )
 
         def some(part):
-            at = part * rows if isinstance(part, int) else pl.multiple_of(part * rows, rows)
+            at = first_line * left_tiles + part * rows
+            at = at if isinstance(at, int) else pl.multiple_of(at, rows)
             got = jnp.dot(a_lines[pl.ds(at, rows), :], right, preferred_element_type=F32).astype(BF16)
             for j in range(lines_at_once):
                 for h in range(TILES_AT_ONCE):
@@ -138,13 +140,13 @@
                         j * left_tiles:(j + 1) * left_tiles, h * LANES:(h + 1) * LANES
                     ]
 
-        loop(LINES // lines_at_once, 1, some)
-
-    loop(right_tiles // TILES_AT_ONCE, 8 if rows == a_lines.shape[0] else 1, some_tiles)
+        loop(lines // lines_at_once, 1, some)
+
+    loop(right_tiles // TILES_AT_ONCE, 8 if lines == lines_at_once else 1, some_tiles)
 
 
 def chosen_sums(sel, first, count, prod, put):
-    for j in range(0, LINES, LINES_AT_ONCE):
+    for j in range(0, prod.shape[0], LINES_AT_ONCE):
         right = jnp.concatenate([prod[j + i, :count, :] for i in range(LINES_AT_ONCE)], axis=1)
         put(
             slice(j * LANES, (j + LINES_AT_ONCE) * LANES),
@@ -182,25 +184,31 @@
         start += done
 
 
-def last_kernel(start, sel, a_lines, acc, b_ref, own, far, cross, near, raw, prod):
+def last_kernel(start, first_line, sel, a_lines, acc, b_ref, own, far, sent, raw, prod):
     pairs = b_ref.shape[0] * a_lines.shape[0] // LINES
     owned = own.shape[0]
-    all_products(a_lines, b_ref, raw, prod, 0)
+    all_products(a_lines, b_ref, raw, prod, 0, first_line)
 
     def put(columns, value):
-        value = value + acc[:, columns]
-        for i, out in enumerate((own, far, cross, near)):
-            out[:, columns] = value[i * owned:(i + 1) * owned].astype(out.dtype)
+        value = value + acc[:, first_line * LANES + columns.start:first_line * LANES + columns.stop]
+        own[:, columns] = value[:owned]
+        far[:, columns] = value[owned:2 * owned]
+        sent[:, columns] = value[2 * owned:].astype(sent.dtype)
 
     chosen_sums(sel, start, pairs, prod, put)
 
 
 def join_kernel(far, arrived, out):
-    out[...] = (far[...] + arrived[...].astype(F32)).astype(out.dtype)
-
-
-def add_kernel(own, arrived, joined, out):
-    out[...] = (own[...] + arrived[...].astype(F32) + joined[...].astype(F32)).astype(out.dtype)
+    out[...] = (far[...] + arrived[:out.shape[0], :].astype(F32)).astype(out.dtype)
+
+
+def add_kernel(*refs):
+    out = refs[-1]
+    count, done = out.shape[0], 0
+    for own, arrived, joined in zip(refs[0:-1:3], refs[1:-1:3], refs[2:-1:3]):
+        total = own[...] + arrived[count:, :].astype(F32) + joined[...].astype(F32)
+        out[:, done:done + total.shape[1]] = total.astype(out.dtype)
+        done += total.shape[1]
 
 
 VMEM = pl.BlockSpec(memory_space=pltpu.VMEM)
@@ -282,24 +290,26 @@
         shard_flops,
         4 * MIB,
     )(sel, a_lines, acc, b_far)
-    own, far, cross, near = call(
-        functools.partial(last_kernel, 3 * pairs),
-        [shape((owned, FLAT), F32)] * 2 + [shape((owned, FLAT), BF16)] * 2,
-        [raw, one],
-        4,
-        "last_shard",
-        shard_flops,
-        4 * MIB,
-    )(sel, a_lines, acc, b_last)
-
-    arrived_cross = exchange(cross, "layer", 1)
-    arrived_near = exchange(near, "layer", 1)
-    (joined,) = call(
-        join_kernel, [shape((owned, FLAT), BF16)], [], 2, "join_cores", owned * FLAT, 1 * MIB
-    )(far, arrived_cross)
+    half, width = LINES // 2, FLAT // 2
+    results = []
+    for first_line in (0, half):
+        own, far, sent = call(
+            functools.partial(last_kernel, 3 * pairs, first_line),
+            [shape((owned, width), F32)] * 2 + [shape((2 * owned, width), BF16)],
+            [raw, shape((half, pairs, LANES), BF16)],
+            4,
+            "last_shard",
+            shard_flops // 2,
+            2 * MIB,
+        )(sel, a_lines, acc, b_last)
+        arrived = exchange(sent, "layer", 1)
+        (joined,) = call(
+            join_kernel, [shape((owned, width), BF16)], [], 2, "join_cores", owned * width, MIB
+        )(far, arrived)
+        results += [own, arrived, exchange(joined, "layer", 2)]
     (out,) = call(
-        add_kernel, [shape((owned, FLAT), BF16)], [], 3, "add_layers", 2 * owned * FLAT, 1 * MIB
-    )(own, arrived_near, exchange(joined, "layer", 2))
+        add_kernel, [shape((owned, FLAT), BF16)], [], len(results), "add_layers", 2 * owned * FLAT, MIB
+    )(*results)
     return out.reshape(1, 1, owned, FLAT)
 
 

time: 25.5 us -> 25.1 us (0.984)
  waiting for transfers between devices: 9.06 us -> 7.24 us
  starting transfers between devices: 9.55 us -> 10.6 us
  Pallas kernels: 5.75 us -> 6.18 us
    ppermute x7 -> x8, waiting for transfers between devices: 9.06 us -> 7.24 us  [exchange(): return lax.ppermute(x, axis, [(i, i ^ q) for i in range(size)])]
    ppermute x7 -> x8, starting transfers between devices: 9.55 us -> 10.6 us  [exchange(): return lax.ppermute(x, axis, [(i, i ^ q) for i in range(size)])]
    pallas_call x3 -> x5, Pallas kernels: 1.88 us -> 2.31 us  [the longest x2 1.54 us: shards(): call(functools.partial(last_kernel, 3 * pairs, first_line), [shape((owned...]
  transfers between devices with their start and end apart: 7 -> 8, of which waited for: 5 -> 6; matrix products, arithmetic and copies ran while one was open for 0% -> 0% of each run, Pallas kernels for 15% -> 19%
where the time goes in v7:
time: 25.1 us; the launch traced here: 25 us
  starting transfers between devices  10.6 us (42%)
  waiting for transfers between devices  7.24 us (29%)
  Pallas kernels  6.18 us (25%)
  local copies, waits for them, and re-layouts  0.91 us (4%)
    ppermute x8, starting transfers between devices, exchange(): return lax.ppermute(x, axis, [(i, i ^ q) for i in range(size)])  10.6 us
    ppermute x8, waiting for transfers between devices, exchange(): return lax.ppermute(x, axis, [(i, i ^ q) for i in range(size)])  7.24 us
    pallas_call x1, Pallas kernels, shards(): call(functools.partial(own_kernel, groups, len(a_parts)), [shape((tiles,...  2.01 us
    pallas_call x2, Pallas kernels, shards(): call(functools.partial(last_kernel, 3 * pairs, first_line), [shape((owned...  1.54 us
    pallas_call x1, Pallas kernels, shards(): call(functools.partial(more_kernel, 2 * pairs), [shape((tiles, FLAT), F32...  1.11 us
    unnamed x8, local copies, waits for them, and re-layouts  0.91 us
    pallas_call x1, Pallas kernels, shards(): call(add_kernel, [shape((owned, FLAT), BF16)], [], len(results), 'add_lay...  0.74 us
    pallas_call x1, Pallas kernels, shards(): call(functools.partial(counts_kernel, cols == 2, left_tiles, left_each, r...  0.73 us
  transfers between devices with their start and end apart: 8, of which 6 were waited for; matrix products, arithmetic and copies ran while one was open for 0% of the time, Pallas kernels for 19%

profile of v7, /device:TPU:0, one launch (start us, length us, event | category | flops | bytes accessed | tf_op | source)
XLA Modules:
  0.0 25.0 jit_solution(9073828299587195362)
XLA Ops:
  0.0 4.0 %collective-permute-start.2 = (bf16[16,4096]{1,0:T(8,128)(2,1)}, bf16[16,4096]{1,0:T(8,128)(2,1)S(1)}, u32[]{:S(2)}, u32[]{:S(2)}) collective-permute-start(bf16[16,4096]{1,0:T(8,128)(2,1)} %bitcast.7), channel_id=1, source_target_pairs={{0,16},{8,24},{16,0},{24,8},{1,17},{9,25},{17,1},{25,9},{2,18},{10... | collective-permute-start | bytes 393224 | tf_op jit(solution)/shard_map/ppermute | solution.py:237
  4.0 1.6 %collective-permute-start.1 = (bf16[16,4096]{1,0:T(8,128)(2,1)}, bf16[16,4096]{1,0:T(8,128)(2,1)S(1)}, u32[]{:S(2)}, u32[]{:S(2)}) collective-permute-start(bf16[16,4096]{1,0:T(8,128)(2,1)} %bitcast.8), channel_id=1, source_target_pairs={{0,8},{8,0},{16,24},{24,16},{1,9},{9,1},{17,25},{25,17},{2,10},{10... | collective-permute-start | bytes 393224 | tf_op jit(solution)/shard_map/ppermute | solution.py:237
  5.6 1.5 %collective-permute-start = (bf16[8,4096]{1,0:T(8,128)(2,1)}, bf16[8,4096]{1,0:T(8,128)(2,1)S(1)}, u32[]{:S(2)}, u32[]{:S(2)}) collective-permute-start(bf16[8,4096]{1,0:T(8,128)(2,1)} %bitcast.10), channel_id=1, source_target_pairs={{0,4},{4,0},{1,5},{5,1},{2,6},{6,2},{3,7},{7,3},{8,12},{12,8},{9,1... | collective-permute-start | bytes 196616 | tf_op jit(solution)/shard_map/ppermute | solution.py:237
  7.1 0.9 %copy-done.2 = bf16[1,1,1,16,4096]{4,3,2,1,0:T(8,128)(2,1)S(1)} copy-done((bf16[1,1,1,16,4096]{4,3,2,1,0:T(8,128)(2,1)S(1)}, bf16[1,1,1,16,4096]{4,3,2,1,0:T(8,128)(2,1)}, u32[]{:S(2)}) %copy-start.2) | copy-done | bytes 131096
  8.0 0.3 %collective-permute-start.3 = (bf16[16,4096]{1,0:T(8,128)(2,1)S(1)}, bf16[16,4096]{1,0:T(8,128)(2,1)S(1)}, u32[]{:S(2)}, u32[]{:S(2)}) collective-permute-start(bf16[16,4096]{1,0:T(8,128)(2,1)S(1)} %stage.1.refs_2_), channel_id=1, source_target_pairs={{0,24},{8,16},{16,8},{24,0},{1,25},{9,17},{17,9},{25,1},{2,26},{10... | collective-permute-start | bytes 393224 | tf_op jit(solution)/shard_map/ppermute | solution.py:237
  8.3 0.0 copy-done
  8.3 0.7 %counts.1.sel = bf16[96,1024]{1,0:T(8,128)(2,1)S(1)} custom-call(s32[1,768]{1,0:T(1,128)S(1)} %bitcast.5, s32[1,768]{1,0:T(1,128)S(1)} %bitcast.6), custom_call_target="tpu_custom_call" | custom-call | flops 1179648 | bytes 1048576 | tf_op jit(solution)/shard_map/counts/pallas_call | solution.py:261
  9.1 1.0 %collective-permute-done.refs_1_ = bf16[8,4096]{1,0:T(8,128)(2,1)S(1)} collective-permute-done((bf16[8,4096]{1,0:T(8,128)(2,1)}, bf16[8,4096]{1,0:T(8,128)(2,1)S(1)}, u32[]{:S(2)}, u32[]{:S(2)}) %collective-permute-start) | collective-permute-done | bytes 65568 | tf_op jit(solution)/shard_map/ppermute | solution.py:237
  10.1 1.0 %collective-permute-done.1.refs_3_ = bf16[16,4096]{1,0:T(8,128)(2,1)S(1)} collective-permute-done((bf16[16,4096]{1,0:T(8,128)(2,1)}, bf16[16,4096]{1,0:T(8,128)(2,1)S(1)}, u32[]{:S(2)}, u32[]{:S(2)}) %collective-permute-start.1) | collective-permute-done | bytes 131104 | tf_op jit(solution)/shard_map/ppermute | solution.py:237
  11.1 2.0 %own_and_near.1 = (f32[96,4096]{1,0:T(8,128)S(1)}, bf16[512,128]{1,0:T(8,128)(2,1)S(1)}) custom-call(bf16[96,1024]{1,0:T(8,128)(2,1)S(1)} %counts.1.sel, bf16[8,4096]{1,0:T(8,128)(2,1)S(1)} %bitcast.11, bf16[8,4096]{1,0:T(8,128)(2,1)S(1)} %collective-permute-done.refs_1_, bf16[16,4096]{1,0:T(8,128)(2,1)S(1)} %stage.1.refs_2_, ...), custom_call_target="tpu_custom_call" | custom-call | flops 939524096 | bytes 8388608 | tf_op jit(solution)/shard_map/own_and_near/pallas_call | solution.py:275
  13.1 0.0 collective-permute-done.2.b_ref
  13.1 1.1 %far_shard.1.acc = f32[96,4096]{1,0:T(8,128)S(1)} custom-call(bf16[96,1024]{1,0:T(8,128)(2,1)S(1)} %counts.1.sel, bf16[512,128]{1,0:T(8,128)(2,1)S(1)} %get-tuple-element.13.a_lines, f32[96,4096]{1,0:T(8,128)S(1)} %get-tuple-element.14.acc, bf16[16,4096]{1,0:T(8,128)(2,1)S(1)} %collective-permute-done.2.b_ref), custom_call_target="tpu_custom_call" | custom-call | flops 469762048 | bytes 4194304 | tf_op jit(solution)/shard_map/far_shard/pallas_call | solution.py:284
  14.2 0.7 %collective-permute-done.3.b_ref = bf16[16,4096]{1,0:T(8,128)(2,1)S(1)} collective-permute-done((bf16[16,4096]{1,0:T(8,128)(2,1)S(1)}, bf16[16,4096]{1,0:T(8,128)(2,1)S(1)}, u32[]{:S(2)}, u32[]{:S(2)}) %collective-permute-start.3) | collective-permute-done | bytes 131104 | tf_op jit(solution)/shard_map/ppermute | solution.py:237
  14.9 0.8 %last_shard.3 = (f32[24,2048]{1,0:T(8,128)S(1)}, f32[24,2048]{1,0:T(8,128)S(1)}, bf16[48,2048]{1,0:T(8,128)(2,1)S(1)}) custom-call(bf16[96,1024]{1,0:T(8,128)(2,1)S(1)} %counts.1.sel, bf16[512,128]{1,0:T(8,128)(2,1)S(1)} %get-tuple-element.13.a_lines, f32[96,4096]{1,0:T(8,128)S(1)} %far_shard.1.acc, bf16[16,4096]{1,0:T(8,128)(2,1)S(1)} %collective-permute-done.3.b_ref), custom_call_target="tpu_custom_call" | custom-call | flops 234881024 | bytes 2097152 | tf_op jit(solution)/shard_map/last_shard/pallas_call | solution.py:296
  15.7 0.1 collective-permute-start.6
  15.8 0.8 %last_shard.2 = (f32[24,2048]{1,0:T(8,128)S(1)}, f32[24,2048]{1,0:T(8,128)S(1)}, bf16[48,2048]{1,0:T(8,128)(2,1)S(1)}) custom-call(bf16[96,1024]{1,0:T(8,128)(2,1)S(1)} %counts.1.sel, bf16[512,128]{1,0:T(8,128)(2,1)S(1)} %get-tuple-element.13.a_lines, f32[96,4096]{1,0:T(8,128)S(1)} %far_shard.1.acc, bf16[16,4096]{1,0:T(8,128)(2,1)S(1)} %collective-permute-done.3.b_ref), custom_call_target="tpu_custom_call" | custom-call | flops 234881024 | bytes 2097152 | tf_op jit(solution)/shard_map/last_shard/pallas_call | solution.py:296
  16.5 0.6 %collective-permute-start.4 = (bf16[48,2048]{1,0:T(8,128)(2,1)S(1)}, bf16[48,2048]{1,0:T(8,128)(2,1)S(1)}, u32[]{:S(2)}, u32[]{:S(2)}) collective-permute-start(bf16[48,2048]{1,0:T(8,128)(2,1)S(1)} %get-tuple-element.16), channel_id=1, source_target_pairs={{0,1},{1,0},{2,3},{3,2},{4,5},{5,4},{6,7},{7,6},{8,9},{9,8},{10,11... | collective-permute-start | bytes 589832 | tf_op jit(solution)/shard_map/ppermute | solution.py:237
  17.1 0.1 collective-permute-done.6.arrived.refs_4_
  17.2 1.6 %collective-permute-start.7 = (bf16[24,2048]{1,0:T(8,128)(2,1)S(1)}, bf16[24,2048]{1,0:T(8,128)(2,1)S(1)}, u32[]{:S(2)}, u32[]{:S(2)}) collective-permute-start(bf16[24,2048]{1,0:T(8,128)(2,1)S(1)} %join_cores.3), channel_id=1, source_target_pairs={{0,2},{1,3},{2,0},{3,1},{4,6},{5,7},{6,4},{7,5},{8,10},{9,11},{10,... | collective-permute-start | bytes 294920 | tf_op jit(solution)/shard_map/ppermute | solution.py:237
  18.8 0.0 collective-permute-done.4.arrived.refs_1_
  18.8 1.0 %collective-permute-start.5 = (bf16[24,2048]{1,0:T(8,128)(2,1)S(1)}, bf16[24,2048]{1,0:T(8,128)(2,1)S(1)}, u32[]{:S(2)}, u32[]{:S(2)}) collective-permute-start(bf16[24,2048]{1,0:T(8,128)(2,1)S(1)} %join_cores.2), channel_id=1, source_target_pairs={{0,2},{1,3},{2,0},{3,1},{4,6},{5,7},{6,4},{7,5},{8,10},{9,11},{10,... | collective-permute-start | bytes 294920 | tf_op jit(solution)/shard_map/ppermute | solution.py:237
  19.8 3.1 %collective-permute-done.7.refs_5_ = bf16[24,2048]{1,0:T(8,128)(2,1)S(1)} collective-permute-done((bf16[24,2048]{1,0:T(8,128)(2,1)S(1)}, bf16[24,2048]{1,0:T(8,128)(2,1)S(1)}, u32[]{:S(2)}, u32[]{:S(2)}) %collective-permute-start.7) | collective-permute-done | bytes 98336 | tf_op jit(solution)/shard_map/ppermute | solution.py:237
  22.9 1.3 %collective-permute-done.5.refs_2_ = bf16[24,2048]{1,0:T(8,128)(2,1)S(1)} collective-permute-done((bf16[24,2048]{1,0:T(8,128)(2,1)S(1)}, bf16[24,2048]{1,0:T(8,128)(2,1)S(1)}, u32[]{:S(2)}, u32[]{:S(2)}) %collective-permute-start.5) | collective-permute-done | bytes 98336 | tf_op jit(solution)/shard_map/ppermute | solution.py:237
  24.2 0.7 %add_layers.1 = bf16[24,4096]{1,0:T(8,128)(2,1)} custom-call(f32[24,2048]{1,0:T(8,128)S(1)} %get-tuple-element.15.refs_0_, bf16[48,2048]{1,0:T(8,128)(2,1)S(1)} %collective-permute-done.4.arrived.refs_1_, bf16[24,2048]{1,0:T(8,128)(2,1)S(1)} %collective-permute-done.5.refs_2_, f32[24,2048]{1,0:T(8,128)S(1)} %get-tuple-element.18.refs_3_, ...), custom_call_target="tpu_custom_call" | custom-call | flops 196608 | bytes 1048576 | tf_op jit(solution)/shard_map/add_layers/pallas_call | solution.py:310
  (9 shorter events, 0.1 us)
Async XLA Ops:
  0.0 13.1 %collective-permute-start.2 = (bf16[16,4096]{1,0:T(8,128)(2,1)}, bf16[16,4096]{1,0:T(8,128)(2,1)S(1)}, u32[]{:S(2)}, u32[]{:S(2)}) collective-permute-start(bf16[16,4096]{1,0:T(8,128)(2,1)} %bitcast.7), channel_id=1, source_target_pairs={{0,16},{8,24},{16,0},{24,8},{1,17},{9,25},{17,1},{25,9},{2,18},{10... | collective-permute-start | bytes 393224 | tf_op jit(solution)/shard_map/ppermute | solution.py:237
  4.0 7.0 %collective-permute-start.1 = (bf16[16,4096]{1,0:T(8,128)(2,1)}, bf16[16,4096]{1,0:T(8,128)(2,1)S(1)}, u32[]{:S(2)}, u32[]{:S(2)}) collective-permute-start(bf16[16,4096]{1,0:T(8,128)(2,1)} %bitcast.8), channel_id=1, source_target_pairs={{0,8},{8,0},{16,24},{24,16},{1,9},{9,1},{17,25},{25,17},{2,10},{10... | collective-permute-start | bytes 393224 | tf_op jit(solution)/shard_map/ppermute | solution.py:237
  5.6 2.7 %copy-start = (s32[1,1,1,768]{3,2,1,0:T(1,128)S(1)}, s32[1,1,1,768]{3,2,1,0:T(1,128)}, u32[]{:S(2)}) copy-start(s32[1,1,1,768]{3,2,1,0:T(1,128)} %param.6) | copy-start | bytes 9220
  5.6 2.7 %copy-start.1 = (s32[1,1,1,768]{3,2,1,0:T(1,128)S(1)}, s32[1,1,1,768]{3,2,1,0:T(1,128)}, u32[]{:S(2)}) copy-start(s32[1,1,1,768]{3,2,1,0:T(1,128)} %param.7) | copy-start | bytes 9220
  5.6 4.5 %collective-permute-start = (bf16[8,4096]{1,0:T(8,128)(2,1)}, bf16[8,4096]{1,0:T(8,128)(2,1)S(1)}, u32[]{:S(2)}, u32[]{:S(2)}) collective-permute-start(bf16[8,4096]{1,0:T(8,128)(2,1)} %bitcast.10), channel_id=1, source_target_pairs={{0,4},{4,0},{1,5},{5,1},{2,6},{6,2},{3,7},{7,3},{8,12},{12,8},{9,1... | collective-permute-start | bytes 196616 | tf_op jit(solution)/shard_map/ppermute | solution.py:237
  7.1 0.9 %copy-start.2 = (bf16[1,1,1,16,4096]{4,3,2,1,0:T(8,128)(2,1)S(1)}, bf16[1,1,1,16,4096]{4,3,2,1,0:T(8,128)(2,1)}, u32[]{:S(2)}) copy-start(bf16[1,1,1,16,4096]{4,3,2,1,0:T(8,128)(2,1)} %param.5) | copy-start | bytes 393220
  8.0 3.1 %copy-start.3 = (bf16[1,1,1,8,4096]{4,3,2,1,0:T(8,128)(2,1)S(1)}, bf16[1,1,1,8,4096]{4,3,2,1,0:T(8,128)(2,1)}, u32[]{:S(2)}) copy-start(bf16[1,1,1,8,4096]{4,3,2,1,0:T(8,128)(2,1)} %param.4) | copy-start | bytes 196612
  8.0 6.9 %collective-permute-start.3 = (bf16[16,4096]{1,0:T(8,128)(2,1)S(1)}, bf16[16,4096]{1,0:T(8,128)(2,1)S(1)}, u32[]{:S(2)}, u32[]{:S(2)}) collective-permute-start(bf16[16,4096]{1,0:T(8,128)(2,1)S(1)} %stage.1.refs_2_), channel_id=1, source_target_pairs={{0,24},{8,16},{16,8},{24,0},{1,25},{9,17},{17,9},{25,1},{2,26},{10... | collective-permute-start | bytes 393224 | tf_op jit(solution)/shard_map/ppermute | solution.py:237
  15.7 1.5 %collective-permute-start.6 = (bf16[48,2048]{1,0:T(8,128)(2,1)S(1)}, bf16[48,2048]{1,0:T(8,128)(2,1)S(1)}, u32[]{:S(2)}, u32[]{:S(2)}) collective-permute-start(bf16[48,2048]{1,0:T(8,128)(2,1)S(1)} %get-tuple-element.19), channel_id=1, source_target_pairs={{0,1},{1,0},{2,3},{3,2},{4,5},{5,4},{6,7},{7,6},{8,9},{9,8},{10,11... | collective-permute-start | bytes 589832 | tf_op jit(solution)/shard_map/ppermute | solution.py:237
  16.5 2.3 %collective-permute-start.4 = (bf16[48,2048]{1,0:T(8,128)(2,1)S(1)}, bf16[48,2048]{1,0:T(8,128)(2,1)S(1)}, u32[]{:S(2)}, u32[]{:S(2)}) collective-permute-start(bf16[48,2048]{1,0:T(8,128)(2,1)S(1)} %get-tuple-element.16), channel_id=1, source_target_pairs={{0,1},{1,0},{2,3},{3,2},{4,5},{5,4},{6,7},{7,6},{8,9},{9,8},{10,11... | collective-permute-start | bytes 589832 | tf_op jit(solution)/shard_map/ppermute | solution.py:237
  17.2 5.7 %collective-permute-start.7 = (bf16[24,2048]{1,0:T(8,128)(2,1)S(1)}, bf16[24,2048]{1,0:T(8,128)(2,1)S(1)}, u32[]{:S(2)}, u32[]{:S(2)}) collective-permute-start(bf16[24,2048]{1,0:T(8,128)(2,1)S(1)} %join_cores.3), channel_id=1, source_target_pairs={{0,2},{1,3},{2,0},{3,1},{4,6},{5,7},{6,4},{7,5},{8,10},{9,11},{10,... | collective-permute-start | bytes 294920 | tf_op jit(solution)/shard_map/ppermute | solution.py:237
  18.8 5.4 %collective-permute-start.5 = (bf16[24,2048]{1,0:T(8,128)(2,1)S(1)}, bf16[24,2048]{1,0:T(8,128)(2,1)S(1)}, u32[]{:S(2)}, u32[]{:S(2)}) collective-permute-start(bf16[24,2048]{1,0:T(8,128)(2,1)S(1)} %join_cores.2), channel_id=1, source_target_pairs={{0,2},{1,3},{2,0},{3,1},{4,6},{5,7},{6,4},{7,5},{8,10},{9,11},{10,... | collective-permute-start | bytes 294920 | tf_op jit(solution)/shard_map/ppermute | solution.py:237

commit v8 on v7

--- a/solution.py
+++ b/solution.py
@@ -16,6 +16,7 @@
 TILES_AT_ONCE = 4
 LINES_AT_ONCE = 4
 MIB = 1 << 20
+OWN_FLOPS = 500 * 10**6
 STAGE_FLOPS = 2 * 10**9
 F32, BF16 = jnp.float32, jnp.bfloat16
 OWNER_ORDER = (0, 2, 3, 1)
@@ -257,7 +258,7 @@
         a_parts = [lax.all_gather(a_local, "col", axis=0, tiled=True)]
     (b_here,) = call(stage_kernel, [shape(b_local.shape, BF16)], [], 1, "stage", STAGE_FLOPS, MIB)(b_local)
     b_near = exchange(b_local, "row", 1)
-    b_last = exchange(b_here, "row", 3)
+    b_last = exchange(b_local, "row", 3)
     (sel,) = call(
         functools.partial(counts_kernel, cols == 2, left_tiles, left_each, right_each),
         [shape((tiles, rows * pairs), BF16)],
@@ -268,38 +269,38 @@
         MIB,
     )(a_index, b_index)
 
-    groups = (2,) if pairs * FLAT * 2 < 4 * MIB else (1, 1)
     raw = shape((right_each * LINES, LANES), F32)
     one = shape((LINES, pairs, LANES), BF16)
     shard_flops = 2 * pairs * LINES * LANES * LANES + 2 * pairs * tiles * FLAT
     acc, a_lines = call(
-        functools.partial(own_kernel, groups, len(a_parts)),
+        functools.partial(own_kernel, (1,), len(a_parts)),
         [shape((tiles, FLAT), F32), shape((left_tiles * LINES, LANES), BF16)],
-        [raw, shape((LINES, max(groups) * pairs, LANES), BF16)],
-        3 + len(a_parts),
-        "own_and_near",
-        2 * shard_flops,
-        8 * MIB,
-    )(sel, *a_parts, b_here, b_near)
-    (acc,) = call(
-        functools.partial(more_kernel, 2 * pairs),
-        [shape((tiles, FLAT), F32)],
         [raw, one],
-        4,
-        "far_shard",
-        shard_flops,
+        2 + len(a_parts),
+        "own_shard",
+        OWN_FLOPS,
         4 * MIB,
-    )(sel, a_lines, acc, b_far)
-    half, width = LINES // 2, FLAT // 2
+    )(sel, *a_parts, b_here)
+    for name, m, b_shard in (("far_shard", 2, b_far), ("near_shard", 1, b_near)):
+        (acc,) = call(
+            functools.partial(more_kernel, m * pairs),
+            [shape((tiles, FLAT), F32)],
+            [raw, one],
+            4,
+            name,
+            shard_flops,
+            4 * MIB,
+        )(sel, a_lines, acc, b_shard)
     results = []
-    for first_line in (0, half):
+    for first_line, lines in ((0, LINES // 4), (LINES // 4, 3 * LINES // 4)):
+        width = lines * LANES
         own, far, sent = call(
             functools.partial(last_kernel, 3 * pairs, first_line),
             [shape((owned, width), F32)] * 2 + [shape((2 * owned, width), BF16)],
-            [raw, shape((half, pairs, LANES), BF16)],
+            [raw, shape((lines, pairs, LANES), BF16)],
             4,
             "last_shard",
-            shard_flops // 2,
+            shard_flops * lines // LINES,
             2 * MIB,
         )(sel, a_lines, acc, b_last)
         arrived = exchange(sent, "layer", 1)

time: 25.1 us -> 25.4 us (1.012)
    pallas_call x2 -> x3, Pallas kernels: 3.13 us -> 3.37 us  [the longest x2 2.22 us: shards(): call(functools.partial(more_kernel, m * pairs), [shape((tiles, FLAT), F32...]
  transfers between devices with their start and end apart: 8 -> 8, of which waited for: 6 -> 5; matrix products, arithmetic and copies ran while one was open for 0% -> 0% of each run, Pallas kernels for 19% -> 19%
where the time goes in v8:
time: 25.4 us; the launch traced here: 25.3 us
  starting transfers between devices  10.6 us (42%)
  waiting for transfers between devices  7.27 us (29%)
  Pallas kernels  6.43 us (25%)
  local copies, waits for them, and re-layouts  0.91 us (4%)
    ppermute x8, starting transfers between devices, exchange(): return lax.ppermute(x, axis, [(i, i ^ q) for i in range(size)])  10.6 us
    ppermute x8, waiting for transfers between devices, exchange(): return lax.ppermute(x, axis, [(i, i ^ q) for i in range(size)])  7.27 us
    pallas_call x2, Pallas kernels, shards(): call(functools.partial(more_kernel, m * pairs), [shape((tiles, FLAT), F32...  2.22 us
    pallas_call x2, Pallas kernels, shards(): call(functools.partial(last_kernel, 3 * pairs, first_line), [shape((owned...  1.55 us
    pallas_call x1, Pallas kernels, shards(): call(functools.partial(own_kernel, (1,), len(a_parts)), [shape((tiles, FL...  1.15 us
    unnamed x8, local copies, waits for them, and re-layouts  0.91 us
    pallas_call x1, Pallas kernels, shards(): call(add_kernel, [shape((owned, FLAT), BF16)], [], len(results), 'add_lay...  0.74 us
    pallas_call x1, Pallas kernels, shards(): call(functools.partial(counts_kernel, cols == 2, left_tiles, left_each, r...  0.73 us
  transfers between devices with their start and end apart: 8, of which 5 were waited for; matrix products, arithmetic and copies ran while one was open for 0% of the time, Pallas kernels for 19%

profile of v8, /device:TPU:0, one launch (start us, length us, event | category | flops | bytes accessed | tf_op | source)
XLA Modules:
  0.0 25.3 jit_solution(4963661200632919553)
XLA Ops:
  0.0 4.0 %collective-permute-start.1 = (bf16[16,4096]{1,0:T(8,128)(2,1)}, bf16[16,4096]{1,0:T(8,128)(2,1)S(1)}, u32[]{:S(2)}, u32[]{:S(2)}) collective-permute-start(bf16[16,4096]{1,0:T(8,128)(2,1)} %bitcast.7), channel_id=1, source_target_pairs={{0,16},{8,24},{16,0},{24,8},{1,17},{9,25},{17,1},{25,9},{2,18},{10... | collective-permute-start | bytes 393224 | tf_op jit(solution)/shard_map/ppermute | solution.py:238
  4.0 1.6 %collective-permute-start.2 = (bf16[16,4096]{1,0:T(8,128)(2,1)}, bf16[16,4096]{1,0:T(8,128)(2,1)S(1)}, u32[]{:S(2)}, u32[]{:S(2)}) collective-permute-start(bf16[16,4096]{1,0:T(8,128)(2,1)} %bitcast.8), channel_id=1, source_target_pairs={{0,8},{8,0},{16,24},{24,16},{1,9},{9,1},{17,25},{25,17},{2,10},{10... | collective-permute-start | bytes 393224 | tf_op jit(solution)/shard_map/ppermute | solution.py:238
  5.6 0.0 collective-permute-start.3
  5.6 1.7 %collective-permute-start = (bf16[8,4096]{1,0:T(8,128)(2,1)}, bf16[8,4096]{1,0:T(8,128)(2,1)S(1)}, u32[]{:S(2)}, u32[]{:S(2)}) collective-permute-start(bf16[8,4096]{1,0:T(8,128)(2,1)} %bitcast.11), channel_id=1, source_target_pairs={{0,4},{4,0},{1,5},{5,1},{2,6},{6,2},{3,7},{7,3},{8,12},{12,8},{9,1... | collective-permute-start | bytes 196616 | tf_op jit(solution)/shard_map/ppermute | solution.py:238
  7.3 0.9 %copy-done.2 = bf16[1,1,1,16,4096]{4,3,2,1,0:T(8,128)(2,1)S(1)} copy-done((bf16[1,1,1,16,4096]{4,3,2,1,0:T(8,128)(2,1)S(1)}, bf16[1,1,1,16,4096]{4,3,2,1,0:T(8,128)(2,1)}, u32[]{:S(2)}) %copy-start.2) | copy-done | bytes 131096
  8.3 0.7 %counts.1.sel = bf16[96,1024]{1,0:T(8,128)(2,1)S(1)} custom-call(s32[1,768]{1,0:T(1,128)S(1)} %bitcast.5, s32[1,768]{1,0:T(1,128)S(1)} %bitcast.6), custom_call_target="tpu_custom_call" | custom-call | flops 1179648 | bytes 1048576 | tf_op jit(solution)/shard_map/counts/pallas_call | solution.py:262
  9.0 1.1 %collective-permute-done.refs_1_ = bf16[8,4096]{1,0:T(8,128)(2,1)S(1)} collective-permute-done((bf16[8,4096]{1,0:T(8,128)(2,1)}, bf16[8,4096]{1,0:T(8,128)(2,1)S(1)}, u32[]{:S(2)}, u32[]{:S(2)}) %collective-permute-start) | collective-permute-done | bytes 65568 | tf_op jit(solution)/shard_map/ppermute | solution.py:238
  10.1 1.2 %own_shard.1 = (f32[96,4096]{1,0:T(8,128)S(1)}, bf16[512,128]{1,0:T(8,128)(2,1)S(1)}) custom-call(bf16[96,1024]{1,0:T(8,128)(2,1)S(1)} %counts.1.sel, bf16[8,4096]{1,0:T(8,128)(2,1)S(1)} %bitcast.12, bf16[8,4096]{1,0:T(8,128)(2,1)S(1)} %collective-permute-done.refs_1_, bf16[16,4096]{1,0:T(8,128)(2,1)S(1)} %stage.1.refs_2_), custom_call_target="tpu_custom_call" | custom-call | flops 500000000 | bytes 4194304 | tf_op jit(solution)/shard_map/own_shard/pallas_call | solution.py:275
  11.3 0.9 %collective-permute-done.1.b_ref = bf16[16,4096]{1,0:T(8,128)(2,1)S(1)} collective-permute-done((bf16[16,4096]{1,0:T(8,128)(2,1)}, bf16[16,4096]{1,0:T(8,128)(2,1)S(1)}, u32[]{:S(2)}, u32[]{:S(2)}) %collective-permute-start.1) | collective-permute-done | bytes 131104 | tf_op jit(solution)/shard_map/ppermute | solution.py:238
  12.2 1.1 %far_shard.1.acc = f32[96,4096]{1,0:T(8,128)S(1)} custom-call(bf16[96,1024]{1,0:T(8,128)(2,1)S(1)} %counts.1.sel, bf16[512,128]{1,0:T(8,128)(2,1)S(1)} %get-tuple-element.13.a_lines, f32[96,4096]{1,0:T(8,128)S(1)} %get-tuple-element.14.acc, bf16[16,4096]{1,0:T(8,128)(2,1)S(1)} %collective-permute-done.1.b_ref), custom_call_target="tpu_custom_call" | custom-call | flops 469762048 | bytes 4194304 | tf_op jit(solution)/shard_map/far_shard/pallas_call | solution.py:285
  13.3 0.0 collective-permute-done.2.b_ref
  13.3 1.1 %near_shard.1.acc = f32[96,4096]{1,0:T(8,128)S(1)} custom-call(bf16[96,1024]{1,0:T(8,128)(2,1)S(1)} %counts.1.sel, bf16[512,128]{1,0:T(8,128)(2,1)S(1)} %get-tuple-element.13.a_lines, f32[96,4096]{1,0:T(8,128)S(1)} %far_shard.1.acc, bf16[16,4096]{1,0:T(8,128)(2,1)S(1)} %collective-permute-done.2.b_ref), custom_call_target="tpu_custom_call" | custom-call | flops 469762048 | bytes 4194304 | tf_op jit(solution)/shard_map/near_shard/pallas_call | solution.py:285
  14.4 0.1 collective-permute-done.3.b_ref
  14.6 1.0 %last_shard.3 = (f32[24,3072]{1,0:T(8,128)S(1)}, f32[24,3072]{1,0:T(8,128)S(1)}, bf16[48,3072]{1,0:T(8,128)(2,1)S(1)}) custom-call(bf16[96,1024]{1,0:T(8,128)(2,1)S(1)} %counts.1.sel, bf16[512,128]{1,0:T(8,128)(2,1)S(1)} %get-tuple-element.13.a_lines, f32[96,4096]{1,0:T(8,128)S(1)} %near_shard.1.acc, bf16[16,4096]{1,0:T(8,128)(2,1)S(1)} %collective-permute-done.3.b_ref), custom_call_target="tpu_custom_call" | custom-call | flops 352321536 | bytes 2097152 | tf_op jit(solution)/shard_map/last_shard/pallas_call | solution.py:297
  15.5 0.1 collective-permute-start.6
  15.6 0.6 %last_shard.2 = (f32[24,1024]{1,0:T(8,128)S(1)}, f32[24,1024]{1,0:T(8,128)S(1)}, bf16[48,1024]{1,0:T(8,128)(2,1)S(1)}) custom-call(bf16[96,1024]{1,0:T(8,128)(2,1)S(1)} %counts.1.sel, bf16[512,128]{1,0:T(8,128)(2,1)S(1)} %get-tuple-element.13.a_lines, f32[96,4096]{1,0:T(8,128)S(1)} %near_shard.1.acc, bf16[16,4096]{1,0:T(8,128)(2,1)S(1)} %collective-permute-done.3.b_ref), custom_call_target="tpu_custom_call" | custom-call | flops 117440512 | bytes 2097152 | tf_op jit(solution)/shard_map/last_shard/pallas_call | solution.py:297
  16.2 0.6 %collective-permute-start.4 = (bf16[48,1024]{1,0:T(8,128)(2,1)S(1)}, bf16[48,1024]{1,0:T(8,128)(2,1)S(1)}, u32[]{:S(2)}, u32[]{:S(2)}) collective-permute-start(bf16[48,1024]{1,0:T(8,128)(2,1)S(1)} %get-tuple-element.16), channel_id=1, source_target_pairs={{0,1},{1,0},{2,3},{3,2},{4,5},{5,4},{6,7},{7,6},{8,9},{9,8},{10,11... | collective-permute-start | bytes 294920 | tf_op jit(solution)/shard_map/ppermute | solution.py:238
  16.8 0.4 %collective-permute-done.6.arrived.refs_4_ = bf16[48,3072]{1,0:T(8,128)(2,1)S(1)} collective-permute-done((bf16[48,3072]{1,0:T(8,128)(2,1)S(1)}, bf16[48,3072]{1,0:T(8,128)(2,1)S(1)}, u32[]{:S(2)}, u32[]{:S(2)}) %collective-permute-start.6) | collective-permute-done | bytes 294944 | tf_op jit(solution)/shard_map/ppermute | solution.py:238
  17.2 2.1 %collective-permute-start.7 = (bf16[24,3072]{1,0:T(8,128)(2,1)S(1)}, bf16[24,3072]{1,0:T(8,128)(2,1)S(1)}, u32[]{:S(2)}, u32[]{:S(2)}) collective-permute-start(bf16[24,3072]{1,0:T(8,128)(2,1)S(1)} %join_cores.3), channel_id=1, source_target_pairs={{0,2},{1,3},{2,0},{3,1},{4,6},{5,7},{6,4},{7,5},{8,10},{9,11},{10,... | collective-permute-start | bytes 442376 | tf_op jit(solution)/shard_map/ppermute | solution.py:238
  19.3 0.0 collective-permute-done.4.arrived.refs_1_
  19.3 0.5 %collective-permute-start.5 = (bf16[24,1024]{1,0:T(8,128)(2,1)S(1)}, bf16[24,1024]{1,0:T(8,128)(2,1)S(1)}, u32[]{:S(2)}, u32[]{:S(2)}) collective-permute-start(bf16[24,1024]{1,0:T(8,128)(2,1)S(1)} %join_cores.2), channel_id=1, source_target_pairs={{0,2},{1,3},{2,0},{3,1},{4,6},{5,7},{6,4},{7,5},{8,10},{9,11},{10,... | collective-permute-start | bytes 147464 | tf_op jit(solution)/shard_map/ppermute | solution.py:238
  19.8 4.7 %collective-permute-done.5.refs_2_ = bf16[24,1024]{1,0:T(8,128)(2,1)S(1)} collective-permute-done((bf16[24,1024]{1,0:T(8,128)(2,1)S(1)}, bf16[24,1024]{1,0:T(8,128)(2,1)S(1)}, u32[]{:S(2)}, u32[]{:S(2)}) %collective-permute-start.5) | collective-permute-done | bytes 49184 | tf_op jit(solution)/shard_map/ppermute | solution.py:238
  24.5 0.0 collective-permute-done.7.refs_5_
  24.5 0.7 %add_layers.1 = bf16[24,4096]{1,0:T(8,128)(2,1)} custom-call(f32[24,1024]{1,0:T(8,128)S(1)} %get-tuple-element.15.refs_0_, bf16[48,1024]{1,0:T(8,128)(2,1)S(1)} %collective-permute-done.4.arrived.refs_1_, bf16[24,1024]{1,0:T(8,128)(2,1)S(1)} %collective-permute-done.5.refs_2_, f32[24,3072]{1,0:T(8,128)S(1)} %get-tuple-element.18.refs_3_, ...), custom_call_target="tpu_custom_call" | custom-call | flops 196608 | bytes 1048576 | tf_op jit(solution)/shard_map/add_layers/pallas_call | solution.py:311
  (10 shorter events, 0.1 us)
Async XLA Ops:
  0.0 12.2 %collective-permute-start.1 = (bf16[16,4096]{1,0:T(8,128)(2,1)}, bf16[16,4096]{1,0:T(8,128)(2,1)S(1)}, u32[]{:S(2)}, u32[]{:S(2)}) collective-permute-start(bf16[16,4096]{1,0:T(8,128)(2,1)} %bitcast.7), channel_id=1, source_target_pairs={{0,16},{8,24},{16,0},{24,8},{1,17},{9,25},{17,1},{25,9},{2,18},{10... | collective-permute-start | bytes 393224 | tf_op jit(solution)/shard_map/ppermute | solution.py:238
  4.0 9.3 %collective-permute-start.2 = (bf16[16,4096]{1,0:T(8,128)(2,1)}, bf16[16,4096]{1,0:T(8,128)(2,1)S(1)}, u32[]{:S(2)}, u32[]{:S(2)}) collective-permute-start(bf16[16,4096]{1,0:T(8,128)(2,1)} %bitcast.8), channel_id=1, source_target_pairs={{0,8},{8,0},{16,24},{24,16},{1,9},{9,1},{17,25},{25,17},{2,10},{10... | collective-permute-start | bytes 393224 | tf_op jit(solution)/shard_map/ppermute | solution.py:238
  5.6 9.0 %collective-permute-start.3 = (bf16[16,4096]{1,0:T(8,128)(2,1)}, bf16[16,4096]{1,0:T(8,128)(2,1)S(1)}, u32[]{:S(2)}, u32[]{:S(2)}) collective-permute-start(bf16[16,4096]{1,0:T(8,128)(2,1)} %bitcast.9), channel_id=1, source_target_pairs={{0,24},{8,16},{16,8},{24,0},{1,25},{9,17},{17,9},{25,1},{2,26},{10... | collective-permute-start | bytes 393224 | tf_op jit(solution)/shard_map/ppermute | solution.py:238
  5.6 2.6 %copy-start = (s32[1,1,1,768]{3,2,1,0:T(1,128)S(1)}, s32[1,1,1,768]{3,2,1,0:T(1,128)}, u32[]{:S(2)}) copy-start(s32[1,1,1,768]{3,2,1,0:T(1,128)} %param.6) | copy-start | bytes 9220
  5.6 2.6 %copy-start.1 = (s32[1,1,1,768]{3,2,1,0:T(1,128)S(1)}, s32[1,1,1,768]{3,2,1,0:T(1,128)}, u32[]{:S(2)}) copy-start(s32[1,1,1,768]{3,2,1,0:T(1,128)} %param.7) | copy-start | bytes 9220
  5.6 4.5 %collective-permute-start = (bf16[8,4096]{1,0:T(8,128)(2,1)}, bf16[8,4096]{1,0:T(8,128)(2,1)S(1)}, u32[]{:S(2)}, u32[]{:S(2)}) collective-permute-start(bf16[8,4096]{1,0:T(8,128)(2,1)} %bitcast.11), channel_id=1, source_target_pairs={{0,4},{4,0},{1,5},{5,1},{2,6},{6,2},{3,7},{7,3},{8,12},{12,8},{9,1... | collective-permute-start | bytes 196616 | tf_op jit(solution)/shard_map/ppermute | solution.py:238
  7.3 0.9 %copy-start.2 = (bf16[1,1,1,16,4096]{4,3,2,1,0:T(8,128)(2,1)S(1)}, bf16[1,1,1,16,4096]{4,3,2,1,0:T(8,128)(2,1)}, u32[]{:S(2)}) copy-start(bf16[1,1,1,16,4096]{4,3,2,1,0:T(8,128)(2,1)} %param.5) | copy-start | bytes 393220
  8.2 1.9 %copy-start.3 = (bf16[1,1,1,8,4096]{4,3,2,1,0:T(8,128)(2,1)S(1)}, bf16[1,1,1,8,4096]{4,3,2,1,0:T(8,128)(2,1)}, u32[]{:S(2)}) copy-start(bf16[1,1,1,8,4096]{4,3,2,1,0:T(8,128)(2,1)} %param.4) | copy-start | bytes 196612
  15.5 1.6 %collective-permute-start.6 = (bf16[48,3072]{1,0:T(8,128)(2,1)S(1)}, bf16[48,3072]{1,0:T(8,128)(2,1)S(1)}, u32[]{:S(2)}, u32[]{:S(2)}) collective-permute-start(bf16[48,3072]{1,0:T(8,128)(2,1)S(1)} %get-tuple-element.19), channel_id=1, source_target_pairs={{0,1},{1,0},{2,3},{3,2},{4,5},{5,4},{6,7},{7,6},{8,9},{9,8},{10,11... | collective-permute-start | bytes 884744 | tf_op jit(solution)/shard_map/ppermute | solution.py:238
  16.2 3.1 %collective-permute-start.4 = (bf16[48,1024]{1,0:T(8,128)(2,1)S(1)}, bf16[48,1024]{1,0:T(8,128)(2,1)S(1)}, u32[]{:S(2)}, u32[]{:S(2)}) collective-permute-start(bf16[48,1024]{1,0:T(8,128)(2,1)S(1)} %get-tuple-element.16), channel_id=1, source_target_pairs={{0,1},{1,0},{2,3},{3,2},{4,5},{5,4},{6,7},{7,6},{8,9},{9,8},{10,11... | collective-permute-start | bytes 294920 | tf_op jit(solution)/shard_map/ppermute | solution.py:238
  17.2 7.3 %collective-permute-start.7 = (bf16[24,3072]{1,0:T(8,128)(2,1)S(1)}, bf16[24,3072]{1,0:T(8,128)(2,1)S(1)}, u32[]{:S(2)}, u32[]{:S(2)}) collective-permute-start(bf16[24,3072]{1,0:T(8,128)(2,1)S(1)} %join_cores.3), channel_id=1, source_target_pairs={{0,2},{1,3},{2,0},{3,1},{4,6},{5,7},{6,4},{7,5},{8,10},{9,11},{10,... | collective-permute-start | bytes 442376 | tf_op jit(solution)/shard_map/ppermute | solution.py:238
  19.3 5.2 %collective-permute-start.5 = (bf16[24,1024]{1,0:T(8,128)(2,1)S(1)}, bf16[24,1024]{1,0:T(8,128)(2,1)S(1)}, u32[]{:S(2)}, u32[]{:S(2)}) collective-permute-start(bf16[24,1024]{1,0:T(8,128)(2,1)S(1)} %join_cores.2), channel_id=1, source_target_pairs={{0,2},{1,3},{2,0},{3,1},{4,6},{5,7},{6,4},{7,5},{8,10},{9,11},{10,... | collective-permute-start | bytes 147464 | tf_op jit(solution)/shard_map/ppermute | solution.py:238

commit v9 on v8

--- a/solution.py
+++ b/solution.py
@@ -13,6 +13,7 @@
 LANES = 128
 LINES = FLAT // LANES
 ROWS_AT_ONCE = 512
+FIRST_LINES = LINES // 2
 TILES_AT_ONCE = 4
 LINES_AT_ONCE = 4
 MIB = 1 << 20
@@ -111,23 +112,31 @@
         a_lines[i * left_tiles:(i + lines_at_once) * left_tiles, :] = got.astype(BF16)
 
 
-def all_products(a_lines, b_ref, raw, prod, first, first_line=0):
+def all_products(a_lines, b_ref, raw, prod, first, first_line=0, rights=None):
     right_tiles = b_ref.shape[0]
     left_tiles = a_lines.shape[0] // LINES
-    for i in range(LINES):
+    for i in range(LINES if raw is not None else 0):
         raw[i * right_tiles:(i + 1) * right_tiles, :] = b_ref[:, i * LANES:(i + 1) * LANES].astype(F32)
     lines = prod.shape[0]
     lines_at_once = min(lines, max(1, ROWS_AT_ONCE // left_tiles))
     rows = lines_at_once * left_tiles
 
     def some_tiles(p):
-        right = jnp.concatenate(
-            [
-                twice_on_diagonal(raw[pl.ds(p * TILES_AT_ONCE + h, LINES, stride=right_tiles), :])
-                for h in range(TILES_AT_ONCE)
-            ],
-            axis=1,
-        )
+        columns = p * TILES_AT_ONCE * LANES
+        columns = columns if isinstance(columns, int) else pl.multiple_of(columns, TILES_AT_ONCE * LANES)
+        columns = pl.ds(columns, TILES_AT_ONCE * LANES)
+        if raw is None:
+            right = rights[:, columns]
+        else:
+            right = jnp.concatenate(
+                [
+                    twice_on_diagonal(raw[pl.ds(p * TILES_AT_ONCE + h, LINES, stride=right_tiles), :])
+                    for h in range(TILES_AT_ONCE)
+                ],
+                axis=1,
+            )
+            if rights is not None:
+                rights[:, columns] = right
 
         def some(part):
             at = first_line * left_tiles + part * rows
@@ -185,10 +194,14 @@
         start += done
 
 
-def last_kernel(start, first_line, sel, a_lines, acc, b_ref, own, far, sent, raw, prod):
+def last_kernel(start, first_line, sel, a_lines, acc, b_ref, *refs):
+    if first_line:
+        (rights, own, far, sent, prod), raw = refs, None
+    else:
+        own, far, sent, rights, raw, prod = refs
     pairs = b_ref.shape[0] * a_lines.shape[0] // LINES
     owned = own.shape[0]
-    all_products(a_lines, b_ref, raw, prod, 0, first_line)
+    all_products(a_lines, b_ref, raw, prod, 0, first_line, rights)
 
     def put(columns, value):
         value = value + acc[:, first_line * LANES + columns.start:first_line * LANES + columns.stop]
@@ -291,18 +304,22 @@
             shard_flops,
             4 * MIB,
         )(sel, a_lines, acc, b_shard)
-    results = []
-    for first_line, lines in ((0, LINES // 4), (LINES // 4, 3 * LINES // 4)):
+    results, kept = [], []
+    for first_line, lines in ((0, FIRST_LINES), (FIRST_LINES, LINES - FIRST_LINES)):
         width = lines * LANES
-        own, far, sent = call(
+        outs = [shape((owned, width), F32)] * 2 + [shape((2 * owned, width), BF16)]
+        if not kept:
+            outs += [shape((LANES, right_each * LANES), BF16)]
+        own, far, sent, *made = call(
             functools.partial(last_kernel, 3 * pairs, first_line),
-            [shape((owned, width), F32)] * 2 + [shape((2 * owned, width), BF16)],
-            [raw, shape((lines, pairs, LANES), BF16)],
-            4,
+            outs,
+            ([] if kept else [raw]) + [shape((lines, pairs, LANES), BF16)],
+            4 + len(kept),
             "last_shard",
             shard_flops * lines // LINES,
             2 * MIB,
-        )(sel, a_lines, acc, b_last)
+        )(sel, a_lines, acc, b_last, *kept)
+        kept = kept or made
         arrived = exchange(sent, "layer", 1)
         (joined,) = call(
             join_kernel, [shape((owned, width), BF16)], [], 2, "join_cores", owned * width, MIB

time: 25.4 us -> 25.1 us (0.988)
  waiting for transfers between devices: 7.27 us -> 6.71 us
  starting transfers between devices: 10.6 us -> 10.9 us
    ppermute x8, waiting for transfers between devices: 7.27 us -> 6.71 us  [exchange(): return lax.ppermute(x, axis, [(i, i ^ q) for i in range(size)])]
    ppermute x8, starting transfers between devices: 10.6 us -> 10.9 us  [exchange(): return lax.ppermute(x, axis, [(i, i ^ q) for i in range(size)])]
  transfers between devices with their start and end apart: 8 -> 8, of which waited for: 5 -> 6; matrix products, arithmetic and copies ran while one was open for 0% -> 0% of each run, Pallas kernels for 19% -> 19%
where the time goes in v9:
time: 25.1 us; the launch traced here: 24.9 us
  starting transfers between devices  10.9 us (43%)
  waiting for transfers between devices  6.71 us (27%)
  Pallas kernels  6.32 us (25%)
  local copies, waits for them, and re-layouts  0.91 us (4%)
    ppermute x8, starting transfers between devices, exchange(): return lax.ppermute(x, axis, [(i, i ^ q) for i in range(size)])  10.9 us
    ppermute x8, waiting for transfers between devices, exchange(): return lax.ppermute(x, axis, [(i, i ^ q) for i in range(size)])  6.71 us
    pallas_call x2, Pallas kernels, shards(): call(functools.partial(more_kernel, m * pairs), [shape((tiles, FLAT), F32...  2.22 us
    pallas_call x2, Pallas kernels, shards(): call(functools.partial(last_kernel, 3 * pairs, first_line), outs, ([] if...  1.43 us
    pallas_call x1, Pallas kernels, shards(): call(functools.partial(own_kernel, (1,), len(a_parts)), [shape((tiles, FL...  1.15 us
    unnamed x8, local copies, waits for them, and re-layouts  0.91 us
    pallas_call x1, Pallas kernels, shards(): call(add_kernel, [shape((owned, FLAT), BF16)], [], len(results), 'add_lay...  0.74 us
    pallas_call x1, Pallas kernels, shards(): call(functools.partial(counts_kernel, cols == 2, left_tiles, left_each, r...  0.73 us
  transfers between devices with their start and end apart: 8, of which 6 were waited for; matrix products, arithmetic and copies ran while one was open for 0% of the time, Pallas kernels for 19%

profile of v9, /device:TPU:0, one launch (start us, length us, event | category | flops | bytes accessed | tf_op | source)
XLA Modules:
  0.0 24.9 jit_solution(9427506170715370858)
XLA Ops:
  0.0 4.0 %collective-permute-start.1 = (bf16[16,4096]{1,0:T(8,128)(2,1)}, bf16[16,4096]{1,0:T(8,128)(2,1)S(1)}, u32[]{:S(2)}, u32[]{:S(2)}) collective-permute-start(bf16[16,4096]{1,0:T(8,128)(2,1)} %bitcast.7), channel_id=1, source_target_pairs={{0,16},{8,24},{16,0},{24,8},{1,17},{9,25},{17,1},{25,9},{2,18},{10... | collective-permute-start | bytes 393224 | tf_op jit(solution)/shard_map/ppermute | solution.py:251
  4.0 1.6 %collective-permute-start.2 = (bf16[16,4096]{1,0:T(8,128)(2,1)}, bf16[16,4096]{1,0:T(8,128)(2,1)S(1)}, u32[]{:S(2)}, u32[]{:S(2)}) collective-permute-start(bf16[16,4096]{1,0:T(8,128)(2,1)} %bitcast.8), channel_id=1, source_target_pairs={{0,8},{8,0},{16,24},{24,16},{1,9},{9,1},{17,25},{25,17},{2,10},{10... | collective-permute-start | bytes 393224 | tf_op jit(solution)/shard_map/ppermute | solution.py:251
  5.6 0.0 collective-permute-start.3
  5.6 1.7 %collective-permute-start = (bf16[8,4096]{1,0:T(8,128)(2,1)}, bf16[8,4096]{1,0:T(8,128)(2,1)S(1)}, u32[]{:S(2)}, u32[]{:S(2)}) collective-permute-start(bf16[8,4096]{1,0:T(8,128)(2,1)} %bitcast.11), channel_id=1, source_target_pairs={{0,4},{4,0},{1,5},{5,1},{2,6},{6,2},{3,7},{7,3},{8,12},{12,8},{9,1... | collective-permute-start | bytes 196616 | tf_op jit(solution)/shard_map/ppermute | solution.py:251
  7.3 0.9 %copy-done.2 = bf16[1,1,1,16,4096]{4,3,2,1,0:T(8,128)(2,1)S(1)} copy-done((bf16[1,1,1,16,4096]{4,3,2,1,0:T(8,128)(2,1)S(1)}, bf16[1,1,1,16,4096]{4,3,2,1,0:T(8,128)(2,1)}, u32[]{:S(2)}) %copy-start.2) | copy-done | bytes 131096
  8.3 0.7 %counts.1.sel = bf16[96,1024]{1,0:T(8,128)(2,1)S(1)} custom-call(s32[1,768]{1,0:T(1,128)S(1)} %bitcast.5, s32[1,768]{1,0:T(1,128)S(1)} %bitcast.6), custom_call_target="tpu_custom_call" | custom-call | flops 1179648 | bytes 1048576 | tf_op jit(solution)/shard_map/counts/pallas_call | solution.py:275
  9.0 1.1 %collective-permute-done.refs_1_ = bf16[8,4096]{1,0:T(8,128)(2,1)S(1)} collective-permute-done((bf16[8,4096]{1,0:T(8,128)(2,1)}, bf16[8,4096]{1,0:T(8,128)(2,1)S(1)}, u32[]{:S(2)}, u32[]{:S(2)}) %collective-permute-start) | collective-permute-done | bytes 65568 | tf_op jit(solution)/shard_map/ppermute | solution.py:251
  10.1 1.2 %own_shard.1 = (f32[96,4096]{1,0:T(8,128)S(1)}, bf16[512,128]{1,0:T(8,128)(2,1)S(1)}) custom-call(bf16[96,1024]{1,0:T(8,128)(2,1)S(1)} %counts.1.sel, bf16[8,4096]{1,0:T(8,128)(2,1)S(1)} %bitcast.12, bf16[8,4096]{1,0:T(8,128)(2,1)S(1)} %collective-permute-done.refs_1_, bf16[16,4096]{1,0:T(8,128)(2,1)S(1)} %stage.1.refs_2_), custom_call_target="tpu_custom_call" | custom-call | flops 500000000 | bytes 4194304 | tf_op jit(solution)/shard_map/own_shard/pallas_call | solution.py:288
  11.3 0.9 %collective-permute-done.1.b_ref = bf16[16,4096]{1,0:T(8,128)(2,1)S(1)} collective-permute-done((bf16[16,4096]{1,0:T(8,128)(2,1)}, bf16[16,4096]{1,0:T(8,128)(2,1)S(1)}, u32[]{:S(2)}, u32[]{:S(2)}) %collective-permute-start.1) | collective-permute-done | bytes 131104 | tf_op jit(solution)/shard_map/ppermute | solution.py:251
  12.2 1.1 %far_shard.1.acc = f32[96,4096]{1,0:T(8,128)S(1)} custom-call(bf16[96,1024]{1,0:T(8,128)(2,1)S(1)} %counts.1.sel, bf16[512,128]{1,0:T(8,128)(2,1)S(1)} %get-tuple-element.14.a_lines, f32[96,4096]{1,0:T(8,128)S(1)} %get-tuple-element.15.acc, bf16[16,4096]{1,0:T(8,128)(2,1)S(1)} %collective-permute-done.1.b_ref), custom_call_target="tpu_custom_call" | custom-call | flops 469762048 | bytes 4194304 | tf_op jit(solution)/shard_map/far_shard/pallas_call | solution.py:298
  13.3 0.0 collective-permute-done.2.b_ref
  13.3 1.1 %near_shard.1.acc = f32[96,4096]{1,0:T(8,128)S(1)} custom-call(bf16[96,1024]{1,0:T(8,128)(2,1)S(1)} %counts.1.sel, bf16[512,128]{1,0:T(8,128)(2,1)S(1)} %get-tuple-element.14.a_lines, f32[96,4096]{1,0:T(8,128)S(1)} %far_shard.1.acc, bf16[16,4096]{1,0:T(8,128)(2,1)S(1)} %collective-permute-done.2.b_ref), custom_call_target="tpu_custom_call" | custom-call | flops 469762048 | bytes 4194304 | tf_op jit(solution)/shard_map/near_shard/pallas_call | solution.py:298
  14.4 0.1 collective-permute-done.3.b_ref
  14.6 0.8 %last_shard.2 = (f32[24,2048]{1,0:T(8,128)S(1)}, f32[24,2048]{1,0:T(8,128)S(1)}, bf16[48,2048]{1,0:T(8,128)(2,1)S(1)}, bf16[128,2048]{1,0:T(8,128)(2,1)S(1)}) custom-call(bf16[96,1024]{1,0:T(8,128)(2,1)S(1)} %counts.1.sel, bf16[512,128]{1,0:T(8,128)(2,1)S(1)} %get-tuple-element.14.a_lines, f32[96,4096]{1,0:T(8,128)S(1)} %near_shard.1.acc, ...), custom_call_target="tpu_custom_call" | custom-call | flops 234881024 | bytes 2097152 | tf_op jit(solution)/shard_map/last_shard/pallas_call | solution.py:313
  15.3 0.1 collective-permute-start.4
  15.4 0.7 %last_shard.3 = (f32[24,2048]{1,0:T(8,128)S(1)}, f32[24,2048]{1,0:T(8,128)S(1)}, bf16[48,2048]{1,0:T(8,128)(2,1)S(1)}) custom-call(bf16[96,1024]{1,0:T(8,128)(2,1)S(1)} %counts.1.sel, bf16[512,128]{1,0:T(8,128)(2,1)S(1)} %get-tuple-element.14.a_lines, f32[96,4096]{1,0:T(8,128)S(1)} %near_shard.1.acc, bf16[16,4096]{1,0:T(8,128)(2,1)S(1)} %collective-permute-done.3.b_ref, ...), custom_call_target="tpu_custom_call" | custom-call | flops 234881024 | bytes 2097152 | tf_op jit(solution)/shard_map/last_shard/pallas_call | solution.py:313
  16.1 0.6 %collective-permute-start.6 = (bf16[48,2048]{1,0:T(8,128)(2,1)S(1)}, bf16[48,2048]{1,0:T(8,128)(2,1)S(1)}, u32[]{:S(2)}, u32[]{:S(2)}) collective-permute-start(bf16[48,2048]{1,0:T(8,128)(2,1)S(1)} %get-tuple-element.21), channel_id=1, source_target_pairs={{0,1},{1,0},{2,3},{3,2},{4,5},{5,4},{6,7},{7,6},{8,9},{9,8},{10,11... | collective-permute-start | bytes 589832 | tf_op jit(solution)/shard_map/ppermute | solution.py:251
  16.7 0.2 collective-permute-done.4.arrived.refs_1_
  16.9 2.1 %collective-permute-start.5 = (bf16[24,2048]{1,0:T(8,128)(2,1)S(1)}, bf16[24,2048]{1,0:T(8,128)(2,1)S(1)}, u32[]{:S(2)}, u32[]{:S(2)}) collective-permute-start(bf16[24,2048]{1,0:T(8,128)(2,1)S(1)} %join_cores.2), channel_id=1, source_target_pairs={{0,2},{1,3},{2,0},{3,1},{4,6},{5,7},{6,4},{7,5},{8,10},{9,11},{10,... | collective-permute-start | bytes 294920 | tf_op jit(solution)/shard_map/ppermute | solution.py:251
  19.0 0.0 collective-permute-done.6.arrived.refs_4_
  19.0 0.9 %collective-permute-start.7 = (bf16[24,2048]{1,0:T(8,128)(2,1)S(1)}, bf16[24,2048]{1,0:T(8,128)(2,1)S(1)}, u32[]{:S(2)}, u32[]{:S(2)}) collective-permute-start(bf16[24,2048]{1,0:T(8,128)(2,1)S(1)} %join_cores.3), channel_id=1, source_target_pairs={{0,2},{1,3},{2,0},{3,1},{4,6},{5,7},{6,4},{7,5},{8,10},{9,11},{10,... | collective-permute-start | bytes 294920 | tf_op jit(solution)/shard_map/ppermute | solution.py:251
  19.9 2.7 %collective-permute-done.5.refs_2_ = bf16[24,2048]{1,0:T(8,128)(2,1)S(1)} collective-permute-done((bf16[24,2048]{1,0:T(8,128)(2,1)S(1)}, bf16[24,2048]{1,0:T(8,128)(2,1)S(1)}, u32[]{:S(2)}, u32[]{:S(2)}) %collective-permute-start.5) | collective-permute-done | bytes 98336 | tf_op jit(solution)/shard_map/ppermute | solution.py:251
  22.6 1.6 %collective-permute-done.7.refs_5_ = bf16[24,2048]{1,0:T(8,128)(2,1)S(1)} collective-permute-done((bf16[24,2048]{1,0:T(8,128)(2,1)S(1)}, bf16[24,2048]{1,0:T(8,128)(2,1)S(1)}, u32[]{:S(2)}, u32[]{:S(2)}) %collective-permute-start.7) | collective-permute-done | bytes 98336 | tf_op jit(solution)/shard_map/ppermute | solution.py:251
  24.2 0.7 %add_layers.1 = bf16[24,4096]{1,0:T(8,128)(2,1)} custom-call(f32[24,2048]{1,0:T(8,128)S(1)} %get-tuple-element.16.refs_0_, bf16[48,2048]{1,0:T(8,128)(2,1)S(1)} %collective-permute-done.4.arrived.refs_1_, bf16[24,2048]{1,0:T(8,128)(2,1)S(1)} %collective-permute-done.5.refs_2_, f32[24,2048]{1,0:T(8,128)S(1)} %get-tuple-element.20.refs_3_, ...), custom_call_target="tpu_custom_call" | custom-call | flops 196608 | bytes 1048576 | tf_op jit(solution)/shard_map/add_layers/pallas_call | solution.py:328
  (10 shorter events, 0.1 us)
Async XLA Ops:
  0.0 12.2 %collective-permute-start.1 = (bf16[16,4096]{1,0:T(8,128)(2,1)}, bf16[16,4096]{1,0:T(8,128)(2,1)S(1)}, u32[]{:S(2)}, u32[]{:S(2)}) collective-permute-start(bf16[16,4096]{1,0:T(8,128)(2,1)} %bitcast.7), channel_id=1, source_target_pairs={{0,16},{8,24},{16,0},{24,8},{1,17},{9,25},{17,1},{25,9},{2,18},{10... | collective-permute-start | bytes 393224 | tf_op jit(solution)/shard_map/ppermute | solution.py:251
  4.0 9.3 %collective-permute-start.2 = (bf16[16,4096]{1,0:T(8,128)(2,1)}, bf16[16,4096]{1,0:T(8,128)(2,1)S(1)}, u32[]{:S(2)}, u32[]{:S(2)}) collective-permute-start(bf16[16,4096]{1,0:T(8,128)(2,1)} %bitcast.8), channel_id=1, source_target_pairs={{0,8},{8,0},{16,24},{24,16},{1,9},{9,1},{17,25},{25,17},{2,10},{10... | collective-permute-start | bytes 393224 | tf_op jit(solution)/shard_map/ppermute | solution.py:251
  5.6 9.0 %collective-permute-start.3 = (bf16[16,4096]{1,0:T(8,128)(2,1)}, bf16[16,4096]{1,0:T(8,128)(2,1)S(1)}, u32[]{:S(2)}, u32[]{:S(2)}) collective-permute-start(bf16[16,4096]{1,0:T(8,128)(2,1)} %bitcast.9), channel_id=1, source_target_pairs={{0,24},{8,16},{16,8},{24,0},{1,25},{9,17},{17,9},{25,1},{2,26},{10... | collective-permute-start | bytes 393224 | tf_op jit(solution)/shard_map/ppermute | solution.py:251
  5.6 2.6 %copy-start = (s32[1,1,1,768]{3,2,1,0:T(1,128)S(1)}, s32[1,1,1,768]{3,2,1,0:T(1,128)}, u32[]{:S(2)}) copy-start(s32[1,1,1,768]{3,2,1,0:T(1,128)} %param.6) | copy-start | bytes 9220
  5.6 2.6 %copy-start.1 = (s32[1,1,1,768]{3,2,1,0:T(1,128)S(1)}, s32[1,1,1,768]{3,2,1,0:T(1,128)}, u32[]{:S(2)}) copy-start(s32[1,1,1,768]{3,2,1,0:T(1,128)} %param.7) | copy-start | bytes 9220
  5.6 4.5 %collective-permute-start = (bf16[8,4096]{1,0:T(8,128)(2,1)}, bf16[8,4096]{1,0:T(8,128)(2,1)S(1)}, u32[]{:S(2)}, u32[]{:S(2)}) collective-permute-start(bf16[8,4096]{1,0:T(8,128)(2,1)} %bitcast.11), channel_id=1, source_target_pairs={{0,4},{4,0},{1,5},{5,1},{2,6},{6,2},{3,7},{7,3},{8,12},{12,8},{9,1... | collective-permute-start | bytes 196616 | tf_op jit(solution)/shard_map/ppermute | solution.py:251
  7.3 0.9 %copy-start.2 = (bf16[1,1,1,16,4096]{4,3,2,1,0:T(8,128)(2,1)S(1)}, bf16[1,1,1,16,4096]{4,3,2,1,0:T(8,128)(2,1)}, u32[]{:S(2)}) copy-start(bf16[1,1,1,16,4096]{4,3,2,1,0:T(8,128)(2,1)} %param.5) | copy-start | bytes 393220
  8.2 1.9 %copy-start.3 = (bf16[1,1,1,8,4096]{4,3,2,1,0:T(8,128)(2,1)S(1)}, bf16[1,1,1,8,4096]{4,3,2,1,0:T(8,128)(2,1)}, u32[]{:S(2)}) copy-start(bf16[1,1,1,8,4096]{4,3,2,1,0:T(8,128)(2,1)} %param.4) | copy-start | bytes 196612
  15.3 1.5 %collective-permute-start.4 = (bf16[48,2048]{1,0:T(8,128)(2,1)S(1)}, bf16[48,2048]{1,0:T(8,128)(2,1)S(1)}, u32[]{:S(2)}, u32[]{:S(2)}) collective-permute-start(bf16[48,2048]{1,0:T(8,128)(2,1)S(1)} %get-tuple-element.17), channel_id=1, source_target_pairs={{0,1},{1,0},{2,3},{3,2},{4,5},{5,4},{6,7},{7,6},{8,9},{9,8},{10,11... | collective-permute-start | bytes 589832 | tf_op jit(solution)/shard_map/ppermute | solution.py:251
  16.1 2.9 %collective-permute-start.6 = (bf16[48,2048]{1,0:T(8,128)(2,1)S(1)}, bf16[48,2048]{1,0:T(8,128)(2,1)S(1)}, u32[]{:S(2)}, u32[]{:S(2)}) collective-permute-start(bf16[48,2048]{1,0:T(8,128)(2,1)S(1)} %get-tuple-element.21), channel_id=1, source_target_pairs={{0,1},{1,0},{2,3},{3,2},{4,5},{5,4},{6,7},{7,6},{8,9},{9,8},{10,11... | collective-permute-start | bytes 589832 | tf_op jit(solution)/shard_map/ppermute | solution.py:251
  16.9 5.7 %collective-permute-start.5 = (bf16[24,2048]{1,0:T(8,128)(2,1)S(1)}, bf16[24,2048]{1,0:T(8,128)(2,1)S(1)}, u32[]{:S(2)}, u32[]{:S(2)}) collective-permute-start(bf16[24,2048]{1,0:T(8,128)(2,1)S(1)} %join_cores.2), channel_id=1, source_target_pairs={{0,2},{1,3},{2,0},{3,1},{4,6},{5,7},{6,4},{7,5},{8,10},{9,11},{10,... | collective-permute-start | bytes 294920 | tf_op jit(solution)/shard_map/ppermute | solution.py:251
  19.0 5.2 %collective-permute-start.7 = (bf16[24,2048]{1,0:T(8,128)(2,1)S(1)}, bf16[24,2048]{1,0:T(8,128)(2,1)S(1)}, u32[]{:S(2)}, u32[]{:S(2)}) collective-permute-start(bf16[24,2048]{1,0:T(8,128)(2,1)S(1)} %join_cores.3), channel_id=1, source_target_pairs={{0,2},{1,3},{2,0},{3,1},{4,6},{5,7},{6,4},{7,5},{8,10},{9,11},{10,... | collective-permute-start | bytes 294920 | tf_op jit(solution)/shard_map/ppermute | solution.py:251

commit v10 on v9

--- a/solution.py
+++ b/solution.py
@@ -172,8 +172,9 @@
     add_shards(0, groups, sel, a_lines, b_refs, None, acc, raw, prod)
 
 
-def more_kernel(start, sel, a_lines, acc, b_ref, out, raw, prod):
-    add_shards(start, (1,), sel, a_lines, (b_ref,), acc, out, raw, prod)
+def more_kernel(start, groups, sel, a_lines, acc, *refs):
+    b_refs, (out, raw, prod) = refs[-4::-1], refs[-3:]
+    add_shards(start, groups, sel, a_lines, b_refs, acc, out, raw, prod)
 
 
 def add_shards(start, groups, sel, a_lines, b_refs, acc, out, raw, prod):
@@ -216,30 +217,34 @@
     out[...] = (far[...] + arrived[:out.shape[0], :].astype(F32)).astype(out.dtype)
 
 
-def add_kernel(*refs):
-    out = refs[-1]
-    count, done = out.shape[0], 0
-    for own, arrived, joined in zip(refs[0:-1:3], refs[1:-1:3], refs[2:-1:3]):
-        total = own[...] + arrived[count:, :].astype(F32) + joined[...].astype(F32)
-        out[:, done:done + total.shape[1]] = total.astype(out.dtype)
-        done += total.shape[1]
+def add_kernel(first_column, own, arrived, joined, *refs):
+    out, total, sem = refs[-3:]
+    count, width = own.shape
+    value = own[...] + arrived[count:, :].astype(F32) + joined[...].astype(F32)
+    total[...] = value.astype(total.dtype)
+    write = pltpu.make_async_copy(total, out.at[:, pl.ds(first_column, width)], sem)
+    write.start()
+    write.wait()
 
 
 VMEM = pl.BlockSpec(memory_space=pltpu.VMEM)
+HBM = pl.BlockSpec(memory_space=pltpu.HBM)
 
 
 def shape(dims, kind):
     return jax.ShapeDtypeStruct(dims, kind)
 
 
-def call(kernel, outs, scratch, n_in, name, flops, moved):
+def call(kernel, outs, scratch, n_in, name, flops, moved, in_place=None):
     held = sum(s.dtype.itemsize * functools.reduce(lambda x, y: x * y, s.shape) for s in outs + scratch)
     return pl.pallas_call(
         kernel,
         out_shape=outs,
-        in_specs=[VMEM] * n_in,
-        out_specs=[VMEM] * len(outs),
-        scratch_shapes=[pltpu.VMEM(s.shape, s.dtype) for s in scratch],
+        in_specs=[VMEM] * n_in + [HBM] * (in_place or 0),
+        out_specs=[VMEM if in_place is None else HBM] * len(outs),
+        scratch_shapes=[pltpu.VMEM(s.shape, s.dtype) for s in scratch]
+        + ([] if in_place is None else [pltpu.SemaphoreType.DMA]),
+        input_output_aliases={n_in: 0} if in_place else {},
         compiler_params=pltpu.CompilerParams(vmem_limit_bytes=min(held + 16 * MIB, 58 * MIB)),
         cost_estimate=pl.CostEstimate(flops=flops, bytes_accessed=moved, transcendentals=0),
         name=name,
@@ -282,6 +287,7 @@
         MIB,
     )(a_index, b_index)
 
+    groups = (2,) if pairs * FLAT * 2 < 4 * MIB else (1, 1)
     raw = shape((right_each * LINES, LANES), F32)
     one = shape((LINES, pairs, LANES), BF16)
     shard_flops = 2 * pairs * LINES * LANES * LANES + 2 * pairs * tiles * FLAT
@@ -294,16 +300,15 @@
         OWN_FLOPS,
         4 * MIB,
     )(sel, *a_parts, b_here)
-    for name, m, b_shard in (("far_shard", 2, b_far), ("near_shard", 1, b_near)):
-        (acc,) = call(
-            functools.partial(more_kernel, m * pairs),
-            [shape((tiles, FLAT), F32)],
-            [raw, one],
-            4,
-            name,
-            shard_flops,
-            4 * MIB,
-        )(sel, a_lines, acc, b_shard)
+    (acc,) = call(
+        functools.partial(more_kernel, pairs, groups),
+        [shape((tiles, FLAT), F32)],
+        [raw, shape((LINES, max(groups) * pairs, LANES), BF16)],
+        5,
+        "near_and_far",
+        2 * shard_flops,
+        8 * MIB,
+    )(sel, a_lines, acc, b_far, b_near)
     results, kept = [], []
     for first_line, lines in ((0, FIRST_LINES), (FIRST_LINES, LINES - FIRST_LINES)):
         width = lines * LANES
@@ -325,9 +330,20 @@
             join_kernel, [shape((owned, width), BF16)], [], 2, "join_cores", owned * width, MIB
         )(far, arrived)
         results += [own, arrived, exchange(joined, "layer", 2)]
-    (out,) = call(
-        add_kernel, [shape((owned, FLAT), BF16)], [], len(results), "add_layers", 2 * owned * FLAT, MIB
-    )(*results)
+    written, column = [], 0
+    for own, arrived, joined in zip(results[0::3], results[1::3], results[2::3]):
+        written = call(
+            functools.partial(add_kernel, column),
+            [shape((owned, FLAT), BF16)],
+            [shape(own.shape, BF16)],
+            3,
+            "add_layers",
+            owned * FLAT,
+            MIB,
+            len(written),
+        )(own, arrived, joined, *written)
+        column += own.shape[1]
+    (out,) = written
     return out.reshape(1, 1, owned, FLAT)
 
 

time: 25.1 us -> 24.9 us (level)
  waiting for transfers between devices: 6.71 us -> 6.27 us
  Pallas kernels: 6.32 us -> 6.7 us
    ppermute x8, waiting for transfers between devices: 6.71 us -> 6.27 us  [exchange(): return lax.ppermute(x, axis, [(i, i ^ q) for i in range(size)])]
    pallas_call x3, Pallas kernels: 2.95 us -> 3.33 us  [the longest x1 1.97 us: shards(): call(functools.partial(more_kernel, pairs, groups), [shape((tiles, FLAT),...]
    ppermute x8, starting transfers between devices: 10.9 us -> 10.7 us  [exchange(): return lax.ppermute(x, axis, [(i, i ^ q) for i in range(size)])]
  transfers between devices with their start and end apart: 8 -> 8, of which waited for: 6 -> 6; matrix products, arithmetic and copies ran while one was open for 0% -> 0% of each run, Pallas kernels for 19% -> 21%
where the time goes in v10:
time: 24.9 us; the launch traced here: 24.6 us
  starting transfers between devices  10.7 us (43%)
  Pallas kernels  6.7 us (27%)
  waiting for transfers between devices  6.27 us (25%)
  local copies, waits for them, and re-layouts  0.91 us (4%)
    ppermute x8, starting transfers between devices, exchange(): return lax.ppermute(x, axis, [(i, i ^ q) for i in range(size)])  10.7 us
    ppermute x8, waiting for transfers between devices, exchange(): return lax.ppermute(x, axis, [(i, i ^ q) for i in range(size)])  6.27 us
    pallas_call x1, Pallas kernels, shards(): call(functools.partial(more_kernel, pairs, groups), [shape((tiles, FLAT),...  1.97 us
    pallas_call x2, Pallas kernels, shards(): call(functools.partial(last_kernel, 3 * pairs, first_line), outs, ([] if...  1.43 us
    pallas_call x2, Pallas kernels, shards(): call(functools.partial(add_kernel, column), [shape((owned, FLAT), BF16)],...  1.36 us
    pallas_call x1, Pallas kernels, shards(): call(functools.partial(own_kernel, (1,), len(a_parts)), [shape((tiles, FL...  1.15 us
    unnamed x8, local copies, waits for them, and re-layouts  0.91 us
    pallas_call x1, Pallas kernels, shards(): call(functools.partial(counts_kernel, cols == 2, left_tiles, left_each, r...  0.73 us
  transfers between devices with their start and end apart: 8, of which 6 were waited for; matrix products, arithmetic and copies ran while one was open for 0% of the time, Pallas kernels for 21%

profile of v10, /device:TPU:0, one launch (start us, length us, event | category | flops | bytes accessed | tf_op | source)
XLA Modules:
  0.0 24.6 jit_solution(10377435512687241864)
XLA Ops:
  0.0 4.0 %collective-permute-start.1 = (bf16[16,4096]{1,0:T(8,128)(2,1)}, bf16[16,4096]{1,0:T(8,128)(2,1)S(1)}, u32[]{:S(2)}, u32[]{:S(2)}) collective-permute-start(bf16[16,4096]{1,0:T(8,128)(2,1)} %bitcast.7), channel_id=1, source_target_pairs={{0,16},{8,24},{16,0},{24,8},{1,17},{9,25},{17,1},{25,9},{2,18},{10... | collective-permute-start | bytes 393224 | tf_op jit(solution)/shard_map/ppermute | solution.py:256
  4.0 1.6 %collective-permute-start.2 = (bf16[16,4096]{1,0:T(8,128)(2,1)}, bf16[16,4096]{1,0:T(8,128)(2,1)S(1)}, u32[]{:S(2)}, u32[]{:S(2)}) collective-permute-start(bf16[16,4096]{1,0:T(8,128)(2,1)} %bitcast.8), channel_id=1, source_target_pairs={{0,8},{8,0},{16,24},{24,16},{1,9},{9,1},{17,25},{25,17},{2,10},{10... | collective-permute-start | bytes 393224 | tf_op jit(solution)/shard_map/ppermute | solution.py:256
  5.6 0.0 collective-permute-start.3
  5.6 1.7 %collective-permute-start = (bf16[8,4096]{1,0:T(8,128)(2,1)}, bf16[8,4096]{1,0:T(8,128)(2,1)S(1)}, u32[]{:S(2)}, u32[]{:S(2)}) collective-permute-start(bf16[8,4096]{1,0:T(8,128)(2,1)} %bitcast.11), channel_id=1, source_target_pairs={{0,4},{4,0},{1,5},{5,1},{2,6},{6,2},{3,7},{7,3},{8,12},{12,8},{9,1... | collective-permute-start | bytes 196616 | tf_op jit(solution)/shard_map/ppermute | solution.py:256
  7.3 0.9 %copy-done.2 = bf16[1,1,1,16,4096]{4,3,2,1,0:T(8,128)(2,1)S(1)} copy-done((bf16[1,1,1,16,4096]{4,3,2,1,0:T(8,128)(2,1)S(1)}, bf16[1,1,1,16,4096]{4,3,2,1,0:T(8,128)(2,1)}, u32[]{:S(2)}) %copy-start.2) | copy-done | bytes 131096
  8.3 0.7 %counts.1.sel = bf16[96,1024]{1,0:T(8,128)(2,1)S(1)} custom-call(s32[1,768]{1,0:T(1,128)S(1)} %bitcast.5, s32[1,768]{1,0:T(1,128)S(1)} %bitcast.6), custom_call_target="tpu_custom_call" | custom-call | flops 1179648 | bytes 1048576 | tf_op jit(solution)/shard_map/counts/pallas_call | solution.py:280
  9.0 1.1 %collective-permute-done.refs_1_ = bf16[8,4096]{1,0:T(8,128)(2,1)S(1)} collective-permute-done((bf16[8,4096]{1,0:T(8,128)(2,1)}, bf16[8,4096]{1,0:T(8,128)(2,1)S(1)}, u32[]{:S(2)}, u32[]{:S(2)}) %collective-permute-start) | collective-permute-done | bytes 65568 | tf_op jit(solution)/shard_map/ppermute | solution.py:256
  10.1 1.1 %own_shard.1 = (f32[96,4096]{1,0:T(8,128)S(1)}, bf16[512,128]{1,0:T(8,128)(2,1)S(1)}) custom-call(bf16[96,1024]{1,0:T(8,128)(2,1)S(1)} %counts.1.sel, bf16[8,4096]{1,0:T(8,128)(2,1)S(1)} %bitcast.12, bf16[8,4096]{1,0:T(8,128)(2,1)S(1)} %collective-permute-done.refs_1_, bf16[16,4096]{1,0:T(8,128)(2,1)S(1)} %stage.1.refs_2_), custom_call_target="tpu_custom_call" | custom-call | flops 500000000 | bytes 4194304 | tf_op jit(solution)/shard_map/own_shard/pallas_call | solution.py:294
  11.3 0.9 %collective-permute-done.1.refs_0_ = bf16[16,4096]{1,0:T(8,128)(2,1)S(1)} collective-permute-done((bf16[16,4096]{1,0:T(8,128)(2,1)}, bf16[16,4096]{1,0:T(8,128)(2,1)S(1)}, u32[]{:S(2)}, u32[]{:S(2)}) %collective-permute-start.1) | collective-permute-done | bytes 131104 | tf_op jit(solution)/shard_map/ppermute | solution.py:256
  12.2 0.0 collective-permute-done.2.refs_1_
  12.2 2.0 %near_and_far.1.acc = f32[96,4096]{1,0:T(8,128)S(1)} custom-call(bf16[96,1024]{1,0:T(8,128)(2,1)S(1)} %counts.1.sel, bf16[512,128]{1,0:T(8,128)(2,1)S(1)} %get-tuple-element.14.a_lines, f32[96,4096]{1,0:T(8,128)S(1)} %get-tuple-element.15.acc, bf16[16,4096]{1,0:T(8,128)(2,1)S(1)} %collective-permute-done.1.refs_0_, ...), custom_call_target="tpu_custom_call" | custom-call | flops 939524096 | bytes 8388608 | tf_op jit(solution)/shard_map/near_and_far/pallas_call | solution.py:303
  14.2 0.4 %collective-permute-done.3.b_ref = bf16[16,4096]{1,0:T(8,128)(2,1)S(1)} collective-permute-done((bf16[16,4096]{1,0:T(8,128)(2,1)}, bf16[16,4096]{1,0:T(8,128)(2,1)S(1)}, u32[]{:S(2)}, u32[]{:S(2)}) %collective-permute-start.3) | collective-permute-done | bytes 131104 | tf_op jit(solution)/shard_map/ppermute | solution.py:256
  14.6 0.8 %last_shard.2 = (f32[24,2048]{1,0:T(8,128)S(1)}, f32[24,2048]{1,0:T(8,128)S(1)}, bf16[48,2048]{1,0:T(8,128)(2,1)S(1)}, bf16[128,2048]{1,0:T(8,128)(2,1)S(1)}) custom-call(bf16[96,1024]{1,0:T(8,128)(2,1)S(1)} %counts.1.sel, bf16[512,128]{1,0:T(8,128)(2,1)S(1)} %get-tuple-element.14.a_lines, f32[96,4096]{1,0:T(8,128)S(1)} %near_and_far.1.acc, ...), custom_call_target="tpu_custom_call" | custom-call | flops 234881024 | bytes 2097152 | tf_op jit(solution)/shard_map/last_shard/pallas_call | solution.py:318
  15.3 0.1 collective-permute-start.6
  15.4 0.7 %last_shard.3 = (f32[24,2048]{1,0:T(8,128)S(1)}, f32[24,2048]{1,0:T(8,128)S(1)}, bf16[48,2048]{1,0:T(8,128)(2,1)S(1)}) custom-call(bf16[96,1024]{1,0:T(8,128)(2,1)S(1)} %counts.1.sel, bf16[512,128]{1,0:T(8,128)(2,1)S(1)} %get-tuple-element.14.a_lines, f32[96,4096]{1,0:T(8,128)S(1)} %near_and_far.1.acc, bf16[16,4096]{1,0:T(8,128)(2,1)S(1)} %collective-permute-done.3.b_ref, ...), custom_call_target="tpu_custom_call" | custom-call | flops 234881024 | bytes 2097152 | tf_op jit(solution)/shard_map/last_shard/pallas_call | solution.py:318
  16.1 0.6 %collective-permute-start.4 = (bf16[48,2048]{1,0:T(8,128)(2,1)S(1)}, bf16[48,2048]{1,0:T(8,128)(2,1)S(1)}, u32[]{:S(2)}, u32[]{:S(2)}) collective-permute-start(bf16[48,2048]{1,0:T(8,128)(2,1)S(1)} %get-tuple-element.18), channel_id=1, source_target_pairs={{0,1},{1,0},{2,3},{3,2},{4,5},{5,4},{6,7},{7,6},{8,9},{9,8},{10,11... | collective-permute-start | bytes 589832 | tf_op jit(solution)/shard_map/ppermute | solution.py:256
  16.7 0.2 collective-permute-done.6.arrived
  16.9 1.8 %collective-permute-start.7 = (bf16[24,2048]{1,0:T(8,128)(2,1)S(1)}, bf16[24,2048]{1,0:T(8,128)(2,1)S(1)}, u32[]{:S(2)}, u32[]{:S(2)}) collective-permute-start(bf16[24,2048]{1,0:T(8,128)(2,1)S(1)} %join_cores.3), channel_id=1, source_target_pairs={{0,2},{1,3},{2,0},{3,1},{4,6},{5,7},{6,4},{7,5},{8,10},{9,11},{10,... | collective-permute-start | bytes 294920 | tf_op jit(solution)/shard_map/ppermute | solution.py:256
  18.7 0.0 collective-permute-done.4.arrived
  18.8 0.9 %collective-permute-start.5 = (bf16[24,2048]{1,0:T(8,128)(2,1)S(1)}, bf16[24,2048]{1,0:T(8,128)(2,1)S(1)}, u32[]{:S(2)}, u32[]{:S(2)}) collective-permute-start(bf16[24,2048]{1,0:T(8,128)(2,1)S(1)} %join_cores.2), channel_id=1, source_target_pairs={{0,2},{1,3},{2,0},{3,1},{4,6},{5,7},{6,4},{7,5},{8,10},{9,11},{10,... | collective-permute-start | bytes 294920 | tf_op jit(solution)/shard_map/ppermute | solution.py:256
  19.6 2.8 %collective-permute-done.7.joined = bf16[24,2048]{1,0:T(8,128)(2,1)S(1)} collective-permute-done((bf16[24,2048]{1,0:T(8,128)(2,1)S(1)}, bf16[24,2048]{1,0:T(8,128)(2,1)S(1)}, u32[]{:S(2)}, u32[]{:S(2)}) %collective-permute-start.7) | collective-permute-done | bytes 98336 | tf_op jit(solution)/shard_map/ppermute | solution.py:256
  22.4 0.7 %add_layers.2.refs_0_ = bf16[24,4096]{1,0:T(8,128)(2,1)} custom-call(f32[24,2048]{1,0:T(8,128)S(1)} %get-tuple-element.20.own, bf16[48,2048]{1,0:T(8,128)(2,1)S(1)} %collective-permute-done.6.arrived, bf16[24,2048]{1,0:T(8,128)(2,1)S(1)} %collective-permute-done.7.joined), custom_call_target="tpu_custom_call" | custom-call | flops 98304 | bytes 1048576 | tf_op jit(solution)/shard_map/add_layers/pallas_call | solution.py:335
  23.1 0.8 %collective-permute-done.5.joined = bf16[24,2048]{1,0:T(8,128)(2,1)S(1)} collective-permute-done((bf16[24,2048]{1,0:T(8,128)(2,1)S(1)}, bf16[24,2048]{1,0:T(8,128)(2,1)S(1)}, u32[]{:S(2)}, u32[]{:S(2)}) %collective-permute-start.5) | collective-permute-done | bytes 98336 | tf_op jit(solution)/shard_map/ppermute | solution.py:256
  23.9 0.7 %add_layers.3 = bf16[24,4096]{1,0:T(8,128)(2,1)} custom-call(f32[24,2048]{1,0:T(8,128)S(1)} %get-tuple-element.17.own, bf16[48,2048]{1,0:T(8,128)(2,1)S(1)} %collective-permute-done.4.arrived, bf16[24,2048]{1,0:T(8,128)(2,1)S(1)} %collective-permute-done.5.joined, bf16[24,4096]{1,0:T(8,128)(2,1)} %add_layers.2.refs_0_), custom_call_target="tpu_custom_call", output_to_operand_aliasing={{}: (3, {})} | custom-call | flops 98304 | bytes 1048576 | tf_op jit(solution)/shard_map/add_layers/pallas_call | solution.py:335
  (10 shorter events, 0.1 us)
Async XLA Ops:
  0.0 12.2 %collective-permute-start.1 = (bf16[16,4096]{1,0:T(8,128)(2,1)}, bf16[16,4096]{1,0:T(8,128)(2,1)S(1)}, u32[]{:S(2)}, u32[]{:S(2)}) collective-permute-start(bf16[16,4096]{1,0:T(8,128)(2,1)} %bitcast.7), channel_id=1, source_target_pairs={{0,16},{8,24},{16,0},{24,8},{1,17},{9,25},{17,1},{25,9},{2,18},{10... | collective-permute-start | bytes 393224 | tf_op jit(solution)/shard_map/ppermute | solution.py:256
  4.0 8.2 %collective-permute-start.2 = (bf16[16,4096]{1,0:T(8,128)(2,1)}, bf16[16,4096]{1,0:T(8,128)(2,1)S(1)}, u32[]{:S(2)}, u32[]{:S(2)}) collective-permute-start(bf16[16,4096]{1,0:T(8,128)(2,1)} %bitcast.8), channel_id=1, source_target_pairs={{0,8},{8,0},{16,24},{24,16},{1,9},{9,1},{17,25},{25,17},{2,10},{10... | collective-permute-start | bytes 393224 | tf_op jit(solution)/shard_map/ppermute | solution.py:256
  5.6 9.0 %collective-permute-start.3 = (bf16[16,4096]{1,0:T(8,128)(2,1)}, bf16[16,4096]{1,0:T(8,128)(2,1)S(1)}, u32[]{:S(2)}, u32[]{:S(2)}) collective-permute-start(bf16[16,4096]{1,0:T(8,128)(2,1)} %bitcast.9), channel_id=1, source_target_pairs={{0,24},{8,16},{16,8},{24,0},{1,25},{9,17},{17,9},{25,1},{2,26},{10... | collective-permute-start | bytes 393224 | tf_op jit(solution)/shard_map/ppermute | solution.py:256
  5.6 2.6 %copy-start = (s32[1,1,1,768]{3,2,1,0:T(1,128)S(1)}, s32[1,1,1,768]{3,2,1,0:T(1,128)}, u32[]{:S(2)}) copy-start(s32[1,1,1,768]{3,2,1,0:T(1,128)} %param.6) | copy-start | bytes 9220
  5.6 2.6 %copy-start.1 = (s32[1,1,1,768]{3,2,1,0:T(1,128)S(1)}, s32[1,1,1,768]{3,2,1,0:T(1,128)}, u32[]{:S(2)}) copy-start(s32[1,1,1,768]{3,2,1,0:T(1,128)} %param.7) | copy-start | bytes 9220
  5.6 4.5 %collective-permute-start = (bf16[8,4096]{1,0:T(8,128)(2,1)}, bf16[8,4096]{1,0:T(8,128)(2,1)S(1)}, u32[]{:S(2)}, u32[]{:S(2)}) collective-permute-start(bf16[8,4096]{1,0:T(8,128)(2,1)} %bitcast.11), channel_id=1, source_target_pairs={{0,4},{4,0},{1,5},{5,1},{2,6},{6,2},{3,7},{7,3},{8,12},{12,8},{9,1... | collective-permute-start | bytes 196616 | tf_op jit(solution)/shard_map/ppermute | solution.py:256
  7.3 0.9 %copy-start.2 = (bf16[1,1,1,16,4096]{4,3,2,1,0:T(8,128)(2,1)S(1)}, bf16[1,1,1,16,4096]{4,3,2,1,0:T(8,128)(2,1)}, u32[]{:S(2)}) copy-start(bf16[1,1,1,16,4096]{4,3,2,1,0:T(8,128)(2,1)} %param.5) | copy-start | bytes 393220
  8.2 1.9 %copy-start.3 = (bf16[1,1,1,8,4096]{4,3,2,1,0:T(8,128)(2,1)S(1)}, bf16[1,1,1,8,4096]{4,3,2,1,0:T(8,128)(2,1)}, u32[]{:S(2)}) copy-start(bf16[1,1,1,8,4096]{4,3,2,1,0:T(8,128)(2,1)} %param.4) | copy-start | bytes 196612
  15.3 1.5 %collective-permute-start.6 = (bf16[48,2048]{1,0:T(8,128)(2,1)S(1)}, bf16[48,2048]{1,0:T(8,128)(2,1)S(1)}, u32[]{:S(2)}, u32[]{:S(2)}) collective-permute-start(bf16[48,2048]{1,0:T(8,128)(2,1)S(1)} %get-tuple-element.21), channel_id=1, source_target_pairs={{0,1},{1,0},{2,3},{3,2},{4,5},{5,4},{6,7},{7,6},{8,9},{9,8},{10,11... | collective-permute-start | bytes 589832 | tf_op jit(solution)/shard_map/ppermute | solution.py:256
  16.1 2.6 %collective-permute-start.4 = (bf16[48,2048]{1,0:T(8,128)(2,1)S(1)}, bf16[48,2048]{1,0:T(8,128)(2,1)S(1)}, u32[]{:S(2)}, u32[]{:S(2)}) collective-permute-start(bf16[48,2048]{1,0:T(8,128)(2,1)S(1)} %get-tuple-element.18), channel_id=1, source_target_pairs={{0,1},{1,0},{2,3},{3,2},{4,5},{5,4},{6,7},{7,6},{8,9},{9,8},{10,11... | collective-permute-start | bytes 589832 | tf_op jit(solution)/shard_map/ppermute | solution.py:256
  16.9 5.5 %collective-permute-start.7 = (bf16[24,2048]{1,0:T(8,128)(2,1)S(1)}, bf16[24,2048]{1,0:T(8,128)(2,1)S(1)}, u32[]{:S(2)}, u32[]{:S(2)}) collective-permute-start(bf16[24,2048]{1,0:T(8,128)(2,1)S(1)} %join_cores.3), channel_id=1, source_target_pairs={{0,2},{1,3},{2,0},{3,1},{4,6},{5,7},{6,4},{7,5},{8,10},{9,11},{10,... | collective-permute-start | bytes 294920 | tf_op jit(solution)/shard_map/ppermute | solution.py:256
  18.8 5.2 %collective-permute-start.5 = (bf16[24,2048]{1,0:T(8,128)(2,1)S(1)}, bf16[24,2048]{1,0:T(8,128)(2,1)S(1)}, u32[]{:S(2)}, u32[]{:S(2)}) collective-permute-start(bf16[24,2048]{1,0:T(8,128)(2,1)S(1)} %join_cores.2), channel_id=1, source_target_pairs={{0,2},{1,3},{2,0},{3,1},{4,6},{5,7},{6,4},{7,5},{8,10},{9,11},{10,... | collective-permute-start | bytes 294920 | tf_op jit(solution)/shard_map/ppermute | solution.py:256

commit v11 on v10

--- a/solution.py
+++ b/solution.py
@@ -14,6 +14,7 @@
 LINES = FLAT // LANES
 ROWS_AT_ONCE = 512
 FIRST_LINES = LINES // 2
+PARTS = 2
 TILES_AT_ONCE = 4
 LINES_AT_ONCE = 4
 MIB = 1 << 20
@@ -202,15 +203,20 @@
         own, far, sent, rights, raw, prod = refs
     pairs = b_ref.shape[0] * a_lines.shape[0] // LINES
     owned = own.shape[0]
-    all_products(a_lines, b_ref, raw, prod, 0, first_line, rights)
-
-    def put(columns, value):
-        value = value + acc[:, first_line * LANES + columns.start:first_line * LANES + columns.stop]
-        own[:, columns] = value[:owned]
-        far[:, columns] = value[owned:2 * owned]
-        sent[:, columns] = value[2 * owned:].astype(sent.dtype)
-
-    chosen_sums(sel, start, pairs, prod, put)
+    lines = prod.shape[0] // PARTS
+    for part in range(PARTS):
+        skipped = part * lines
+        here = prod.at[skipped:skipped + lines]
+        all_products(a_lines, b_ref, None if part else raw, here, 0, first_line + skipped, rights)
+
+        def put(columns, value, skipped=skipped):
+            columns = slice(columns.start + skipped * LANES, columns.stop + skipped * LANES)
+            value = value + acc[:, first_line * LANES + columns.start:first_line * LANES + columns.stop]
+            own[:, columns] = value[:owned]
+            far[:, columns] = value[owned:2 * owned]
+            sent[:, columns] = value[2 * owned:].astype(sent.dtype)
+
+        chosen_sums(sel, start, pairs, here, put)
 
 
 def join_kernel(far, arrived, out):
@@ -288,7 +294,7 @@
     )(a_index, b_index)
 
     groups = (2,) if pairs * FLAT * 2 < 4 * MIB else (1, 1)
-    raw = shape((right_each * LINES, LANES), F32)
+    raw = shape((right_each * (LINES + 1), LANES), F32)
     one = shape((LINES, pairs, LANES), BF16)
     shard_flops = 2 * pairs * LINES * LANES * LANES + 2 * pairs * tiles * FLAT
     acc, a_lines = call(

time: 24.9 us -> 25.1 us (level)
  Pallas kernels: 6.7 us -> 7.16 us
  waiting for transfers between devices: 6.27 us -> 5.81 us
    ppermute x8, waiting for transfers between devices: 6.27 us -> 5.81 us  [exchange(): return lax.ppermute(x, axis, [(i, i ^ q) for i in range(size)])]
    pallas_call x2, Pallas kernels: 1.43 us -> 1.82 us  [shards(): call(functools.partial(last_kernel, 3 * pairs, first_line), outs, ([] if...]
  transfers between devices with their start and end apart: 8 -> 8, of which waited for: 6 -> 5; matrix products, arithmetic and copies ran while one was open for 0% -> 0% of each run, Pallas kernels for 21% -> 22%
where the time goes in v11:
time: 25.1 us; the launch traced here: 24.9 us
  starting transfers between devices  10.9 us (43%)
  Pallas kernels  7.16 us (29%)
  waiting for transfers between devices  5.81 us (23%)
  local copies, waits for them, and re-layouts  0.91 us (4%)
    ppermute x8, starting transfers between devices, exchange(): return lax.ppermute(x, axis, [(i, i ^ q) for i in range(size)])  10.9 us
    ppermute x8, waiting for transfers between devices, exchange(): return lax.ppermute(x, axis, [(i, i ^ q) for i in range(size)])  5.81 us
    pallas_call x1, Pallas kernels, shards(): call(functools.partial(more_kernel, pairs, groups), [shape((tiles, FLAT),...  2.04 us
    pallas_call x2, Pallas kernels, shards(): call(functools.partial(last_kernel, 3 * pairs, first_line), outs, ([] if...  1.82 us
    pallas_call x2, Pallas kernels, shards(): call(functools.partial(add_kernel, column), [shape((owned, FLAT), BF16)],...  1.37 us
    pallas_call x1, Pallas kernels, shards(): call(functools.partial(own_kernel, (1,), len(a_parts)), [shape((tiles, FL...  1.15 us
    unnamed x8, local copies, waits for them, and re-layouts  0.91 us
    pallas_call x1, Pallas kernels, shards(): call(functools.partial(counts_kernel, cols == 2, left_tiles, left_each, r...  0.73 us
  transfers between devices with their start and end apart: 8, of which 5 were waited for; matrix products, arithmetic and copies ran while one was open for 0% of the time, Pallas kernels for 22%

profile of v11, /device:TPU:0, one launch (start us, length us, event | category | flops | bytes accessed | tf_op | source)
XLA Modules:
  0.0 24.9 jit_solution(2179842975246013759)
XLA Ops:
  0.0 4.0 %collective-permute-start.1 = (bf16[16,4096]{1,0:T(8,128)(2,1)}, bf16[16,4096]{1,0:T(8,128)(2,1)S(1)}, u32[]{:S(2)}, u32[]{:S(2)}) collective-permute-start(bf16[16,4096]{1,0:T(8,128)(2,1)} %bitcast.7), channel_id=1, source_target_pairs={{0,16},{8,24},{16,0},{24,8},{1,17},{9,25},{17,1},{25,9},{2,18},{10... | collective-permute-start | bytes 393224 | tf_op jit(solution)/shard_map/ppermute | solution.py:262
  4.0 1.6 %collective-permute-start.2 = (bf16[16,4096]{1,0:T(8,128)(2,1)}, bf16[16,4096]{1,0:T(8,128)(2,1)S(1)}, u32[]{:S(2)}, u32[]{:S(2)}) collective-permute-start(bf16[16,4096]{1,0:T(8,128)(2,1)} %bitcast.8), channel_id=1, source_target_pairs={{0,8},{8,0},{16,24},{24,16},{1,9},{9,1},{17,25},{25,17},{2,10},{10... | collective-permute-start | bytes 393224 | tf_op jit(solution)/shard_map/ppermute | solution.py:262
  5.6 0.0 collective-permute-start.3
  5.6 1.7 %collective-permute-start = (bf16[8,4096]{1,0:T(8,128)(2,1)}, bf16[8,4096]{1,0:T(8,128)(2,1)S(1)}, u32[]{:S(2)}, u32[]{:S(2)}) collective-permute-start(bf16[8,4096]{1,0:T(8,128)(2,1)} %bitcast.11), channel_id=1, source_target_pairs={{0,4},{4,0},{1,5},{5,1},{2,6},{6,2},{3,7},{7,3},{8,12},{12,8},{9,1... | collective-permute-start | bytes 196616 | tf_op jit(solution)/shard_map/ppermute | solution.py:262
  7.3 0.9 %copy-done.2 = bf16[1,1,1,16,4096]{4,3,2,1,0:T(8,128)(2,1)S(1)} copy-done((bf16[1,1,1,16,4096]{4,3,2,1,0:T(8,128)(2,1)S(1)}, bf16[1,1,1,16,4096]{4,3,2,1,0:T(8,128)(2,1)}, u32[]{:S(2)}) %copy-start.2) | copy-done | bytes 131096
  8.3 0.7 %counts.1.sel = bf16[96,1024]{1,0:T(8,128)(2,1)S(1)} custom-call(s32[1,768]{1,0:T(1,128)S(1)} %bitcast.5, s32[1,768]{1,0:T(1,128)S(1)} %bitcast.6), custom_call_target="tpu_custom_call" | custom-call | flops 1179648 | bytes 1048576 | tf_op jit(solution)/shard_map/counts/pallas_call | solution.py:286
  9.0 1.1 %collective-permute-done.refs_1_ = bf16[8,4096]{1,0:T(8,128)(2,1)S(1)} collective-permute-done((bf16[8,4096]{1,0:T(8,128)(2,1)}, bf16[8,4096]{1,0:T(8,128)(2,1)S(1)}, u32[]{:S(2)}, u32[]{:S(2)}) %collective-permute-start) | collective-permute-done | bytes 65568 | tf_op jit(solution)/shard_map/ppermute | solution.py:262
  10.1 1.2 %own_shard.1 = (f32[96,4096]{1,0:T(8,128)S(1)}, bf16[512,128]{1,0:T(8,128)(2,1)S(1)}) custom-call(bf16[96,1024]{1,0:T(8,128)(2,1)S(1)} %counts.1.sel, bf16[8,4096]{1,0:T(8,128)(2,1)S(1)} %bitcast.12, bf16[8,4096]{1,0:T(8,128)(2,1)S(1)} %collective-permute-done.refs_1_, bf16[16,4096]{1,0:T(8,128)(2,1)S(1)} %stage.1.refs_2_), custom_call_target="tpu_custom_call" | custom-call | flops 500000000 | bytes 4194304 | tf_op jit(solution)/shard_map/own_shard/pallas_call | solution.py:300
  11.3 0.9 %collective-permute-done.1.refs_0_ = bf16[16,4096]{1,0:T(8,128)(2,1)S(1)} collective-permute-done((bf16[16,4096]{1,0:T(8,128)(2,1)}, bf16[16,4096]{1,0:T(8,128)(2,1)S(1)}, u32[]{:S(2)}, u32[]{:S(2)}) %collective-permute-start.1) | collective-permute-done | bytes 131104 | tf_op jit(solution)/shard_map/ppermute | solution.py:262
  12.2 0.0 collective-permute-done.2.refs_1_
  12.2 2.0 %near_and_far.1.acc = f32[96,4096]{1,0:T(8,128)S(1)} custom-call(bf16[96,1024]{1,0:T(8,128)(2,1)S(1)} %counts.1.sel, bf16[512,128]{1,0:T(8,128)(2,1)S(1)} %get-tuple-element.14.a_lines, f32[96,4096]{1,0:T(8,128)S(1)} %get-tuple-element.15.acc, bf16[16,4096]{1,0:T(8,128)(2,1)S(1)} %collective-permute-done.1.refs_0_, ...), custom_call_target="tpu_custom_call" | custom-call | flops 939524096 | bytes 8388608 | tf_op jit(solution)/shard_map/near_and_far/pallas_call | solution.py:309
  14.2 0.3 %collective-permute-done.3.b_ref = bf16[16,4096]{1,0:T(8,128)(2,1)S(1)} collective-permute-done((bf16[16,4096]{1,0:T(8,128)(2,1)}, bf16[16,4096]{1,0:T(8,128)(2,1)S(1)}, u32[]{:S(2)}, u32[]{:S(2)}) %collective-permute-start.3) | collective-permute-done | bytes 131104 | tf_op jit(solution)/shard_map/ppermute | solution.py:262
  14.6 1.0 %last_shard.2 = (f32[24,2048]{1,0:T(8,128)S(1)}, f32[24,2048]{1,0:T(8,128)S(1)}, bf16[48,2048]{1,0:T(8,128)(2,1)S(1)}, bf16[128,2048]{1,0:T(8,128)(2,1)S(1)}) custom-call(bf16[96,1024]{1,0:T(8,128)(2,1)S(1)} %counts.1.sel, bf16[512,128]{1,0:T(8,128)(2,1)S(1)} %get-tuple-element.14.a_lines, f32[96,4096]{1,0:T(8,128)S(1)} %near_and_far.1.acc, ...), custom_call_target="tpu_custom_call" | custom-call | flops 234881024 | bytes 2097152 | tf_op jit(solution)/shard_map/last_shard/pallas_call | solution.py:324
  15.5 0.1 collective-permute-start.6
  15.6 0.9 %last_shard.3 = (f32[24,2048]{1,0:T(8,128)S(1)}, f32[24,2048]{1,0:T(8,128)S(1)}, bf16[48,2048]{1,0:T(8,128)(2,1)S(1)}) custom-call(bf16[96,1024]{1,0:T(8,128)(2,1)S(1)} %counts.1.sel, bf16[512,128]{1,0:T(8,128)(2,1)S(1)} %get-tuple-element.14.a_lines, f32[96,4096]{1,0:T(8,128)S(1)} %near_and_far.1.acc, bf16[16,4096]{1,0:T(8,128)(2,1)S(1)} %collective-permute-done.3.b_ref, ...), custom_call_target="tpu_custom_call" | custom-call | flops 234881024 | bytes 2097152 | tf_op jit(solution)/shard_map/last_shard/pallas_call | solution.py:324
  16.5 0.6 %collective-permute-start.4 = (bf16[48,2048]{1,0:T(8,128)(2,1)S(1)}, bf16[48,2048]{1,0:T(8,128)(2,1)S(1)}, u32[]{:S(2)}, u32[]{:S(2)}) collective-permute-start(bf16[48,2048]{1,0:T(8,128)(2,1)S(1)} %get-tuple-element.18), channel_id=1, source_target_pairs={{0,1},{1,0},{2,3},{3,2},{4,5},{5,4},{6,7},{7,6},{8,9},{9,8},{10,11... | collective-permute-start | bytes 589832 | tf_op jit(solution)/shard_map/ppermute | solution.py:262
  17.0 0.0 collective-permute-done.6.arrived
  17.1 1.9 %collective-permute-start.7 = (bf16[24,2048]{1,0:T(8,128)(2,1)S(1)}, bf16[24,2048]{1,0:T(8,128)(2,1)S(1)}, u32[]{:S(2)}, u32[]{:S(2)}) collective-permute-start(bf16[24,2048]{1,0:T(8,128)(2,1)S(1)} %join_cores.3), channel_id=1, source_target_pairs={{0,2},{1,3},{2,0},{3,1},{4,6},{5,7},{6,4},{7,5},{8,10},{9,11},{10,... | collective-permute-start | bytes 294920 | tf_op jit(solution)/shard_map/ppermute | solution.py:262
  19.0 0.0 collective-permute-done.4.arrived
  19.0 1.0 %collective-permute-start.5 = (bf16[24,2048]{1,0:T(8,128)(2,1)S(1)}, bf16[24,2048]{1,0:T(8,128)(2,1)S(1)}, u32[]{:S(2)}, u32[]{:S(2)}) collective-permute-start(bf16[24,2048]{1,0:T(8,128)(2,1)S(1)} %join_cores.2), channel_id=1, source_target_pairs={{0,2},{1,3},{2,0},{3,1},{4,6},{5,7},{6,4},{7,5},{8,10},{9,11},{10,... | collective-permute-start | bytes 294920 | tf_op jit(solution)/shard_map/ppermute | solution.py:262
  20.1 2.6 %collective-permute-done.7.joined = bf16[24,2048]{1,0:T(8,128)(2,1)S(1)} collective-permute-done((bf16[24,2048]{1,0:T(8,128)(2,1)S(1)}, bf16[24,2048]{1,0:T(8,128)(2,1)S(1)}, u32[]{:S(2)}, u32[]{:S(2)}) %collective-permute-start.7) | collective-permute-done | bytes 98336 | tf_op jit(solution)/shard_map/ppermute | solution.py:262
  22.6 0.7 %add_layers.2.refs_0_ = bf16[24,4096]{1,0:T(8,128)(2,1)} custom-call(f32[24,2048]{1,0:T(8,128)S(1)} %get-tuple-element.20.own, bf16[48,2048]{1,0:T(8,128)(2,1)S(1)} %collective-permute-done.6.arrived, bf16[24,2048]{1,0:T(8,128)(2,1)S(1)} %collective-permute-done.7.joined), custom_call_target="tpu_custom_call" | custom-call | flops 98304 | bytes 1048576 | tf_op jit(solution)/shard_map/add_layers/pallas_call | solution.py:341
  23.3 0.8 %collective-permute-done.5.joined = bf16[24,2048]{1,0:T(8,128)(2,1)S(1)} collective-permute-done((bf16[24,2048]{1,0:T(8,128)(2,1)S(1)}, bf16[24,2048]{1,0:T(8,128)(2,1)S(1)}, u32[]{:S(2)}, u32[]{:S(2)}) %collective-permute-start.5) | collective-permute-done | bytes 98336 | tf_op jit(solution)/shard_map/ppermute | solution.py:262
  24.2 0.7 %add_layers.3 = bf16[24,4096]{1,0:T(8,128)(2,1)} custom-call(f32[24,2048]{1,0:T(8,128)S(1)} %get-tuple-element.17.own, bf16[48,2048]{1,0:T(8,128)(2,1)S(1)} %collective-permute-done.4.arrived, bf16[24,2048]{1,0:T(8,128)(2,1)S(1)} %collective-permute-done.5.joined, bf16[24,4096]{1,0:T(8,128)(2,1)} %add_layers.2.refs_0_), custom_call_target="tpu_custom_call", output_to_operand_aliasing={{}: (3, {})} | custom-call | flops 98304 | bytes 1048576 | tf_op jit(solution)/shard_map/add_layers/pallas_call | solution.py:341
  (10 shorter events, 0.1 us)
Async XLA Ops:
  0.0 12.2 %collective-permute-start.1 = (bf16[16,4096]{1,0:T(8,128)(2,1)}, bf16[16,4096]{1,0:T(8,128)(2,1)S(1)}, u32[]{:S(2)}, u32[]{:S(2)}) collective-permute-start(bf16[16,4096]{1,0:T(8,128)(2,1)} %bitcast.7), channel_id=1, source_target_pairs={{0,16},{8,24},{16,0},{24,8},{1,17},{9,25},{17,1},{25,9},{2,18},{10... | collective-permute-start | bytes 393224 | tf_op jit(solution)/shard_map/ppermute | solution.py:262
  4.0 8.2 %collective-permute-start.2 = (bf16[16,4096]{1,0:T(8,128)(2,1)}, bf16[16,4096]{1,0:T(8,128)(2,1)S(1)}, u32[]{:S(2)}, u32[]{:S(2)}) collective-permute-start(bf16[16,4096]{1,0:T(8,128)(2,1)} %bitcast.8), channel_id=1, source_target_pairs={{0,8},{8,0},{16,24},{24,16},{1,9},{9,1},{17,25},{25,17},{2,10},{10... | collective-permute-start | bytes 393224 | tf_op jit(solution)/shard_map/ppermute | solution.py:262
  5.6 9.0 %collective-permute-start.3 = (bf16[16,4096]{1,0:T(8,128)(2,1)}, bf16[16,4096]{1,0:T(8,128)(2,1)S(1)}, u32[]{:S(2)}, u32[]{:S(2)}) collective-permute-start(bf16[16,4096]{1,0:T(8,128)(2,1)} %bitcast.9), channel_id=1, source_target_pairs={{0,24},{8,16},{16,8},{24,0},{1,25},{9,17},{17,9},{25,1},{2,26},{10... | collective-permute-start | bytes 393224 | tf_op jit(solution)/shard_map/ppermute | solution.py:262
  5.6 2.6 %copy-start = (s32[1,1,1,768]{3,2,1,0:T(1,128)S(1)}, s32[1,1,1,768]{3,2,1,0:T(1,128)}, u32[]{:S(2)}) copy-start(s32[1,1,1,768]{3,2,1,0:T(1,128)} %param.6) | copy-start | bytes 9220
  5.6 2.6 %copy-start.1 = (s32[1,1,1,768]{3,2,1,0:T(1,128)S(1)}, s32[1,1,1,768]{3,2,1,0:T(1,128)}, u32[]{:S(2)}) copy-start(s32[1,1,1,768]{3,2,1,0:T(1,128)} %param.7) | copy-start | bytes 9220
  5.6 4.5 %collective-permute-start = (bf16[8,4096]{1,0:T(8,128)(2,1)}, bf16[8,4096]{1,0:T(8,128)(2,1)S(1)}, u32[]{:S(2)}, u32[]{:S(2)}) collective-permute-start(bf16[8,4096]{1,0:T(8,128)(2,1)} %bitcast.11), channel_id=1, source_target_pairs={{0,4},{4,0},{1,5},{5,1},{2,6},{6,2},{3,7},{7,3},{8,12},{12,8},{9,1... | collective-permute-start | bytes 196616 | tf_op jit(solution)/shard_map/ppermute | solution.py:262
  7.3 0.9 %copy-start.2 = (bf16[1,1,1,16,4096]{4,3,2,1,0:T(8,128)(2,1)S(1)}, bf16[1,1,1,16,4096]{4,3,2,1,0:T(8,128)(2,1)}, u32[]{:S(2)}) copy-start(bf16[1,1,1,16,4096]{4,3,2,1,0:T(8,128)(2,1)} %param.5) | copy-start | bytes 393220
  8.2 1.9 %copy-start.3 = (bf16[1,1,1,8,4096]{4,3,2,1,0:T(8,128)(2,1)S(1)}, bf16[1,1,1,8,4096]{4,3,2,1,0:T(8,128)(2,1)}, u32[]{:S(2)}) copy-start(bf16[1,1,1,8,4096]{4,3,2,1,0:T(8,128)(2,1)} %param.4) | copy-start | bytes 196612
  15.5 1.5 %collective-permute-start.6 = (bf16[48,2048]{1,0:T(8,128)(2,1)S(1)}, bf16[48,2048]{1,0:T(8,128)(2,1)S(1)}, u32[]{:S(2)}, u32[]{:S(2)}) collective-permute-start(bf16[48,2048]{1,0:T(8,128)(2,1)S(1)} %get-tuple-element.21), channel_id=1, source_target_pairs={{0,1},{1,0},{2,3},{3,2},{4,5},{5,4},{6,7},{7,6},{8,9},{9,8},{10,11... | collective-permute-start | bytes 589832 | tf_op jit(solution)/shard_map/ppermute | solution.py:262
  16.5 2.5 %collective-permute-start.4 = (bf16[48,2048]{1,0:T(8,128)(2,1)S(1)}, bf16[48,2048]{1,0:T(8,128)(2,1)S(1)}, u32[]{:S(2)}, u32[]{:S(2)}) collective-permute-start(bf16[48,2048]{1,0:T(8,128)(2,1)S(1)} %get-tuple-element.18), channel_id=1, source_target_pairs={{0,1},{1,0},{2,3},{3,2},{4,5},{5,4},{6,7},{7,6},{8,9},{9,8},{10,11... | collective-permute-start | bytes 589832 | tf_op jit(solution)/shard_map/ppermute | solution.py:262
  17.1 5.6 %collective-permute-start.7 = (bf16[24,2048]{1,0:T(8,128)(2,1)S(1)}, bf16[24,2048]{1,0:T(8,128)(2,1)S(1)}, u32[]{:S(2)}, u32[]{:S(2)}) collective-permute-start(bf16[24,2048]{1,0:T(8,128)(2,1)S(1)} %join_cores.3), channel_id=1, source_target_pairs={{0,2},{1,3},{2,0},{3,1},{4,6},{5,7},{6,4},{7,5},{8,10},{9,11},{10,... | collective-permute-start | bytes 294920 | tf_op jit(solution)/shard_map/ppermute | solution.py:262
  19.0 5.2 %collective-permute-start.5 = (bf16[24,2048]{1,0:T(8,128)(2,1)S(1)}, bf16[24,2048]{1,0:T(8,128)(2,1)S(1)}, u32[]{:S(2)}, u32[]{:S(2)}) collective-permute-start(bf16[24,2048]{1,0:T(8,128)(2,1)S(1)} %join_cores.2), channel_id=1, source_target_pairs={{0,2},{1,3},{2,0},{3,1},{4,6},{5,7},{6,4},{7,5},{8,10},{9,11},{10,... | collective-permute-start | bytes 294920 | tf_op jit(solution)/shard_map/ppermute | solution.py:262

commit v12 on v10

--- a/solution.py
+++ b/solution.py
@@ -288,7 +288,7 @@
     )(a_index, b_index)
 
     groups = (2,) if pairs * FLAT * 2 < 4 * MIB else (1, 1)
-    raw = shape((right_each * LINES, LANES), F32)
+    raw = shape((right_each * (LINES + 1), LANES), F32)
     one = shape((LINES, pairs, LANES), BF16)
     shard_flops = 2 * pairs * LINES * LANES * LANES + 2 * pairs * tiles * FLAT
     acc, a_lines = call(

time: 24.9 us -> 24.9 us (level)
  transfers between devices with their start and end apart: 8 -> 8, of which waited for: 6 -> 6; matrix products, arithmetic and copies ran while one was open for 0% -> 0% of each run, Pallas kernels for 21% -> 22%
where the time goes in v12:
time: 24.9 us; the launch traced here: 24.7 us
  starting transfers between devices  10.7 us (43%)
  Pallas kernels  6.77 us (27%)
  waiting for transfers between devices  6.19 us (25%)
  local copies, waits for them, and re-layouts  0.91 us (4%)
    ppermute x8, starting transfers between devices, exchange(): return lax.ppermute(x, axis, [(i, i ^ q) for i in range(size)])  10.7 us
    ppermute x8, waiting for transfers between devices, exchange(): return lax.ppermute(x, axis, [(i, i ^ q) for i in range(size)])  6.19 us
    pallas_call x1, Pallas kernels, shards(): call(functools.partial(more_kernel, pairs, groups), [shape((tiles, FLAT),...  2.04 us
    pallas_call x2, Pallas kernels, shards(): call(functools.partial(last_kernel, 3 * pairs, first_line), outs, ([] if...  1.43 us
    pallas_call x2, Pallas kernels, shards(): call(functools.partial(add_kernel, column), [shape((owned, FLAT), BF16)],...  1.37 us
    pallas_call x1, Pallas kernels, shards(): call(functools.partial(own_kernel, (1,), len(a_parts)), [shape((tiles, FL...  1.15 us
    unnamed x8, local copies, waits for them, and re-layouts  0.91 us
    pallas_call x1, Pallas kernels, shards(): call(functools.partial(counts_kernel, cols == 2, left_tiles, left_each, r...  0.73 us
  transfers between devices with their start and end apart: 8, of which 6 were waited for; matrix products, arithmetic and copies ran while one was open for 0% of the time, Pallas kernels for 22%

profile of v12, /device:TPU:0, one launch (start us, length us, event | category | flops | bytes accessed | tf_op | source)
XLA Modules:
  0.0 24.7 jit_solution(8018208585385092054)
XLA Ops:
  0.0 4.0 %collective-permute-start.1 = (bf16[16,4096]{1,0:T(8,128)(2,1)}, bf16[16,4096]{1,0:T(8,128)(2,1)S(1)}, u32[]{:S(2)}, u32[]{:S(2)}) collective-permute-start(bf16[16,4096]{1,0:T(8,128)(2,1)} %bitcast.7), channel_id=1, source_target_pairs={{0,16},{8,24},{16,0},{24,8},{1,17},{9,25},{17,1},{25,9},{2,18},{10... | collective-permute-start | bytes 393224 | tf_op jit(solution)/shard_map/ppermute | solution.py:256
  4.0 1.6 %collective-permute-start.2 = (bf16[16,4096]{1,0:T(8,128)(2,1)}, bf16[16,4096]{1,0:T(8,128)(2,1)S(1)}, u32[]{:S(2)}, u32[]{:S(2)}) collective-permute-start(bf16[16,4096]{1,0:T(8,128)(2,1)} %bitcast.8), channel_id=1, source_target_pairs={{0,8},{8,0},{16,24},{24,16},{1,9},{9,1},{17,25},{25,17},{2,10},{10... | collective-permute-start | bytes 393224 | tf_op jit(solution)/shard_map/ppermute | solution.py:256
  5.6 0.0 collective-permute-start.3
  5.6 1.7 %collective-permute-start = (bf16[8,4096]{1,0:T(8,128)(2,1)}, bf16[8,4096]{1,0:T(8,128)(2,1)S(1)}, u32[]{:S(2)}, u32[]{:S(2)}) collective-permute-start(bf16[8,4096]{1,0:T(8,128)(2,1)} %bitcast.11), channel_id=1, source_target_pairs={{0,4},{4,0},{1,5},{5,1},{2,6},{6,2},{3,7},{7,3},{8,12},{12,8},{9,1... | collective-permute-start | bytes 196616 | tf_op jit(solution)/shard_map/ppermute | solution.py:256
  7.3 0.9 %copy-done.2 = bf16[1,1,1,16,4096]{4,3,2,1,0:T(8,128)(2,1)S(1)} copy-done((bf16[1,1,1,16,4096]{4,3,2,1,0:T(8,128)(2,1)S(1)}, bf16[1,1,1,16,4096]{4,3,2,1,0:T(8,128)(2,1)}, u32[]{:S(2)}) %copy-start.2) | copy-done | bytes 131096
  8.3 0.7 %counts.1.sel = bf16[96,1024]{1,0:T(8,128)(2,1)S(1)} custom-call(s32[1,768]{1,0:T(1,128)S(1)} %bitcast.5, s32[1,768]{1,0:T(1,128)S(1)} %bitcast.6), custom_call_target="tpu_custom_call" | custom-call | flops 1179648 | bytes 1048576 | tf_op jit(solution)/shard_map/counts/pallas_call | solution.py:280
  9.0 1.1 %collective-permute-done.refs_1_ = bf16[8,4096]{1,0:T(8,128)(2,1)S(1)} collective-permute-done((bf16[8,4096]{1,0:T(8,128)(2,1)}, bf16[8,4096]{1,0:T(8,128)(2,1)S(1)}, u32[]{:S(2)}, u32[]{:S(2)}) %collective-permute-start) | collective-permute-done | bytes 65568 | tf_op jit(solution)/shard_map/ppermute | solution.py:256
  10.1 1.2 %own_shard.1 = (f32[96,4096]{1,0:T(8,128)S(1)}, bf16[512,128]{1,0:T(8,128)(2,1)S(1)}) custom-call(bf16[96,1024]{1,0:T(8,128)(2,1)S(1)} %counts.1.sel, bf16[8,4096]{1,0:T(8,128)(2,1)S(1)} %bitcast.12, bf16[8,4096]{1,0:T(8,128)(2,1)S(1)} %collective-permute-done.refs_1_, bf16[16,4096]{1,0:T(8,128)(2,1)S(1)} %stage.1.refs_2_), custom_call_target="tpu_custom_call" | custom-call | flops 500000000 | bytes 4194304 | tf_op jit(solution)/shard_map/own_shard/pallas_call | solution.py:294
  11.3 0.9 %collective-permute-done.1.refs_0_ = bf16[16,4096]{1,0:T(8,128)(2,1)S(1)} collective-permute-done((bf16[16,4096]{1,0:T(8,128)(2,1)}, bf16[16,4096]{1,0:T(8,128)(2,1)S(1)}, u32[]{:S(2)}, u32[]{:S(2)}) %collective-permute-start.1) | collective-permute-done | bytes 131104 | tf_op jit(solution)/shard_map/ppermute | solution.py:256
  12.2 0.0 collective-permute-done.2.refs_1_
  12.2 2.0 %near_and_far.1.acc = f32[96,4096]{1,0:T(8,128)S(1)} custom-call(bf16[96,1024]{1,0:T(8,128)(2,1)S(1)} %counts.1.sel, bf16[512,128]{1,0:T(8,128)(2,1)S(1)} %get-tuple-element.14.a_lines, f32[96,4096]{1,0:T(8,128)S(1)} %get-tuple-element.15.acc, bf16[16,4096]{1,0:T(8,128)(2,1)S(1)} %collective-permute-done.1.refs_0_, ...), custom_call_target="tpu_custom_call" | custom-call | flops 939524096 | bytes 8388608 | tf_op jit(solution)/shard_map/near_and_far/pallas_call | solution.py:303
  14.2 0.3 %collective-permute-done.3.b_ref = bf16[16,4096]{1,0:T(8,128)(2,1)S(1)} collective-permute-done((bf16[16,4096]{1,0:T(8,128)(2,1)}, bf16[16,4096]{1,0:T(8,128)(2,1)S(1)}, u32[]{:S(2)}, u32[]{:S(2)}) %collective-permute-start.3) | collective-permute-done | bytes 131104 | tf_op jit(solution)/shard_map/ppermute | solution.py:256
  14.6 0.8 %last_shard.2 = (f32[24,2048]{1,0:T(8,128)S(1)}, f32[24,2048]{1,0:T(8,128)S(1)}, bf16[48,2048]{1,0:T(8,128)(2,1)S(1)}, bf16[128,2048]{1,0:T(8,128)(2,1)S(1)}) custom-call(bf16[96,1024]{1,0:T(8,128)(2,1)S(1)} %counts.1.sel, bf16[512,128]{1,0:T(8,128)(2,1)S(1)} %get-tuple-element.14.a_lines, f32[96,4096]{1,0:T(8,128)S(1)} %near_and_far.1.acc, ...), custom_call_target="tpu_custom_call" | custom-call | flops 234881024 | bytes 2097152 | tf_op jit(solution)/shard_map/last_shard/pallas_call | solution.py:318
  15.3 0.1 collective-permute-start.6
  15.4 0.7 %last_shard.3 = (f32[24,2048]{1,0:T(8,128)S(1)}, f32[24,2048]{1,0:T(8,128)S(1)}, bf16[48,2048]{1,0:T(8,128)(2,1)S(1)}) custom-call(bf16[96,1024]{1,0:T(8,128)(2,1)S(1)} %counts.1.sel, bf16[512,128]{1,0:T(8,128)(2,1)S(1)} %get-tuple-element.14.a_lines, f32[96,4096]{1,0:T(8,128)S(1)} %near_and_far.1.acc, bf16[16,4096]{1,0:T(8,128)(2,1)S(1)} %collective-permute-done.3.b_ref, ...), custom_call_target="tpu_custom_call" | custom-call | flops 234881024 | bytes 2097152 | tf_op jit(solution)/shard_map/last_shard/pallas_call | solution.py:318
  16.1 0.6 %collective-permute-start.4 = (bf16[48,2048]{1,0:T(8,128)(2,1)S(1)}, bf16[48,2048]{1,0:T(8,128)(2,1)S(1)}, u32[]{:S(2)}, u32[]{:S(2)}) collective-permute-start(bf16[48,2048]{1,0:T(8,128)(2,1)S(1)} %get-tuple-element.18), channel_id=1, source_target_pairs={{0,1},{1,0},{2,3},{3,2},{4,5},{5,4},{6,7},{7,6},{8,9},{9,8},{10,11... | collective-permute-start | bytes 589832 | tf_op jit(solution)/shard_map/ppermute | solution.py:256
  16.6 0.2 collective-permute-done.6.arrived
  16.9 1.9 %collective-permute-start.7 = (bf16[24,2048]{1,0:T(8,128)(2,1)S(1)}, bf16[24,2048]{1,0:T(8,128)(2,1)S(1)}, u32[]{:S(2)}, u32[]{:S(2)}) collective-permute-start(bf16[24,2048]{1,0:T(8,128)(2,1)S(1)} %join_cores.3), channel_id=1, source_target_pairs={{0,2},{1,3},{2,0},{3,1},{4,6},{5,7},{6,4},{7,5},{8,10},{9,11},{10,... | collective-permute-start | bytes 294920 | tf_op jit(solution)/shard_map/ppermute | solution.py:256
  18.8 0.0 collective-permute-done.4.arrived
  18.8 0.9 %collective-permute-start.5 = (bf16[24,2048]{1,0:T(8,128)(2,1)S(1)}, bf16[24,2048]{1,0:T(8,128)(2,1)S(1)}, u32[]{:S(2)}, u32[]{:S(2)}) collective-permute-start(bf16[24,2048]{1,0:T(8,128)(2,1)S(1)} %join_cores.2), channel_id=1, source_target_pairs={{0,2},{1,3},{2,0},{3,1},{4,6},{5,7},{6,4},{7,5},{8,10},{9,11},{10,... | collective-permute-start | bytes 294920 | tf_op jit(solution)/shard_map/ppermute | solution.py:256
  19.7 2.8 %collective-permute-done.7.joined = bf16[24,2048]{1,0:T(8,128)(2,1)S(1)} collective-permute-done((bf16[24,2048]{1,0:T(8,128)(2,1)S(1)}, bf16[24,2048]{1,0:T(8,128)(2,1)S(1)}, u32[]{:S(2)}, u32[]{:S(2)}) %collective-permute-start.7) | collective-permute-done | bytes 98336 | tf_op jit(solution)/shard_map/ppermute | solution.py:256
  22.5 0.7 %add_layers.2.refs_0_ = bf16[24,4096]{1,0:T(8,128)(2,1)} custom-call(f32[24,2048]{1,0:T(8,128)S(1)} %get-tuple-element.20.own, bf16[48,2048]{1,0:T(8,128)(2,1)S(1)} %collective-permute-done.6.arrived, bf16[24,2048]{1,0:T(8,128)(2,1)S(1)} %collective-permute-done.7.joined), custom_call_target="tpu_custom_call" | custom-call | flops 98304 | bytes 1048576 | tf_op jit(solution)/shard_map/add_layers/pallas_call | solution.py:335
  23.2 0.8 %collective-permute-done.5.joined = bf16[24,2048]{1,0:T(8,128)(2,1)S(1)} collective-permute-done((bf16[24,2048]{1,0:T(8,128)(2,1)S(1)}, bf16[24,2048]{1,0:T(8,128)(2,1)S(1)}, u32[]{:S(2)}, u32[]{:S(2)}) %collective-permute-start.5) | collective-permute-done | bytes 98336 | tf_op jit(solution)/shard_map/ppermute | solution.py:256
  24.0 0.7 %add_layers.3 = bf16[24,4096]{1,0:T(8,128)(2,1)} custom-call(f32[24,2048]{1,0:T(8,128)S(1)} %get-tuple-element.17.own, bf16[48,2048]{1,0:T(8,128)(2,1)S(1)} %collective-permute-done.4.arrived, bf16[24,2048]{1,0:T(8,128)(2,1)S(1)} %collective-permute-done.5.joined, bf16[24,4096]{1,0:T(8,128)(2,1)} %add_layers.2.refs_0_), custom_call_target="tpu_custom_call", output_to_operand_aliasing={{}: (3, {})} | custom-call | flops 98304 | bytes 1048576 | tf_op jit(solution)/shard_map/add_layers/pallas_call | solution.py:335
  (10 shorter events, 0.1 us)
Async XLA Ops:
  0.0 12.2 %collective-permute-start.1 = (bf16[16,4096]{1,0:T(8,128)(2,1)}, bf16[16,4096]{1,0:T(8,128)(2,1)S(1)}, u32[]{:S(2)}, u32[]{:S(2)}) collective-permute-start(bf16[16,4096]{1,0:T(8,128)(2,1)} %bitcast.7), channel_id=1, source_target_pairs={{0,16},{8,24},{16,0},{24,8},{1,17},{9,25},{17,1},{25,9},{2,18},{10... | collective-permute-start | bytes 393224 | tf_op jit(solution)/shard_map/ppermute | solution.py:256
  4.0 8.2 %collective-permute-start.2 = (bf16[16,4096]{1,0:T(8,128)(2,1)}, bf16[16,4096]{1,0:T(8,128)(2,1)S(1)}, u32[]{:S(2)}, u32[]{:S(2)}) collective-permute-start(bf16[16,4096]{1,0:T(8,128)(2,1)} %bitcast.8), channel_id=1, source_target_pairs={{0,8},{8,0},{16,24},{24,16},{1,9},{9,1},{17,25},{25,17},{2,10},{10... | collective-permute-start | bytes 393224 | tf_op jit(solution)/shard_map/ppermute | solution.py:256
  5.6 9.0 %collective-permute-start.3 = (bf16[16,4096]{1,0:T(8,128)(2,1)}, bf16[16,4096]{1,0:T(8,128)(2,1)S(1)}, u32[]{:S(2)}, u32[]{:S(2)}) collective-permute-start(bf16[16,4096]{1,0:T(8,128)(2,1)} %bitcast.9), channel_id=1, source_target_pairs={{0,24},{8,16},{16,8},{24,0},{1,25},{9,17},{17,9},{25,1},{2,26},{10... | collective-permute-start | bytes 393224 | tf_op jit(solution)/shard_map/ppermute | solution.py:256
  5.6 2.6 %copy-start = (s32[1,1,1,768]{3,2,1,0:T(1,128)S(1)}, s32[1,1,1,768]{3,2,1,0:T(1,128)}, u32[]{:S(2)}) copy-start(s32[1,1,1,768]{3,2,1,0:T(1,128)} %param.6) | copy-start | bytes 9220
  5.6 2.6 %copy-start.1 = (s32[1,1,1,768]{3,2,1,0:T(1,128)S(1)}, s32[1,1,1,768]{3,2,1,0:T(1,128)}, u32[]{:S(2)}) copy-start(s32[1,1,1,768]{3,2,1,0:T(1,128)} %param.7) | copy-start | bytes 9220
  5.6 4.5 %collective-permute-start = (bf16[8,4096]{1,0:T(8,128)(2,1)}, bf16[8,4096]{1,0:T(8,128)(2,1)S(1)}, u32[]{:S(2)}, u32[]{:S(2)}) collective-permute-start(bf16[8,4096]{1,0:T(8,128)(2,1)} %bitcast.11), channel_id=1, source_target_pairs={{0,4},{4,0},{1,5},{5,1},{2,6},{6,2},{3,7},{7,3},{8,12},{12,8},{9,1... | collective-permute-start | bytes 196616 | tf_op jit(solution)/shard_map/ppermute | solution.py:256
  7.3 0.9 %copy-start.2 = (bf16[1,1,1,16,4096]{4,3,2,1,0:T(8,128)(2,1)S(1)}, bf16[1,1,1,16,4096]{4,3,2,1,0:T(8,128)(2,1)}, u32[]{:S(2)}) copy-start(bf16[1,1,1,16,4096]{4,3,2,1,0:T(8,128)(2,1)} %param.5) | copy-start | bytes 393220
  8.2 1.9 %copy-start.3 = (bf16[1,1,1,8,4096]{4,3,2,1,0:T(8,128)(2,1)S(1)}, bf16[1,1,1,8,4096]{4,3,2,1,0:T(8,128)(2,1)}, u32[]{:S(2)}) copy-start(bf16[1,1,1,8,4096]{4,3,2,1,0:T(8,128)(2,1)} %param.4) | copy-start | bytes 196612
  15.3 1.5 %collective-permute-start.6 = (bf16[48,2048]{1,0:T(8,128)(2,1)S(1)}, bf16[48,2048]{1,0:T(8,128)(2,1)S(1)}, u32[]{:S(2)}, u32[]{:S(2)}) collective-permute-start(bf16[48,2048]{1,0:T(8,128)(2,1)S(1)} %get-tuple-element.21), channel_id=1, source_target_pairs={{0,1},{1,0},{2,3},{3,2},{4,5},{5,4},{6,7},{7,6},{8,9},{9,8},{10,11... | collective-permute-start | bytes 589832 | tf_op jit(solution)/shard_map/ppermute | solution.py:256
  16.1 2.7 %collective-permute-start.4 = (bf16[48,2048]{1,0:T(8,128)(2,1)S(1)}, bf16[48,2048]{1,0:T(8,128)(2,1)S(1)}, u32[]{:S(2)}, u32[]{:S(2)}) collective-permute-start(bf16[48,2048]{1,0:T(8,128)(2,1)S(1)} %get-tuple-element.18), channel_id=1, source_target_pairs={{0,1},{1,0},{2,3},{3,2},{4,5},{5,4},{6,7},{7,6},{8,9},{9,8},{10,11... | collective-permute-start | bytes 589832 | tf_op jit(solution)/shard_map/ppermute | solution.py:256
  16.9 5.6 %collective-permute-start.7 = (bf16[24,2048]{1,0:T(8,128)(2,1)S(1)}, bf16[24,2048]{1,0:T(8,128)(2,1)S(1)}, u32[]{:S(2)}, u32[]{:S(2)}) collective-permute-start(bf16[24,2048]{1,0:T(8,128)(2,1)S(1)} %join_cores.3), channel_id=1, source_target_pairs={{0,2},{1,3},{2,0},{3,1},{4,6},{5,7},{6,4},{7,5},{8,10},{9,11},{10,... | collective-permute-start | bytes 294920 | tf_op jit(solution)/shard_map/ppermute | solution.py:256
  18.8 5.2 %collective-permute-start.5 = (bf16[24,2048]{1,0:T(8,128)(2,1)S(1)}, bf16[24,2048]{1,0:T(8,128)(2,1)S(1)}, u32[]{:S(2)}, u32[]{:S(2)}) collective-permute-start(bf16[24,2048]{1,0:T(8,128)(2,1)S(1)} %join_cores.2), channel_id=1, source_target_pairs={{0,2},{1,3},{2,0},{3,1},{4,6},{5,7},{6,4},{7,5},{8,10},{9,11},{10,... | collective-permute-start | bytes 294920 | tf_op jit(solution)/shard_map/ppermute | solution.py:256

commit v13 on v12

--- a/solution.py
+++ b/solution.py
@@ -14,8 +14,8 @@
 LINES = FLAT // LANES
 ROWS_AT_ONCE = 512
 FIRST_LINES = LINES // 2
-TILES_AT_ONCE = 4
-LINES_AT_ONCE = 4
+TILES_AT_ONCE = 8
+LINES_AT_ONCE = 8
 MIB = 1 << 20
 OWN_FLOPS = 500 * 10**6
 STAGE_FLOPS = 2 * 10**9

time: 24.9 us -> 24.9 us (level)
  no operation moved by 1% of the time
where the time goes in v13:
time: 24.9 us; the launch traced here: 24.6 us
  starting transfers between devices  10.7 us (43%)
  Pallas kernels  6.76 us (27%)
  waiting for transfers between devices  6.21 us (25%)
  local copies, waits for them, and re-layouts  0.91 us (4%)
    ppermute x8, starting transfers between devices, exchange(): return lax.ppermute(x, axis, [(i, i ^ q) for i in range(size)])  10.7 us
    ppermute x8, waiting for transfers between devices, exchange(): return lax.ppermute(x, axis, [(i, i ^ q) for i in range(size)])  6.21 us
    pallas_call x1, Pallas kernels, shards(): call(functools.partial(more_kernel, pairs, groups), [shape((tiles, FLAT),...  2.02 us
    pallas_call x2, Pallas kernels, shards(): call(functools.partial(last_kernel, 3 * pairs, first_line), outs, ([] if...  1.43 us
    pallas_call x2, Pallas kernels, shards(): call(functools.partial(add_kernel, column), [shape((owned, FLAT), BF16)],...  1.37 us
    pallas_call x1, Pallas kernels, shards(): call(functools.partial(own_kernel, (1,), len(a_parts)), [shape((tiles, FL...  1.16 us
    unnamed x8, local copies, waits for them, and re-layouts  0.91 us
    pallas_call x1, Pallas kernels, shards(): call(functools.partial(counts_kernel, cols == 2, left_tiles, left_each, r...  0.73 us
  transfers between devices with their start and end apart: 8, of which 6 were waited for; matrix products, arithmetic and copies ran while one was open for 0% of the time, Pallas kernels for 22%

profile of v13, /device:TPU:0, one launch (start us, length us, event | category | flops | bytes accessed | tf_op | source)
XLA Modules:
  0.0 24.6 jit_solution(9049912887702245638)
XLA Ops:
  0.0 4.0 %collective-permute-start.1 = (bf16[16,4096]{1,0:T(8,128)(2,1)}, bf16[16,4096]{1,0:T(8,128)(2,1)S(1)}, u32[]{:S(2)}, u32[]{:S(2)}) collective-permute-start(bf16[16,4096]{1,0:T(8,128)(2,1)} %bitcast.7), channel_id=1, source_target_pairs={{0,16},{8,24},{16,0},{24,8},{1,17},{9,25},{17,1},{25,9},{2,18},{10... | collective-permute-start | bytes 393224 | tf_op jit(solution)/shard_map/ppermute | solution.py:256
  4.0 1.6 %collective-permute-start.2 = (bf16[16,4096]{1,0:T(8,128)(2,1)}, bf16[16,4096]{1,0:T(8,128)(2,1)S(1)}, u32[]{:S(2)}, u32[]{:S(2)}) collective-permute-start(bf16[16,4096]{1,0:T(8,128)(2,1)} %bitcast.8), channel_id=1, source_target_pairs={{0,8},{8,0},{16,24},{24,16},{1,9},{9,1},{17,25},{25,17},{2,10},{10... | collective-permute-start | bytes 393224 | tf_op jit(solution)/shard_map/ppermute | solution.py:256
  5.6 0.0 collective-permute-start.3
  5.6 1.7 %collective-permute-start = (bf16[8,4096]{1,0:T(8,128)(2,1)}, bf16[8,4096]{1,0:T(8,128)(2,1)S(1)}, u32[]{:S(2)}, u32[]{:S(2)}) collective-permute-start(bf16[8,4096]{1,0:T(8,128)(2,1)} %bitcast.11), channel_id=1, source_target_pairs={{0,4},{4,0},{1,5},{5,1},{2,6},{6,2},{3,7},{7,3},{8,12},{12,8},{9,1... | collective-permute-start | bytes 196616 | tf_op jit(solution)/shard_map/ppermute | solution.py:256
  7.3 0.9 %copy-done.2 = bf16[1,1,1,16,4096]{4,3,2,1,0:T(8,128)(2,1)S(1)} copy-done((bf16[1,1,1,16,4096]{4,3,2,1,0:T(8,128)(2,1)S(1)}, bf16[1,1,1,16,4096]{4,3,2,1,0:T(8,128)(2,1)}, u32[]{:S(2)}) %copy-start.2) | copy-done | bytes 131096
  8.3 0.7 %counts.1.sel = bf16[96,1024]{1,0:T(8,128)(2,1)S(1)} custom-call(s32[1,768]{1,0:T(1,128)S(1)} %bitcast.5, s32[1,768]{1,0:T(1,128)S(1)} %bitcast.6), custom_call_target="tpu_custom_call" | custom-call | flops 1179648 | bytes 1048576 | tf_op jit(solution)/shard_map/counts/pallas_call | solution.py:280
  9.0 1.1 %collective-permute-done.refs_1_ = bf16[8,4096]{1,0:T(8,128)(2,1)S(1)} collective-permute-done((bf16[8,4096]{1,0:T(8,128)(2,1)}, bf16[8,4096]{1,0:T(8,128)(2,1)S(1)}, u32[]{:S(2)}, u32[]{:S(2)}) %collective-permute-start) | collective-permute-done | bytes 65568 | tf_op jit(solution)/shard_map/ppermute | solution.py:256
  10.1 1.2 %own_shard.1 = (f32[96,4096]{1,0:T(8,128)S(1)}, bf16[512,128]{1,0:T(8,128)(2,1)S(1)}) custom-call(bf16[96,1024]{1,0:T(8,128)(2,1)S(1)} %counts.1.sel, bf16[8,4096]{1,0:T(8,128)(2,1)S(1)} %bitcast.12, bf16[8,4096]{1,0:T(8,128)(2,1)S(1)} %collective-permute-done.refs_1_, bf16[16,4096]{1,0:T(8,128)(2,1)S(1)} %stage.1.refs_2_), custom_call_target="tpu_custom_call" | custom-call | flops 500000000 | bytes 4194304 | tf_op jit(solution)/shard_map/own_shard/pallas_call | solution.py:294
  11.3 0.9 %collective-permute-done.1.refs_0_ = bf16[16,4096]{1,0:T(8,128)(2,1)S(1)} collective-permute-done((bf16[16,4096]{1,0:T(8,128)(2,1)}, bf16[16,4096]{1,0:T(8,128)(2,1)S(1)}, u32[]{:S(2)}, u32[]{:S(2)}) %collective-permute-start.1) | collective-permute-done | bytes 131104 | tf_op jit(solution)/shard_map/ppermute | solution.py:256
  12.2 0.0 collective-permute-done.2.refs_1_
  12.2 2.0 %near_and_far.1.acc = f32[96,4096]{1,0:T(8,128)S(1)} custom-call(bf16[96,1024]{1,0:T(8,128)(2,1)S(1)} %counts.1.sel, bf16[512,128]{1,0:T(8,128)(2,1)S(1)} %get-tuple-element.14.a_lines, f32[96,4096]{1,0:T(8,128)S(1)} %get-tuple-element.15.acc, bf16[16,4096]{1,0:T(8,128)(2,1)S(1)} %collective-permute-done.1.refs_0_, ...), custom_call_target="tpu_custom_call" | custom-call | flops 939524096 | bytes 8388608 | tf_op jit(solution)/shard_map/near_and_far/pallas_call | solution.py:303
  14.2 0.4 %collective-permute-done.3.b_ref = bf16[16,4096]{1,0:T(8,128)(2,1)S(1)} collective-permute-done((bf16[16,4096]{1,0:T(8,128)(2,1)}, bf16[16,4096]{1,0:T(8,128)(2,1)S(1)}, u32[]{:S(2)}, u32[]{:S(2)}) %collective-permute-start.3) | collective-permute-done | bytes 131104 | tf_op jit(solution)/shard_map/ppermute | solution.py:256
  14.6 0.8 %last_shard.2 = (f32[24,2048]{1,0:T(8,128)S(1)}, f32[24,2048]{1,0:T(8,128)S(1)}, bf16[48,2048]{1,0:T(8,128)(2,1)S(1)}, bf16[128,2048]{1,0:T(8,128)(2,1)S(1)}) custom-call(bf16[96,1024]{1,0:T(8,128)(2,1)S(1)} %counts.1.sel, bf16[512,128]{1,0:T(8,128)(2,1)S(1)} %get-tuple-element.14.a_lines, f32[96,4096]{1,0:T(8,128)S(1)} %near_and_far.1.acc, ...), custom_call_target="tpu_custom_call" | custom-call | flops 234881024 | bytes 2097152 | tf_op jit(solution)/shard_map/last_shard/pallas_call | solution.py:318
  15.3 0.1 collective-permute-start.6
  15.4 0.7 %last_shard.3 = (f32[24,2048]{1,0:T(8,128)S(1)}, f32[24,2048]{1,0:T(8,128)S(1)}, bf16[48,2048]{1,0:T(8,128)(2,1)S(1)}) custom-call(bf16[96,1024]{1,0:T(8,128)(2,1)S(1)} %counts.1.sel, bf16[512,128]{1,0:T(8,128)(2,1)S(1)} %get-tuple-element.14.a_lines, f32[96,4096]{1,0:T(8,128)S(1)} %near_and_far.1.acc, bf16[16,4096]{1,0:T(8,128)(2,1)S(1)} %collective-permute-done.3.b_ref, ...), custom_call_target="tpu_custom_call" | custom-call | flops 234881024 | bytes 2097152 | tf_op jit(solution)/shard_map/last_shard/pallas_call | solution.py:318
  16.1 0.6 %collective-permute-start.4 = (bf16[48,2048]{1,0:T(8,128)(2,1)S(1)}, bf16[48,2048]{1,0:T(8,128)(2,1)S(1)}, u32[]{:S(2)}, u32[]{:S(2)}) collective-permute-start(bf16[48,2048]{1,0:T(8,128)(2,1)S(1)} %get-tuple-element.18), channel_id=1, source_target_pairs={{0,1},{1,0},{2,3},{3,2},{4,5},{5,4},{6,7},{7,6},{8,9},{9,8},{10,11... | collective-permute-start | bytes 589832 | tf_op jit(solution)/shard_map/ppermute | solution.py:256
  16.7 0.2 collective-permute-done.6.arrived
  16.9 1.9 %collective-permute-start.7 = (bf16[24,2048]{1,0:T(8,128)(2,1)S(1)}, bf16[24,2048]{1,0:T(8,128)(2,1)S(1)}, u32[]{:S(2)}, u32[]{:S(2)}) collective-permute-start(bf16[24,2048]{1,0:T(8,128)(2,1)S(1)} %join_cores.3), channel_id=1, source_target_pairs={{0,2},{1,3},{2,0},{3,1},{4,6},{5,7},{6,4},{7,5},{8,10},{9,11},{10,... | collective-permute-start | bytes 294920 | tf_op jit(solution)/shard_map/ppermute | solution.py:256
  18.8 0.0 collective-permute-done.4.arrived
  18.8 0.9 %collective-permute-start.5 = (bf16[24,2048]{1,0:T(8,128)(2,1)S(1)}, bf16[24,2048]{1,0:T(8,128)(2,1)S(1)}, u32[]{:S(2)}, u32[]{:S(2)}) collective-permute-start(bf16[24,2048]{1,0:T(8,128)(2,1)S(1)} %join_cores.2), channel_id=1, source_target_pairs={{0,2},{1,3},{2,0},{3,1},{4,6},{5,7},{6,4},{7,5},{8,10},{9,11},{10,... | collective-permute-start | bytes 294920 | tf_op jit(solution)/shard_map/ppermute | solution.py:256
  19.6 2.8 %collective-permute-done.7.joined = bf16[24,2048]{1,0:T(8,128)(2,1)S(1)} collective-permute-done((bf16[24,2048]{1,0:T(8,128)(2,1)S(1)}, bf16[24,2048]{1,0:T(8,128)(2,1)S(1)}, u32[]{:S(2)}, u32[]{:S(2)}) %collective-permute-start.7) | collective-permute-done | bytes 98336 | tf_op jit(solution)/shard_map/ppermute | solution.py:256
  22.4 0.7 %add_layers.2.refs_0_ = bf16[24,4096]{1,0:T(8,128)(2,1)} custom-call(f32[24,2048]{1,0:T(8,128)S(1)} %get-tuple-element.20.own, bf16[48,2048]{1,0:T(8,128)(2,1)S(1)} %collective-permute-done.6.arrived, bf16[24,2048]{1,0:T(8,128)(2,1)S(1)} %collective-permute-done.7.joined), custom_call_target="tpu_custom_call" | custom-call | flops 98304 | bytes 1048576 | tf_op jit(solution)/shard_map/add_layers/pallas_call | solution.py:335
  23.1 0.8 %collective-permute-done.5.joined = bf16[24,2048]{1,0:T(8,128)(2,1)S(1)} collective-permute-done((bf16[24,2048]{1,0:T(8,128)(2,1)S(1)}, bf16[24,2048]{1,0:T(8,128)(2,1)S(1)}, u32[]{:S(2)}, u32[]{:S(2)}) %collective-permute-start.5) | collective-permute-done | bytes 98336 | tf_op jit(solution)/shard_map/ppermute | solution.py:256
  24.0 0.7 %add_layers.3 = bf16[24,4096]{1,0:T(8,128)(2,1)} custom-call(f32[24,2048]{1,0:T(8,128)S(1)} %get-tuple-element.17.own, bf16[48,2048]{1,0:T(8,128)(2,1)S(1)} %collective-permute-done.4.arrived, bf16[24,2048]{1,0:T(8,128)(2,1)S(1)} %collective-permute-done.5.joined, bf16[24,4096]{1,0:T(8,128)(2,1)} %add_layers.2.refs_0_), custom_call_target="tpu_custom_call", output_to_operand_aliasing={{}: (3, {})} | custom-call | flops 98304 | bytes 1048576 | tf_op jit(solution)/shard_map/add_layers/pallas_call | solution.py:335
  (10 shorter events, 0.1 us)
Async XLA Ops:
  0.0 12.2 %collective-permute-start.1 = (bf16[16,4096]{1,0:T(8,128)(2,1)}, bf16[16,4096]{1,0:T(8,128)(2,1)S(1)}, u32[]{:S(2)}, u32[]{:S(2)}) collective-permute-start(bf16[16,4096]{1,0:T(8,128)(2,1)} %bitcast.7), channel_id=1, source_target_pairs={{0,16},{8,24},{16,0},{24,8},{1,17},{9,25},{17,1},{25,9},{2,18},{10... | collective-permute-start | bytes 393224 | tf_op jit(solution)/shard_map/ppermute | solution.py:256
  4.0 8.2 %collective-permute-start.2 = (bf16[16,4096]{1,0:T(8,128)(2,1)}, bf16[16,4096]{1,0:T(8,128)(2,1)S(1)}, u32[]{:S(2)}, u32[]{:S(2)}) collective-permute-start(bf16[16,4096]{1,0:T(8,128)(2,1)} %bitcast.8), channel_id=1, source_target_pairs={{0,8},{8,0},{16,24},{24,16},{1,9},{9,1},{17,25},{25,17},{2,10},{10... | collective-permute-start | bytes 393224 | tf_op jit(solution)/shard_map/ppermute | solution.py:256
  5.6 9.0 %collective-permute-start.3 = (bf16[16,4096]{1,0:T(8,128)(2,1)}, bf16[16,4096]{1,0:T(8,128)(2,1)S(1)}, u32[]{:S(2)}, u32[]{:S(2)}) collective-permute-start(bf16[16,4096]{1,0:T(8,128)(2,1)} %bitcast.9), channel_id=1, source_target_pairs={{0,24},{8,16},{16,8},{24,0},{1,25},{9,17},{17,9},{25,1},{2,26},{10... | collective-permute-start | bytes 393224 | tf_op jit(solution)/shard_map/ppermute | solution.py:256
  5.6 2.6 %copy-start = (s32[1,1,1,768]{3,2,1,0:T(1,128)S(1)}, s32[1,1,1,768]{3,2,1,0:T(1,128)}, u32[]{:S(2)}) copy-start(s32[1,1,1,768]{3,2,1,0:T(1,128)} %param.6) | copy-start | bytes 9220
  5.6 2.6 %copy-start.1 = (s32[1,1,1,768]{3,2,1,0:T(1,128)S(1)}, s32[1,1,1,768]{3,2,1,0:T(1,128)}, u32[]{:S(2)}) copy-start(s32[1,1,1,768]{3,2,1,0:T(1,128)} %param.7) | copy-start | bytes 9220
  5.6 4.5 %collective-permute-start = (bf16[8,4096]{1,0:T(8,128)(2,1)}, bf16[8,4096]{1,0:T(8,128)(2,1)S(1)}, u32[]{:S(2)}, u32[]{:S(2)}) collective-permute-start(bf16[8,4096]{1,0:T(8,128)(2,1)} %bitcast.11), channel_id=1, source_target_pairs={{0,4},{4,0},{1,5},{5,1},{2,6},{6,2},{3,7},{7,3},{8,12},{12,8},{9,1... | collective-permute-start | bytes 196616 | tf_op jit(solution)/shard_map/ppermute | solution.py:256
  7.3 0.9 %copy-start.2 = (bf16[1,1,1,16,4096]{4,3,2,1,0:T(8,128)(2,1)S(1)}, bf16[1,1,1,16,4096]{4,3,2,1,0:T(8,128)(2,1)}, u32[]{:S(2)}) copy-start(bf16[1,1,1,16,4096]{4,3,2,1,0:T(8,128)(2,1)} %param.5) | copy-start | bytes 393220
  8.2 1.9 %copy-start.3 = (bf16[1,1,1,8,4096]{4,3,2,1,0:T(8,128)(2,1)S(1)}, bf16[1,1,1,8,4096]{4,3,2,1,0:T(8,128)(2,1)}, u32[]{:S(2)}) copy-start(bf16[1,1,1,8,4096]{4,3,2,1,0:T(8,128)(2,1)} %param.4) | copy-start | bytes 196612
  15.3 1.5 %collective-permute-start.6 = (bf16[48,2048]{1,0:T(8,128)(2,1)S(1)}, bf16[48,2048]{1,0:T(8,128)(2,1)S(1)}, u32[]{:S(2)}, u32[]{:S(2)}) collective-permute-start(bf16[48,2048]{1,0:T(8,128)(2,1)S(1)} %get-tuple-element.21), channel_id=1, source_target_pairs={{0,1},{1,0},{2,3},{3,2},{4,5},{5,4},{6,7},{7,6},{8,9},{9,8},{10,11... | collective-permute-start | bytes 589832 | tf_op jit(solution)/shard_map/ppermute | solution.py:256
  16.1 2.7 %collective-permute-start.4 = (bf16[48,2048]{1,0:T(8,128)(2,1)S(1)}, bf16[48,2048]{1,0:T(8,128)(2,1)S(1)}, u32[]{:S(2)}, u32[]{:S(2)}) collective-permute-start(bf16[48,2048]{1,0:T(8,128)(2,1)S(1)} %get-tuple-element.18), channel_id=1, source_target_pairs={{0,1},{1,0},{2,3},{3,2},{4,5},{5,4},{6,7},{7,6},{8,9},{9,8},{10,11... | collective-permute-start | bytes 589832 | tf_op jit(solution)/shard_map/ppermute | solution.py:256
  16.9 5.6 %collective-permute-start.7 = (bf16[24,2048]{1,0:T(8,128)(2,1)S(1)}, bf16[24,2048]{1,0:T(8,128)(2,1)S(1)}, u32[]{:S(2)}, u32[]{:S(2)}) collective-permute-start(bf16[24,2048]{1,0:T(8,128)(2,1)S(1)} %join_cores.3), channel_id=1, source_target_pairs={{0,2},{1,3},{2,0},{3,1},{4,6},{5,7},{6,4},{7,5},{8,10},{9,11},{10,... | collective-permute-start | bytes 294920 | tf_op jit(solution)/shard_map/ppermute | solution.py:256
  18.8 5.2 %collective-permute-start.5 = (bf16[24,2048]{1,0:T(8,128)(2,1)S(1)}, bf16[24,2048]{1,0:T(8,128)(2,1)S(1)}, u32[]{:S(2)}, u32[]{:S(2)}) collective-permute-start(bf16[24,2048]{1,0:T(8,128)(2,1)S(1)} %join_cores.2), channel_id=1, source_target_pairs={{0,2},{1,3},{2,0},{3,1},{4,6},{5,7},{6,4},{7,5},{8,10},{9,11},{10,... | collective-permute-start | bytes 294920 | tf_op jit(solution)/shard_map/ppermute | solution.py:256

commit v14 on v13

--- a/solution.py
+++ b/solution.py
@@ -275,7 +275,7 @@
     else:
         a_parts = [lax.all_gather(a_local, "col", axis=0, tiled=True)]
     (b_here,) = call(stage_kernel, [shape(b_local.shape, BF16)], [], 1, "stage", STAGE_FLOPS, MIB)(b_local)
-    b_near = exchange(b_local, "row", 1)
+    b_near = exchange(b_here, "row", 1)
     b_last = exchange(b_local, "row", 3)
     (sel,) = call(
         functools.partial(counts_kernel, cols == 2, left_tiles, left_each, right_each),

time: 24.9 us -> 28.9 us (1.16)
  waiting for transfers between devices: 6.21 us -> 10.5 us
  Pallas kernels: 6.76 us -> 7.69 us
  local copies, waits for them, and re-layouts: 0.91 us -> 0.01 us
    ppermute x8, waiting for transfers between devices: 6.21 us -> 10.5 us  [exchange(): return lax.ppermute(x, axis, [(i, i ^ q) for i in range(size)])]
    pallas_call x1, Pallas kernels: 0.01 us -> 0.94 us  [shards(): call(stage_kernel, [shape(b_local.shape, BF16)], [], 1, 'stage', STAGE_FL...]
    unnamed x8 -> x6, local copies, waits for them, and re-layouts: 0.91 us -> 0.01 us
  transfers between devices with their start and end apart: 8 -> 8, of which waited for: 6 -> 5; matrix products, arithmetic and copies ran while one was open for 0% -> 0% of each run, Pallas kernels for 22% -> 18%
where the time goes in v14:
time: 28.9 us; the launch traced here: 28.7 us
  starting transfers between devices  10.5 us (36%)
  waiting for transfers between devices  10.5 us (36%)
  Pallas kernels  7.69 us (27%)
    ppermute x8, waiting for transfers between devices, exchange(): return lax.ppermute(x, axis, [(i, i ^ q) for i in range(size)])  10.5 us
    ppermute x8, starting transfers between devices, exchange(): return lax.ppermute(x, axis, [(i, i ^ q) for i in range(size)])  10.5 us
    pallas_call x1, Pallas kernels, shards(): call(functools.partial(more_kernel, pairs, groups), [shape((tiles, FLAT),...  2.01 us
    pallas_call x2, Pallas kernels, shards(): call(functools.partial(last_kernel, 3 * pairs, first_line), outs, ([] if...  1.44 us
    pallas_call x2, Pallas kernels, shards(): call(functools.partial(add_kernel, column), [shape((owned, FLAT), BF16)],...  1.37 us
    pallas_call x1, Pallas kernels, shards(): call(functools.partial(own_kernel, (1,), len(a_parts)), [shape((tiles, FL...  1.15 us
    pallas_call x1, Pallas kernels, shards(): call(stage_kernel, [shape(b_local.shape, BF16)], [], 1, 'stage', STAGE_FL...  0.94 us
    pallas_call x1, Pallas kernels, shards(): call(functools.partial(counts_kernel, cols == 2, left_tiles, left_each, r...  0.73 us
  transfers between devices with their start and end apart: 8, of which 5 were waited for; matrix products, arithmetic and copies ran while one was open for 0% of the time, Pallas kernels for 18%

profile of v14, /device:TPU:0, one launch (start us, length us, event | category | flops | bytes accessed | tf_op | source)
XLA Modules:
  0.0 28.7 jit_solution(4597366715174040594)
XLA Ops:
  0.0 0.9 %stage.1.refs_2_ = bf16[16,4096]{1,0:T(8,128)(2,1)S(1)} custom-call(bf16[16,4096]{1,0:T(8,128)(2,1)} %bitcast.3.refs_0_), custom_call_target="tpu_custom_call" | custom-call | flops 2000000000 | bytes 1048576 | tf_op jit(solution)/shard_map/stage/pallas_call | solution.py:277
  1.0 3.1 %collective-permute-start.2 = (bf16[16,4096]{1,0:T(8,128)(2,1)S(1)}, bf16[16,4096]{1,0:T(8,128)(2,1)S(1)}, u32[]{:S(2)}, u32[]{:S(2)}) collective-permute-start(bf16[16,4096]{1,0:T(8,128)(2,1)S(1)} %stage.1.refs_2_), channel_id=1, source_target_pairs={{0,8},{8,0},{16,24},{24,16},{1,9},{9,1},{17,25},{25,17},{2,10},{10... | collective-permute-start | bytes 393224 | tf_op jit(solution)/shard_map/ppermute | solution.py:256
  4.0 2.6 %collective-permute-start.1 = (bf16[16,4096]{1,0:T(8,128)(2,1)}, bf16[16,4096]{1,0:T(8,128)(2,1)S(1)}, u32[]{:S(2)}, u32[]{:S(2)}) collective-permute-start(bf16[16,4096]{1,0:T(8,128)(2,1)} %bitcast.3.refs_0_), channel_id=1, source_target_pairs={{0,16},{8,24},{16,0},{24,8},{1,17},{9,25},{17,1},{25,9},{2,18},{10... | collective-permute-start | bytes 393224 | tf_op jit(solution)/shard_map/ppermute | solution.py:256
  6.6 1.5 %collective-permute-start = (bf16[8,4096]{1,0:T(8,128)(2,1)S(1)}, bf16[8,4096]{1,0:T(8,128)(2,1)S(1)}, u32[]{:S(2)}, u32[]{:S(2)}) collective-permute-start(bf16[8,4096]{1,0:T(8,128)(2,1)S(1)} %bitcast.7), channel_id=1, source_target_pairs={{0,4},{4,0},{1,5},{5,1},{2,6},{6,2},{3,7},{7,3},{8,12},{12,8},{9,1... | collective-permute-start | bytes 196616 | tf_op jit(solution)/shard_map/ppermute | solution.py:256
  8.1 0.2 collective-permute-start.3
  8.4 0.7 %counts.1.sel = bf16[96,1024]{1,0:T(8,128)(2,1)S(1)} custom-call(s32[1,768]{1,0:T(1,128)S(1)} %bitcast.5, s32[1,768]{1,0:T(1,128)S(1)} %bitcast.6), custom_call_target="tpu_custom_call" | custom-call | flops 1179648 | bytes 1048576 | tf_op jit(solution)/shard_map/counts/pallas_call | solution.py:280
  9.1 1.8 %collective-permute-done.refs_1_ = bf16[8,4096]{1,0:T(8,128)(2,1)S(1)} collective-permute-done((bf16[8,4096]{1,0:T(8,128)(2,1)S(1)}, bf16[8,4096]{1,0:T(8,128)(2,1)S(1)}, u32[]{:S(2)}, u32[]{:S(2)}) %collective-permute-start) | collective-permute-done | bytes 65568 | tf_op jit(solution)/shard_map/ppermute | solution.py:256
  10.9 1.2 %own_shard.1 = (f32[96,4096]{1,0:T(8,128)S(1)}, bf16[512,128]{1,0:T(8,128)(2,1)S(1)}) custom-call(bf16[96,1024]{1,0:T(8,128)(2,1)S(1)} %counts.1.sel, bf16[8,4096]{1,0:T(8,128)(2,1)S(1)} %bitcast.8, bf16[8,4096]{1,0:T(8,128)(2,1)S(1)} %collective-permute-done.refs_1_, bf16[16,4096]{1,0:T(8,128)(2,1)S(1)} %stage.1.refs_2_), custom_call_target="tpu_custom_call" | custom-call | flops 500000000 | bytes 4194304 | tf_op jit(solution)/shard_map/own_shard/pallas_call | solution.py:294
  12.1 0.0 collective-permute-done.2.refs_1_
  12.1 4.6 %collective-permute-done.1.refs_0_ = bf16[16,4096]{1,0:T(8,128)(2,1)S(1)} collective-permute-done((bf16[16,4096]{1,0:T(8,128)(2,1)}, bf16[16,4096]{1,0:T(8,128)(2,1)S(1)}, u32[]{:S(2)}, u32[]{:S(2)}) %collective-permute-start.1) | collective-permute-done | bytes 131104 | tf_op jit(solution)/shard_map/ppermute | solution.py:256
  16.7 2.0 %near_and_far.1.acc = f32[96,4096]{1,0:T(8,128)S(1)} custom-call(bf16[96,1024]{1,0:T(8,128)(2,1)S(1)} %counts.1.sel, bf16[512,128]{1,0:T(8,128)(2,1)S(1)} %get-tuple-element.14.a_lines, f32[96,4096]{1,0:T(8,128)S(1)} %get-tuple-element.15.acc, bf16[16,4096]{1,0:T(8,128)(2,1)S(1)} %collective-permute-done.1.refs_0_, ...), custom_call_target="tpu_custom_call" | custom-call | flops 939524096 | bytes 8388608 | tf_op jit(solution)/shard_map/near_and_far/pallas_call | solution.py:303
  18.7 0.0 collective-permute-done.3.b_ref
  18.7 0.8 %last_shard.2 = (f32[24,2048]{1,0:T(8,128)S(1)}, f32[24,2048]{1,0:T(8,128)S(1)}, bf16[48,2048]{1,0:T(8,128)(2,1)S(1)}, bf16[128,2048]{1,0:T(8,128)(2,1)S(1)}) custom-call(bf16[96,1024]{1,0:T(8,128)(2,1)S(1)} %counts.1.sel, bf16[512,128]{1,0:T(8,128)(2,1)S(1)} %get-tuple-element.14.a_lines, f32[96,4096]{1,0:T(8,128)S(1)} %near_and_far.1.acc, ...), custom_call_target="tpu_custom_call" | custom-call | flops 234881024 | bytes 2097152 | tf_op jit(solution)/shard_map/last_shard/pallas_call | solution.py:318
  19.5 0.1 collective-permute-start.6
  19.6 0.7 %last_shard.3 = (f32[24,2048]{1,0:T(8,128)S(1)}, f32[24,2048]{1,0:T(8,128)S(1)}, bf16[48,2048]{1,0:T(8,128)(2,1)S(1)}) custom-call(bf16[96,1024]{1,0:T(8,128)(2,1)S(1)} %counts.1.sel, bf16[512,128]{1,0:T(8,128)(2,1)S(1)} %get-tuple-element.14.a_lines, f32[96,4096]{1,0:T(8,128)S(1)} %near_and_far.1.acc, bf16[16,4096]{1,0:T(8,128)(2,1)S(1)} %collective-permute-done.3.b_ref, ...), custom_call_target="tpu_custom_call" | custom-call | flops 234881024 | bytes 2097152 | tf_op jit(solution)/shard_map/last_shard/pallas_call | solution.py:318
  20.3 0.6 %collective-permute-start.4 = (bf16[48,2048]{1,0:T(8,128)(2,1)S(1)}, bf16[48,2048]{1,0:T(8,128)(2,1)S(1)}, u32[]{:S(2)}, u32[]{:S(2)}) collective-permute-start(bf16[48,2048]{1,0:T(8,128)(2,1)S(1)} %get-tuple-element.18), channel_id=1, source_target_pairs={{0,1},{1,0},{2,3},{3,2},{4,5},{5,4},{6,7},{7,6},{8,9},{9,8},{10,11... | collective-permute-start | bytes 589832 | tf_op jit(solution)/shard_map/ppermute | solution.py:256
  20.8 0.2 collective-permute-done.6.arrived
  21.1 1.6 %collective-permute-start.7 = (bf16[24,2048]{1,0:T(8,128)(2,1)S(1)}, bf16[24,2048]{1,0:T(8,128)(2,1)S(1)}, u32[]{:S(2)}, u32[]{:S(2)}) collective-permute-start(bf16[24,2048]{1,0:T(8,128)(2,1)S(1)} %join_cores.3), channel_id=1, source_target_pairs={{0,2},{1,3},{2,0},{3,1},{4,6},{5,7},{6,4},{7,5},{8,10},{9,11},{10,... | collective-permute-start | bytes 294920 | tf_op jit(solution)/shard_map/ppermute | solution.py:256
  22.6 0.0 collective-permute-done.4.arrived
  22.7 0.9 %collective-permute-start.5 = (bf16[24,2048]{1,0:T(8,128)(2,1)S(1)}, bf16[24,2048]{1,0:T(8,128)(2,1)S(1)}, u32[]{:S(2)}, u32[]{:S(2)}) collective-permute-start(bf16[24,2048]{1,0:T(8,128)(2,1)S(1)} %join_cores.2), channel_id=1, source_target_pairs={{0,2},{1,3},{2,0},{3,1},{4,6},{5,7},{6,4},{7,5},{8,10},{9,11},{10,... | collective-permute-start | bytes 294920 | tf_op jit(solution)/shard_map/ppermute | solution.py:256
  23.5 3.2 %collective-permute-done.7.joined = bf16[24,2048]{1,0:T(8,128)(2,1)S(1)} collective-permute-done((bf16[24,2048]{1,0:T(8,128)(2,1)S(1)}, bf16[24,2048]{1,0:T(8,128)(2,1)S(1)}, u32[]{:S(2)}, u32[]{:S(2)}) %collective-permute-start.7) | collective-permute-done | bytes 98336 | tf_op jit(solution)/shard_map/ppermute | solution.py:256
  26.7 0.7 %add_layers.2.refs_0_ = bf16[24,4096]{1,0:T(8,128)(2,1)} custom-call(f32[24,2048]{1,0:T(8,128)S(1)} %get-tuple-element.20.own, bf16[48,2048]{1,0:T(8,128)(2,1)S(1)} %collective-permute-done.6.arrived, bf16[24,2048]{1,0:T(8,128)(2,1)S(1)} %collective-permute-done.7.joined), custom_call_target="tpu_custom_call" | custom-call | flops 98304 | bytes 1048576 | tf_op jit(solution)/shard_map/add_layers/pallas_call | solution.py:335
  27.4 0.6 %collective-permute-done.5.joined = bf16[24,2048]{1,0:T(8,128)(2,1)S(1)} collective-permute-done((bf16[24,2048]{1,0:T(8,128)(2,1)S(1)}, bf16[24,2048]{1,0:T(8,128)(2,1)S(1)}, u32[]{:S(2)}, u32[]{:S(2)}) %collective-permute-start.5) | collective-permute-done | bytes 98336 | tf_op jit(solution)/shard_map/ppermute | solution.py:256
  28.1 0.7 %add_layers.3 = bf16[24,4096]{1,0:T(8,128)(2,1)} custom-call(f32[24,2048]{1,0:T(8,128)S(1)} %get-tuple-element.17.own, bf16[48,2048]{1,0:T(8,128)(2,1)S(1)} %collective-permute-done.4.arrived, bf16[24,2048]{1,0:T(8,128)(2,1)S(1)} %collective-permute-done.5.joined, bf16[24,4096]{1,0:T(8,128)(2,1)} %add_layers.2.refs_0_), custom_call_target="tpu_custom_call", output_to_operand_aliasing={{}: (3, {})} | custom-call | flops 98304 | bytes 1048576 | tf_op jit(solution)/shard_map/add_layers/pallas_call | solution.py:335
  (8 shorter events, 0.1 us)
Async XLA Ops:
  0.0 6.6 %copy-start.2 = (bf16[1,1,1,8,4096]{4,3,2,1,0:T(8,128)(2,1)S(1)}, bf16[1,1,1,8,4096]{4,3,2,1,0:T(8,128)(2,1)}, u32[]{:S(2)}) copy-start(bf16[1,1,1,8,4096]{4,3,2,1,0:T(8,128)(2,1)} %param.4) | copy-start | bytes 196612
  0.0 8.4 %copy-start = (s32[1,1,1,768]{3,2,1,0:T(1,128)S(1)}, s32[1,1,1,768]{3,2,1,0:T(1,128)}, u32[]{:S(2)}) copy-start(s32[1,1,1,768]{3,2,1,0:T(1,128)} %param.6) | copy-start | bytes 9220
  0.0 8.4 %copy-start.1 = (s32[1,1,1,768]{3,2,1,0:T(1,128)S(1)}, s32[1,1,1,768]{3,2,1,0:T(1,128)}, u32[]{:S(2)}) copy-start(s32[1,1,1,768]{3,2,1,0:T(1,128)} %param.7) | copy-start | bytes 9220
  1.0 11.1 %collective-permute-start.2 = (bf16[16,4096]{1,0:T(8,128)(2,1)S(1)}, bf16[16,4096]{1,0:T(8,128)(2,1)S(1)}, u32[]{:S(2)}, u32[]{:S(2)}) collective-permute-start(bf16[16,4096]{1,0:T(8,128)(2,1)S(1)} %stage.1.refs_2_), channel_id=1, source_target_pairs={{0,8},{8,0},{16,24},{24,16},{1,9},{9,1},{17,25},{25,17},{2,10},{10... | collective-permute-start | bytes 393224 | tf_op jit(solution)/shard_map/ppermute | solution.py:256
  4.0 12.7 %collective-permute-start.1 = (bf16[16,4096]{1,0:T(8,128)(2,1)}, bf16[16,4096]{1,0:T(8,128)(2,1)S(1)}, u32[]{:S(2)}, u32[]{:S(2)}) collective-permute-start(bf16[16,4096]{1,0:T(8,128)(2,1)} %bitcast.3.refs_0_), channel_id=1, source_target_pairs={{0,16},{8,24},{16,0},{24,8},{1,17},{9,25},{17,1},{25,9},{2,18},{10... | collective-permute-start | bytes 393224 | tf_op jit(solution)/shard_map/ppermute | solution.py:256
  6.6 4.3 %collective-permute-start = (bf16[8,4096]{1,0:T(8,128)(2,1)S(1)}, bf16[8,4096]{1,0:T(8,128)(2,1)S(1)}, u32[]{:S(2)}, u32[]{:S(2)}) collective-permute-start(bf16[8,4096]{1,0:T(8,128)(2,1)S(1)} %bitcast.7), channel_id=1, source_target_pairs={{0,4},{4,0},{1,5},{5,1},{2,6},{6,2},{3,7},{7,3},{8,12},{12,8},{9,1... | collective-permute-start | bytes 196616 | tf_op jit(solution)/shard_map/ppermute | solution.py:256
  8.1 10.6 %collective-permute-start.3 = (bf16[16,4096]{1,0:T(8,128)(2,1)}, bf16[16,4096]{1,0:T(8,128)(2,1)S(1)}, u32[]{:S(2)}, u32[]{:S(2)}) collective-permute-start(bf16[16,4096]{1,0:T(8,128)(2,1)} %bitcast.3.refs_0_), channel_id=1, source_target_pairs={{0,24},{8,16},{16,8},{24,0},{1,25},{9,17},{17,9},{25,1},{2,26},{10... | collective-permute-start | bytes 393224 | tf_op jit(solution)/shard_map/ppermute | solution.py:256
  19.5 1.5 %collective-permute-start.6 = (bf16[48,2048]{1,0:T(8,128)(2,1)S(1)}, bf16[48,2048]{1,0:T(8,128)(2,1)S(1)}, u32[]{:S(2)}, u32[]{:S(2)}) collective-permute-start(bf16[48,2048]{1,0:T(8,128)(2,1)S(1)} %get-tuple-element.21), channel_id=1, source_target_pairs={{0,1},{1,0},{2,3},{3,2},{4,5},{5,4},{6,7},{7,6},{8,9},{9,8},{10,11... | collective-permute-start | bytes 589832 | tf_op jit(solution)/shard_map/ppermute | solution.py:256
  20.3 2.4 %collective-permute-start.4 = (bf16[48,2048]{1,0:T(8,128)(2,1)S(1)}, bf16[48,2048]{1,0:T(8,128)(2,1)S(1)}, u32[]{:S(2)}, u32[]{:S(2)}) collective-permute-start(bf16[48,2048]{1,0:T(8,128)(2,1)S(1)} %get-tuple-element.18), channel_id=1, source_target_pairs={{0,1},{1,0},{2,3},{3,2},{4,5},{5,4},{6,7},{7,6},{8,9},{9,8},{10,11... | collective-permute-start | bytes 589832 | tf_op jit(solution)/shard_map/ppermute | solution.py:256
  21.1 5.7 %collective-permute-start.7 = (bf16[24,2048]{1,0:T(8,128)(2,1)S(1)}, bf16[24,2048]{1,0:T(8,128)(2,1)S(1)}, u32[]{:S(2)}, u32[]{:S(2)}) collective-permute-start(bf16[24,2048]{1,0:T(8,128)(2,1)S(1)} %join_cores.3), channel_id=1, source_target_pairs={{0,2},{1,3},{2,0},{3,1},{4,6},{5,7},{6,4},{7,5},{8,10},{9,11},{10,... | collective-permute-start | bytes 294920 | tf_op jit(solution)/shard_map/ppermute | solution.py:256
  22.7 5.4 %collective-permute-start.5 = (bf16[24,2048]{1,0:T(8,128)(2,1)S(1)}, bf16[24,2048]{1,0:T(8,128)(2,1)S(1)}, u32[]{:S(2)}, u32[]{:S(2)}) collective-permute-start(bf16[24,2048]{1,0:T(8,128)(2,1)S(1)} %join_cores.2), channel_id=1, source_target_pairs={{0,2},{1,3},{2,0},{3,1},{4,6},{5,7},{6,4},{7,5},{8,10},{9,11},{10,... | collective-permute-start | bytes 294920 | tf_op jit(solution)/shard_map/ppermute | solution.py:256
